TPU v7x, 32 devices: a whole 2x2x4 slice. The times are simulated.
32 devices in a mesh: groups: 2 (over y), gx: 8 (over z, x), gy: 2 (over core).
Axes of the slice: x: 2, y: 2, z: 4, core: 2. Of those that a mesh axis runs over, the one named last changes fastest.
Arguments:
- displacement: float32 [3, 16, 64, 128], P(None, ('groups', 'gx'), 'gy'), parts along dimension 1, may hold values from -6 to 6
- velocity: float32 [3, 16, 64, 128], P(None, ('groups', 'gx'), 'gy'), parts along dimension 1, may hold values from -6 to 6
- species: int32 [8, 64, 128], P('gx', 'gy'), may hold values from 0 to 1, as said below
- mass_factor: float32 [8, 64, 128], P('gx', 'gy'), may hold values from 0.6 to 1.6
- spring: float32 [8, 64, 128], P('gx', 'gy'), may hold values from 0.5 to 2
- force_blocks: float32 [8, 3, 3], replicated, may hold values from -0.6 to 0.6
- shell_table: int32 [3, 9], replicated, may hold values from 0 to 7
Outputs:
- mass_grad: float32 [16, 64, 128], P(('groups', 'gx'), 'gy'), parts along dimension 0
- spring_grad: float32 [16, 64, 128], P(('groups', 'gx'), 'gy'), parts along dimension 0
There are 2 independent parts, one for each index of `groups`. A program takes and returns all parts, laid end to end along the dimension named above; an argument that names none is the same for every part. Nothing has to cross between parts.
Inputs may be any that keep to these rules, and one draw needn't show every extreme that they name: `species`: 1 marks germanium, 0 silicon; the lower half of the transport dimension is mostly silicon, the upper half mostly germanium.
All inputs are finite; a program needn't handle non-finite values.
Results may differ from a plain program's by a relative error of at most 0.0003.
Values sent between devices are 32-bit elements; how exact they have to be, the bound alone decides.
No kernel may reach another device: no remote copies, remote signals or barrier semaphores. Data moves between devices by JAX's collectives and lax.ppermute only.
A program may use at most 128 MiB of HBM per device.

v0:
```python
import jax
import jax.numpy as jnp
from jax import lax
from jax.sharding import PartitionSpec as P

ZCELLS = 128
STEPS = 5


DIRECTIONS = (
    (1, 0, 0),
    (0, 1, 0),
    (0, 0, 1),
    (1, 1, 0),
    (1, -1, 0),
    (1, 0, 1),
    (1, 0, -1),
    (0, 1, 1),
    (0, 1, -1),
)
time_step = 0.5
germanium_ratio = 1.5856


def padded_2(cells, sides, width):
    for axis, dim in sides:
        count = lax.axis_size(axis)
        head = lax.slice_in_dim(cells, 0, width, axis=dim)
        tail = lax.slice_in_dim(cells, cells.shape[dim] - width, cells.shape[dim], axis=dim)
        cells = jnp.concatenate(
            [
                lax.ppermute(tail, axis, [(i, (i + 1) % count) for i in range(count)]),
                cells,
                lax.ppermute(head, axis, [((i + 1) % count, i) for i in range(count)]),
            ],
            axis=dim,
        )
    return cells


def shift_depth(field, depth):
    if depth == 0:
        return field
    border = jnp.zeros_like(field[..., :1])
    if depth > 0:
        return jnp.concatenate([field[..., 1:], border], axis=-1)
    return jnp.concatenate([border, field[..., :-1]], axis=-1)


def pair_blocks(force_blocks, shell_table):
    symmetric = 0.5 * (force_blocks + jnp.swapaxes(force_blocks, 1, 2))
    labels = jnp.arange(force_blocks.shape[0], dtype=jnp.int32)
    selector = (shell_table[:, :, None] == labels[None, None, :]).astype(jnp.float32)
    return jnp.einsum("kdn,nrc->kdrc", selector, symmetric, precision=lax.Precision.HIGHEST)


def coupling(kinds, centre_kind, other_kind, valid):
    weight_low = (1.0 - centre_kind) * (1.0 - other_kind)
    weight_high = centre_kind * other_kind
    weight_mixed = 1.0 - weight_low - weight_high
    return [
        [
            (
                weight_low * kinds[0, first, second]
                + weight_mixed * kinds[1, first, second]
                + weight_high * kinds[2, first, second]
            )
            * valid
            for second in range(3)
        ]
        for first in range(3)
    ]


def apply_coupling(matrix, difference):
    return jnp.stack(
        [
            matrix[first][0] * difference[0]
            + matrix[first][1] * difference[1]
            + matrix[first][2] * difference[2]
            for first in range(3)
        ]
    )


def operator_terms(
    value, value_at, partner, partner_at, species_float, spring, params_at, valid_at, blocks
):
    total = jnp.zeros_like(value)
    spring_part = jnp.zeros_like(spring)
    for direction in range(9):
        for flipped in (1, -1):
            offset = tuple((flipped * entry for entry in DIRECTIONS[direction]))
            other_kind, other_spring = params_at(offset)
            matrix = coupling(blocks[:, direction], species_float, other_kind, valid_at(offset))
            image = apply_coupling(matrix, value - value_at(offset))
            total = total + 0.5 * (spring + other_spring) * image
            if partner is not None:
                spring_part = spring_part + 0.5 * jnp.sum(
                    (partner - partner_at(offset)) * image, axis=0
                )
    return (total, spring_part)


def pick(padded, offset):
    width_x = padded.shape[1] - 2
    width_y = padded.shape[2] - 2
    window = padded[
        :, 1 + offset[0] : 1 + offset[0] + width_x, 1 + offset[1] : 1 + offset[1] + width_y, :
    ]
    return shift_depth(window, offset[2])


def centre(padded):
    return padded[:, 1:-1, 1:-1, :]


def pad_state(field):
    return padded_2(field, (("gx", 1), ("gy", 2)), 1)


def body(displacement, velocity, species, mass_factor, spring, force_blocks, shell_table):
    blocks = pair_blocks(force_blocks, shell_table)
    species_float = species.astype(jnp.float32)
    species_mass = 1.0 + germanium_ratio * species_float
    mass = species_mass * mass_factor
    material = padded_2(jnp.stack([species_float, spring]), (("gx", 1), ("gy", 2)), 1)
    filled = jnp.ones_like(spring)

    def params_at(offset):
        beside_all = pick(material, offset)
        return (beside_all[0], beside_all[1])

    def valid_at(offset):
        return shift_depth(filled, offset[2])

    def acting(padded_value, padded_partner):
        value_at = lambda offset: pick(padded_value, offset)
        if padded_partner is None:
            return operator_terms(
                centre(padded_value),
                value_at,
                None,
                None,
                species_float,
                spring,
                params_at,
                valid_at,
                blocks,
            )
        partner_at = lambda offset: pick(padded_partner, offset)
        return operator_terms(
            centre(padded_value),
            value_at,
            centre(padded_partner),
            partner_at,
            species_float,
            spring,
            params_at,
            valid_at,
            blocks,
        )

    half_step = 0.5 * time_step
    drift = 0.5 * time_step * time_step
    states = [displacement]
    padded_states = [pad_state(displacement)]
    accels = [-acting(padded_states[0], None)[0] / mass]
    moving = velocity
    for count in range(STEPS):
        advanced = states[-1] + time_step * moving + drift * accels[-1]
        padded_advanced = pad_state(advanced)
        fresh = -acting(padded_advanced, None)[0] / mass
        moving = moving + half_step * (accels[-1] + fresh)
        states.append(advanced)
        padded_states.append(padded_advanced)
        accels.append(fresh)
    depth_index = lax.broadcasted_iota(jnp.int32, spring.shape, 2)
    detect = (depth_index >= ZCELLS // 2).astype(jnp.float32)
    velocity_bar = detect * mass * moving
    mass_bar = 0.5 * detect * jnp.sum(moving * moving, axis=0)
    spring_bar = jnp.zeros_like(spring)
    state_bar = jnp.zeros_like(displacement)
    accel_bar = jnp.zeros_like(displacement)
    for level in range(STEPS, -1, -1):
        if level > 0:
            accel_bar = accel_bar + half_step * velocity_bar
        scaled = accel_bar / mass
        padded_scaled = padded_2(scaled, (("gx", 1), ("gy", 2)), 1)
        padded_partner = padded_states[level]
        pushed, spring_term = acting(padded_scaled, padded_partner)
        state_bar = state_bar - pushed
        mass_bar = mass_bar - jnp.sum(accel_bar * accels[level], axis=0) / mass
        spring_bar = spring_bar - spring_term
        if level > 0:
            accel_bar = drift * state_bar + half_step * velocity_bar
            velocity_bar = velocity_bar + time_step * state_bar
    return (mass_bar * species_mass, spring_bar)


def solution(mesh):
    return jax.shard_map(
        body,
        mesh=mesh,
        in_specs=(
            P(None, ("groups", "gx"), "gy", None),
            P(None, ("groups", "gx"), "gy", None),
            P("gx", "gy", None),
            P("gx", "gy", None),
            P("gx", "gy", None),
            P(),
            P(),
        ),
        out_specs=(P(("groups", "gx"), "gy", None), P(("groups", "gx"), "gy", None)),
        check_vma=False,
    )
```

profile of v0, /device:TPU:1, one launch (start us, length us, event | category | flops | bytes accessed | tf_op | source)
XLA Modules:
  0.0 428.9 jit_solution(14636290518023250806)
XLA Ops:
  33.5 5.6 %add_bitcast_fusion.611 = (f32[1,1,32,128]{3,2,1,0:T(8,128)S(1)}, f32[1,32,128]{2,1,0:T(8,128)S(1)}, f32[1,32,128]{2,1,0:T(8,128)S(1)}, f32[1,32,128]{2,1,0:T(8,...) fusion(f32[3,1,32,128]{3,2,1,0:T(8,128)S(1)} %get-tuple-element.1349, ...), kind=kLoop, calls=%fused_computation.2193 | loop fusion | flops 131072 | bytes 245540 | tf_op jit(solution)/shard_map/stack | solution.py:76
  50.1 5.7 %add_bitcast_fusion.606 = (f32[1,1,32,128]{3,2,1,0:T(8,128)S(1)}, f32[1,32,128]{2,1,0:T(8,128)S(1)}, f32[1,32,128]{2,1,0:T(8,128)S(1)}, f32[1,32,128]{2,1,0:T(8,128)S(1)}) fusion(f32[3,1,32,128]{3,2,1,0:T(8,128)S(1)} %get-tuple-element.1348, f32[1,32,128]{2,1,0:T(8,128)S(1)} %copy-done.2, f32[1,32,128]{2,1,0:T(8,128)S(1)} %get-tuple-element.227, ...), kind=kLoop, calls=%fused_computation.2171 | loop fusion | flops 102400 | bytes 163876 | tf_op jit(solution)/shard_map/stack | solution.py:76
  55.8 5.7 %add_bitcast_fusion.609 = (f32[1,1,32,128]{3,2,1,0:T(8,128)S(1)}, f32[1,32,128]{2,1,0:T(8,128)S(1)}, f32[1,32,128]{2,1,0:T(8,128)S(1)}, f32[1,32,128]{2,1,0:T(8,128)S(1)}) fusion(f32[3,1,32,128]{3,2,1,0:T(8,128)S(1)} %get-tuple-element.1349, f32[1,32,128]{2,1,0:T(8,128)S(1)} %copy-done.3, f32[1,32,128]{2,1,0:T(8,128)S(1)} %get-tuple-element.213, ...), kind=kLoop, calls=%fused_computation.2185 | loop fusion | flops 102400 | bytes 163876 | tf_op jit(solution)/shard_map/stack | solution.py:76
  61.6 5.8 %add_bitcast_fusion.614 = (f32[1,1,32,128]{3,2,1,0:T(8,128)S(1)}, f32[1,32,128]{2,1,0:T(8,128)S(1)}, f32[1,32,128]{2,1,0:T(8,128)S(1)}, f32[1,32,128]{2,1,0:T(8,...) fusion(f32[3,1,32,128]{3,2,1,0:T(8,128)S(1)} %get-tuple-element.1350, ...), kind=kLoop, calls=%fused_computation.2207 | loop fusion | flops 131072 | bytes 245540 | tf_op jit(solution)/shard_map/stack | solution.py:76
  67.4 5.7 %add_bitcast_fusion.617 = (f32[1,1,32,128]{3,2,1,0:T(8,128)S(1)}, f32[1,32,128]{2,1,0:T(8,128)S(1)}, f32[1,32,128]{2,1,0:T(8,128)S(1)}, f32[1,32,128]{2,1,0:T(8,...) fusion(f32[3,1,32,128]{3,2,1,0:T(8,128)S(1)} %get-tuple-element.1351, ...), kind=kLoop, calls=%fused_computation.2221 | loop fusion | flops 131072 | bytes 245540 | tf_op jit(solution)/shard_map/stack | solution.py:76
  73.1 5.7 %add_bitcast_fusion.613 = (f32[1,1,32,128]{3,2,1,0:T(8,128)S(1)}, f32[1,32,128]{2,1,0:T(8,128)S(1)}, f32[1,32,128]{2,1,0:T(8,128)S(1)}, f32[1,32,128]{2,1,0:T(8,128)S(1)}) fusion(f32[3,1,32,128]{3,2,1,0:T(8,128)S(1)} %get-tuple-element.1350, f32[1,32,128]{2,1,0:T(8,128)S(1)} %copy-done.3, f32[1,32,128]{2,1,0:T(8,128)S(1)} %get-tuple-element.199, ...), kind=kLoop, calls=%fused_computation.2203 | loop fusion | flops 102400 | bytes 163876 | tf_op jit(solution)/shard_map/stack | solution.py:76
  78.8 5.7 %add_bitcast_fusion.616 = (f32[1,1,32,128]{3,2,1,0:T(8,128)S(1)}, f32[1,32,128]{2,1,0:T(8,128)S(1)}, f32[1,32,128]{2,1,0:T(8,128)S(1)}, f32[1,32,128]{2,1,0:T(8,128)S(1)}) fusion(f32[3,1,32,128]{3,2,1,0:T(8,128)S(1)} %get-tuple-element.1351, f32[1,32,128]{2,1,0:T(8,128)S(1)} %copy-done.2, f32[1,32,128]{2,1,0:T(8,128)S(1)} %get-tuple-element.185, ...), kind=kLoop, calls=%fused_computation.2217 | loop fusion | flops 102400 | bytes 163876 | tf_op jit(solution)/shard_map/stack | solution.py:76
  95.7 5.7 %add_bitcast_fusion.632 = (f32[1,1,32,128]{3,2,1,0:T(8,128)S(1)}, f32[1,32,128]{2,1,0:T(8,128)S(1)}, f32[1,32,128]{2,1,0:T(8,128)S(1)}, f32[1,32,128]{2,1,0:T(8,...) fusion(f32[3,1,32,128]{3,2,1,0:T(8,128)S(1)} %get-tuple-element.1352, ...), kind=kLoop, calls=%fused_computation.2291 | loop fusion | flops 131072 | bytes 245540 | tf_op jit(solution)/shard_map/stack | solution.py:76
  101.4 5.6 %add_bitcast_fusion.635 = (f32[1,1,32,128]{3,2,1,0:T(8,128)S(1)}, f32[1,32,128]{2,1,0:T(8,128)S(1)}, f32[1,32,128]{2,1,0:T(8,128)S(1)}, f32[1,32,128]{2,1,0:T(8,...) fusion(f32[3,1,32,128]{3,2,1,0:T(8,128)S(1)} %get-tuple-element.1353, ...), kind=kLoop, calls=%fused_computation.2305 | loop fusion | flops 131072 | bytes 245540 | tf_op jit(solution)/shard_map/stack | solution.py:76
  107.0 5.6 %add_bitcast_fusion.631 = (f32[1,1,32,128]{3,2,1,0:T(8,128)S(1)}, f32[1,32,128]{2,1,0:T(8,128)S(1)}, f32[1,32,128]{2,1,0:T(8,128)S(1)}, f32[1,32,128]{2,1,0:T(8,128)S(1)}) fusion(f32[3,1,32,128]{3,2,1,0:T(8,128)S(1)} %get-tuple-element.1352, f32[1,32,128]{2,1,0:T(8,128)S(1)} %copy-done.3, f32[1,32,128]{2,1,0:T(8,128)S(1)} %get-tuple-element.115, ...), kind=kLoop, calls=%fused_computation.2287 | loop fusion | flops 102400 | bytes 163876 | tf_op jit(solution)/shard_map/stack | solution.py:76
  112.7 5.6 %add_bitcast_fusion.634 = (f32[1,1,32,128]{3,2,1,0:T(8,128)S(1)}, f32[1,32,128]{2,1,0:T(8,128)S(1)}, f32[1,32,128]{2,1,0:T(8,128)S(1)}, f32[1,32,128]{2,1,0:T(8,128)S(1)}) fusion(f32[3,1,32,128]{3,2,1,0:T(8,128)S(1)} %get-tuple-element.1353, f32[1,32,128]{2,1,0:T(8,128)S(1)} %copy-done.2, f32[1,32,128]{2,1,0:T(8,128)S(1)} %get-tuple-element.101, ...), kind=kLoop, calls=%fused_computation.2301 | loop fusion | flops 102400 | bytes 163876 | tf_op jit(solution)/shard_map/stack | solution.py:76
  118.3 5.6 %add_bitcast_fusion.630 = (f32[1,1,32,128]{3,2,1,0:T(8,128)S(1)}, f32[1,32,128]{2,1,0:T(8,128)S(1)}, f32[1,32,128]{2,1,0:T(8,128)S(1)}, f32[1,32,128]{2,1,0:T(8,128)S(1)}) fusion(f32[3,1,32,128]{3,2,1,0:T(8,128)S(1)} %get-tuple-element.1352, f32[1,32,128]{2,1,0:T(8,128)S(1)} %copy-done.3, f32[1,32,128]{2,1,0:T(8,128)S(1)} %get-tuple-element.115, ...), kind=kLoop, calls=%fused_computation.2283 | loop fusion | flops 102400 | bytes 163876 | tf_op jit(solution)/shard_map/stack | solution.py:76
  123.9 5.6 %add_bitcast_fusion.633 = (f32[1,1,32,128]{3,2,1,0:T(8,128)S(1)}, f32[1,32,128]{2,1,0:T(8,128)S(1)}, f32[1,32,128]{2,1,0:T(8,128)S(1)}, f32[1,32,128]{2,1,0:T(8,128)S(1)}) fusion(f32[3,1,32,128]{3,2,1,0:T(8,128)S(1)} %get-tuple-element.1353, f32[1,32,128]{2,1,0:T(8,128)S(1)} %copy-done.2, f32[1,32,128]{2,1,0:T(8,128)S(1)} %get-tuple-element.101, ...), kind=kLoop, calls=%fused_computation.2297 | loop fusion | flops 102400 | bytes 163876 | tf_op jit(solution)/shard_map/stack | solution.py:76
  152.4 5.7 %add_bitcast_fusion.645 = (f32[1,1,32,128]{3,2,1,0:T(8,128)S(1)}, f32[1,32,128]{2,1,0:T(8,128)S(1)}, f32[1,32,128]{2,1,0:T(8,128)S(1)}, f32[1,32,128]{2,1,0:T(8,128)S(1)}) fusion(f32[3,1,32,128]{3,2,1,0:T(8,128)S(1)} %get-tuple-element.1346, f32[1,32,128]{2,1,0:T(8,128)S(1)} %get-tuple-element.45, f32[]{:T(128)} %bitcast.34, f32[]{:T(128)} %bitcast.33, ...), kind=kLoop, calls=%fused_computation.2353 | loop fusion | flops 90112 | bytes 147492 | tf_op jit(solution)/shard_map/stack | solution.py:76
  158.1 5.7 %add_bitcast_fusion.642 = (f32[1,1,32,128]{3,2,1,0:T(8,128)S(1)}, f32[1,32,128]{2,1,0:T(8,128)S(1)}, f32[1,32,128]{2,1,0:T(8,128)S(1)}, f32[1,32,128]{2,1,0:T(8,128)S(1)}) fusion(f32[3,1,32,128]{3,2,1,0:T(8,128)S(1)} %get-tuple-element.1354, f32[1,32,128]{2,1,0:T(8,128)S(1)} %get-tuple-element.59, f32[]{:T(128)} %bitcast.34, f32[]{:T(128)} %bitcast.33, ...), kind=kLoop, calls=%fused_computation.2339 | loop fusion | flops 90112 | bytes 147492 | tf_op jit(solution)/shard_map/stack | solution.py:76
  164.0 5.6 %add_bitcast_fusion.599 = (f32[1,1,32,128]{3,2,1,0:T(8,128)S(1)}, f32[1,32,128]{2,1,0:T(8,128)S(1)}, f32[1,32,128]{2,1,0:T(8,128)S(1)}, f32[1,32,128]{2,1,0:T(8,...) fusion(f32[3,1,32,128]{3,2,1,0:T(8,128)S(1)} %get-tuple-element.359, ...), kind=kLoop, calls=%fused_computation.2137 | loop fusion | flops 131072 | bytes 245540 | tf_op jit(solution)/shard_map/stack | solution.py:76
  186.4 5.9 %add_bitcast_fusion.597 = (f32[1,1,32,128]{3,2,1,0:T(8,128)S(1)}, f32[1,32,128]{2,1,0:T(8,128)S(1)}, f32[1,32,128]{2,1,0:T(8,128)S(1)}, f32[1,32,128]{2,1,0:T(8,128)S(1)}) fusion(f32[3,1,32,128]{3,2,1,0:T(8,128)S(1)} %get-tuple-element.359, f32[1,32,128]{2,1,0:T(8,128)S(1)} %copy-done.3, f32[1,32,128]{2,1,0:T(8,128)S(1)} %get-tuple-element.269, ...), kind=kLoop, calls=%fused_computation.2129 | loop fusion | flops 102400 | bytes 163876 | tf_op jit(solution)/shard_map/stack | solution.py:76
  192.3 5.9 %add_bitcast_fusion.594 = (f32[1,1,32,128]{3,2,1,0:T(8,128)S(1)}, f32[1,32,128]{2,1,0:T(8,128)S(1)}, f32[1,32,128]{2,1,0:T(8,128)S(1)}, f32[1,32,128]{2,1,0:T(8,128)S(1)}) fusion(f32[3,1,32,128]{3,2,1,0:T(8,128)S(1)} %get-tuple-element.366, f32[1,32,128]{2,1,0:T(8,128)S(1)} %copy-done.2, f32[1,32,128]{2,1,0:T(8,128)S(1)} %get-tuple-element.283, ...), kind=kLoop, calls=%fused_computation.2115 | loop fusion | flops 102400 | bytes 163876 | tf_op jit(solution)/shard_map/stack | solution.py:76
  220.1 5.8 %add_bitcast_fusion.600 = (f32[1,1,32,128]{3,2,1,0:T(8,128)S(1)}, f32[1,32,128]{2,1,0:T(8,128)S(1)}, f32[1,32,128]{2,1,0:T(8,128)S(1)}, f32[1,32,128]{2,1,0:T(8,128)S(1)}) fusion(f32[3,1,32,128]{3,2,1,0:T(8,128)S(1)} %get-tuple-element.1355, f32[1,32,128]{2,1,0:T(8,128)S(1)} %copy-done.3, f32[1,32,128]{2,1,0:T(8,128)S(1)} %get-tuple-element.255, ...), kind=kLoop, calls=%fused_computation.2143 | loop fusion | flops 102400 | bytes 163876 | tf_op jit(solution)/shard_map/stack | solution.py:76
  225.8 5.8 %add_bitcast_fusion.603 = (f32[1,1,32,128]{3,2,1,0:T(8,128)S(1)}, f32[1,32,128]{2,1,0:T(8,128)S(1)}, f32[1,32,128]{2,1,0:T(8,128)S(1)}, f32[1,32,128]{2,1,0:T(8,128)S(1)}) fusion(f32[3,1,32,128]{3,2,1,0:T(8,128)S(1)} %get-tuple-element.1356, f32[1,32,128]{2,1,0:T(8,128)S(1)} %copy-done.2, f32[1,32,128]{2,1,0:T(8,128)S(1)} %get-tuple-element.241, ...), kind=kLoop, calls=%fused_computation.2157 | loop fusion | flops 102400 | bytes 163876 | tf_op jit(solution)/shard_map/stack | solution.py:76
  231.6 5.7 %fusion.206 = (f32[32,128]{1,0:T(8,128)S(1)}, f32[32,128]{1,0:T(8,128)S(1)}, f32[32,128]{1,0:T(8,128)S(1)}, f32[1,1,32,128]{3,2,1,0:T(8,128)S(1)}, f32[1,32,128]...) fusion(f32[1,32,128]{2,1,0:T(8,128)S(1)} %copy-done, ...), kind=kLoop, calls=%fused_computation.1470 | loop fusion | flops 135168 | bytes 294948 | tf_op jit(solution)/shard_map/mul | solution.py:97
  237.2 5.7 %fusion.203 = (f32[32,128]{1,0:T(8,128)S(1)}, f32[32,128]{1,0:T(8,128)S(1)}, f32[32,128]{1,0:T(8,128)S(1)}, f32[1,1,32,128]{3,2,1,0:T(8,128)S(1)}, f32[1,32,128]...) fusion(f32[1,32,128]{2,1,0:T(8,128)S(1)} %copy-done, ...), kind=kLoop, calls=%fused_computation.1462 | loop fusion | flops 135168 | bytes 294948 | tf_op jit(solution)/shard_map/mul | solution.py:97
  242.9 5.6 %add_bitcast_fusion.618 = (f32[1,1,32,128]{3,2,1,0:T(8,128)S(1)}, f32[1,32,128]{2,1,0:T(8,128)S(1)}, f32[1,32,128]{2,1,0:T(8,128)S(1)}, f32[1,32,128]{2,1,0:T(8,128)S(1)}) fusion(f32[3,1,32,128]{3,2,1,0:T(8,128)S(1)} %get-tuple-element.360, f32[1,32,128]{2,1,0:T(8,128)S(1)} %get-tuple-element.472, f32[]{:T(128)} %bitcast.214, f32[]{:T(128)} %bitcast.213, ...), kind=kLoop, calls=%fused_computation.2227 | loop fusion | flops 90112 | bytes 147492 | tf_op jit(solution)/shard_map/stack | solution.py:76
  254.1 5.6 %add_bitcast_fusion.619 = (f32[1,1,32,128]{3,2,1,0:T(8,128)S(1)}, f32[1,32,128]{2,1,0:T(8,128)S(1)}, f32[1,32,128]{2,1,0:T(8,128)S(1)}, f32[1,32,128]{2,1,0:T(8,128)S(1)}) fusion(f32[3,1,32,128]{3,2,1,0:T(8,128)S(1)} %get-tuple-element.360, f32[1,32,128]{2,1,0:T(8,128)S(1)} %get-tuple-element.472, f32[]{:T(128)} %bitcast.204, f32[]{:T(128)} %bitcast.203, ...), kind=kLoop, calls=%fused_computation.2231 | loop fusion | flops 90112 | bytes 147492 | tf_op jit(solution)/shard_map/stack | solution.py:76
  259.7 5.6 %add_bitcast_fusion.622 = (f32[1,1,32,128]{3,2,1,0:T(8,128)S(1)}, f32[1,32,128]{2,1,0:T(8,128)S(1)}, f32[1,32,128]{2,1,0:T(8,128)S(1)}, f32[1,32,128]{2,1,0:T(8,128)S(1)}) fusion(f32[3,1,32,128]{3,2,1,0:T(8,128)S(1)} %get-tuple-element.368, f32[1,32,128]{2,1,0:T(8,128)S(1)} %get-tuple-element.478, f32[]{:T(128)} %bitcast.204, f32[]{:T(128)} %bitcast.203, ...), kind=kLoop, calls=%fused_computation.2245 | loop fusion | flops 90112 | bytes 147492 | tf_op jit(solution)/shard_map/stack | solution.py:76
  270.8 5.7 %add_bitcast_fusion.639 = (f32[1,1,32,128]{3,2,1,0:T(8,128)S(1)}, f32[1,32,128]{2,1,0:T(8,128)S(1)}, f32[1,32,128]{2,1,0:T(8,128)S(1)}, f32[1,32,128]{2,1,0:T(8,128)S(1)}) fusion(f32[3,1,32,128]{3,2,1,0:T(8,128)S(1)} %get-tuple-element.358, f32[1,32,128]{2,1,0:T(8,128)S(1)} %get-tuple-element.73, f32[]{:T(128)} %bitcast.79, f32[]{:T(128)} %bitcast.78, ...), kind=kLoop, calls=%fused_computation.2325 | loop fusion | flops 90112 | bytes 147492 | tf_op jit(solution)/shard_map/stack | solution.py:76
  276.5 5.7 %add_bitcast_fusion.636 = (f32[1,1,32,128]{3,2,1,0:T(8,128)S(1)}, f32[1,32,128]{2,1,0:T(8,128)S(1)}, f32[1,32,128]{2,1,0:T(8,128)S(1)}, f32[1,32,128]{2,1,0:T(8,128)S(1)}) fusion(f32[3,1,32,128]{3,2,1,0:T(8,128)S(1)} %get-tuple-element.369, f32[1,32,128]{2,1,0:T(8,128)S(1)} %get-tuple-element.1389, f32[]{:T(128)} %bitcast.79, f32[]{:T(128)} %bitcast.78, ...), kind=kLoop, calls=%fused_computation.2311 | loop fusion | flops 90112 | bytes 147492 | tf_op jit(solution)/shard_map/stack | solution.py:76
  282.1 5.8 %add_bitcast_fusion.640 = (f32[1,1,32,128]{3,2,1,0:T(8,128)S(1)}, f32[1,32,128]{2,1,0:T(8,128)S(1)}, f32[1,32,128]{2,1,0:T(8,128)S(1)}, f32[1,32,128]{2,1,0:T(8,128)S(1)}) fusion(f32[3,1,32,128]{3,2,1,0:T(8,128)S(1)} %get-tuple-element.358, f32[1,32,128]{2,1,0:T(8,128)S(1)} %get-tuple-element.73, f32[]{:T(128)} %bitcast.69, f32[]{:T(128)} %bitcast.68, ...), kind=kLoop, calls=%fused_computation.2329 | loop fusion | flops 90112 | bytes 147492 | tf_op jit(solution)/shard_map/stack | solution.py:76
  287.9 5.8 %add_bitcast_fusion.637 = (f32[1,1,32,128]{3,2,1,0:T(8,128)S(1)}, f32[1,32,128]{2,1,0:T(8,128)S(1)}, f32[1,32,128]{2,1,0:T(8,128)S(1)}, f32[1,32,128]{2,1,0:T(8,128)S(1)}) fusion(f32[3,1,32,128]{3,2,1,0:T(8,128)S(1)} %get-tuple-element.369, f32[1,32,128]{2,1,0:T(8,128)S(1)} %get-tuple-element.1389, f32[]{:T(128)} %bitcast.69, f32[]{:T(128)} %bitcast.68, ...), kind=kLoop, calls=%fused_computation.2315 | loop fusion | flops 90112 | bytes 147492 | tf_op jit(solution)/shard_map/stack | solution.py:76
  293.7 5.6 %add_bitcast_fusion.629 = (f32[1,1,32,128]{3,2,1,0:T(8,128)S(1)}, f32[1,32,128]{2,1,0:T(8,128)S(1)}, f32[1,32,128]{2,1,0:T(8,128)S(1)}, f32[1,32,128]{2,1,0:T(8,...) fusion(f32[3,1,32,128]{3,2,1,0:T(8,128)S(1)} %get-tuple-element, ...), kind=kLoop, calls=%fused_computation.2277 | loop fusion | flops 212992 | bytes 344100 | tf_op jit(solution)/shard_map/stack | solution.py:76
  310.1 5.7 %add_bitcast_fusion.628 = (f32[1,1,32,128]{3,2,1,0:T(8,128)S(1)}, f32[1,32,128]{2,1,0:T(8,128)S(1)}, f32[1,32,128]{2,1,0:T(8,128)S(1)}, f32[1,32,128]{2,1,0:T(8,128)S(1)}) fusion(f32[3,1,32,128]{3,2,1,0:T(8,128)S(1)} %get-tuple-element.361, f32[1,32,128]{2,1,0:T(8,128)S(1)} %get-tuple-element.129, f32[]{:T(128)} %bitcast.159, f32[]{:T(128)} %bitcast.158, ...), kind=kLoop, calls=%fused_computation.2273 | loop fusion | flops 90112 | bytes 147492 | tf_op jit(solution)/shard_map/stack | solution.py:76
  315.9 5.7 %add_bitcast_fusion.625 = (f32[1,1,32,128]{3,2,1,0:T(8,128)S(1)}, f32[1,32,128]{2,1,0:T(8,128)S(1)}, f32[1,32,128]{2,1,0:T(8,128)S(1)}, f32[1,32,128]{2,1,0:T(8,128)S(1)}) fusion(f32[3,1,32,128]{3,2,1,0:T(8,128)S(1)} %get-tuple-element.367, f32[1,32,128]{2,1,0:T(8,128)S(1)} %get-tuple-element.1395, f32[]{:T(128)} %bitcast.159, f32[]{:T(128)} %bitcast.158, ...), kind=kLoop, calls=%fused_computation.2259 | loop fusion | flops 90112 | bytes 147492 | tf_op jit(solution)/shard_map/stack | solution.py:76
  (539 shorter events, 243.3 us)
Async XLA Ops:
  1.4 22.5 %collective-permute-start.2 = (f32[2,1,32,128]{3,2,1,0:T(8,128)S(1)}, f32[2,1,32,128]{3,2,1,0:T(8,128)S(1)}, u32[]{:S(2)}, u32[]{:S(2)}) collective-permute-start(f32[2,1,32,128]{3,2,1,0:T(8,128)S(1)} %pad_maximum_fusion.102), channel_id=1, source_target_pairs={{0,2},{2,4},{4,6},{6,8},{8,10},{10,12},{12,14},{14,0},{1,3},{3,5},... | collective-permute-start | bytes 98312 | tf_op jit(solution)/shard_map/ppermute | solution.py:32
  3.5 20.4 %collective-permute-start = (f32[2,1,32,128]{3,2,1,0:T(8,128)S(1)}, f32[2,1,32,128]{3,2,1,0:T(8,128)S(1)}, u32[]{:S(2)}, u32[]{:S(2)}) collective-permute-start(f32[2,1,32,128]{3,2,1,0:T(8,128)S(1)} %pad_maximum_fusion.102), channel_id=1, source_target_pairs={{2,0},{4,2},{6,4},{8,6},{10,8},{12,10},{14,12},{0,14},{3,1},{5,3},... | collective-permute-start | bytes 98312 | tf_op jit(solution)/shard_map/ppermute | solution.py:34
  6.6 20.2 %collective-permute-start.3 = (f32[3,1,32,128]{3,2,1,0:T(8,128)S(1)}, f32[3,1,32,128]{3,2,1,0:T(8,128)S(1)}, u32[]{:S(2)}, u32[]{:S(2)}) collective-permute-start(f32[3,1,32,128]{3,2,1,0:T(8,128)S(1)} %copy-done.4), channel_id=1, source_target_pairs={{0,2},{2,4},{4,6},{6,8},{8,10},{10,12},{12,14},{14,0},{1,3},{3,5},... | collective-permute-start | bytes 147464 | tf_op jit(solution)/shard_map/ppermute | solution.py:32
  6.6 20.3 %collective-permute-start.1 = (f32[3,1,32,128]{3,2,1,0:T(8,128)S(1)}, f32[3,1,32,128]{3,2,1,0:T(8,128)S(1)}, u32[]{:S(2)}, u32[]{:S(2)}) collective-permute-start(f32[3,1,32,128]{3,2,1,0:T(8,128)S(1)} %copy-done.4), channel_id=1, source_target_pairs={{2,0},{4,2},{6,4},{8,6},{10,8},{12,10},{14,12},{0,14},{3,1},{5,3},... | collective-permute-start | bytes 147464 | tf_op jit(solution)/shard_map/ppermute | solution.py:34
  23.9 2.4 collective-permute-start.4
  129.5 34.2 %collective-permute-start.5 = (f32[3,3,1,128]{3,2,1,0:T(1,128)S(1)}, f32[3,3,1,128]{3,2,1,0:T(1,128)S(1)}, u32[]{:S(2)}, u32[]{:S(2)}) collective-permute-start(f32[3,3,1,128]{3,2,1,0:T(1,128)S(1)} %get-tuple-element.460), channel_id=1, source_target_pairs={{1,0},{0,1},{3,2},{2,3},{5,4},{4,5},{7,6},{6,7},{9,8},{8,9},{11,10... | collective-permute-start | bytes 13832 | tf_op jit(solution)/shard_map/ppermute | solution.py:34
  129.8 34.0 %collective-permute-start.7 = (f32[3,3,1,128]{3,2,1,0:T(1,128)S(1)}, f32[3,3,1,128]{3,2,1,0:T(1,128)S(1)}, u32[]{:S(2)}, u32[]{:S(2)}) collective-permute-start(f32[3,3,1,128]{3,2,1,0:T(1,128)S(1)} %get-tuple-element.461), channel_id=1, source_target_pairs={{0,1},{1,0},{2,3},{3,2},{4,5},{5,4},{6,7},{7,6},{8,9},{9,8},{10,11... | collective-permute-start | bytes 13832 | tf_op jit(solution)/shard_map/ppermute | solution.py:32
  322.6 5.7 %collective-permute-start.9 = (f32[3,1,32,128]{3,2,1,0:T(8,128)S(1)}, f32[3,1,32,128]{3,2,1,0:T(8,128)S(1)}, u32[]{:S(2)}, u32[]{:S(2)}) collective-permute-start(f32[3,1,32,128]{3,2,1,0:T(8,128)S(1)} %get-tuple-element.38), channel_id=1, source_target_pairs={{0,2},{2,4},{4,6},{6,8},{8,10},{10,12},{12,14},{14,0},{1,3},{3,5},... | collective-permute-start | bytes 147464 | tf_op jit(solution)/shard_map/ppermute | solution.py:32
  322.7 5.6 %collective-permute-start.8 = (f32[3,1,32,128]{3,2,1,0:T(8,128)S(1)}, f32[3,1,32,128]{3,2,1,0:T(8,128)S(1)}, u32[]{:S(2)}, u32[]{:S(2)}) collective-permute-start(f32[3,1,32,128]{3,2,1,0:T(8,128)S(1)} %get-tuple-element.38), channel_id=1, source_target_pairs={{2,0},{4,2},{6,4},{8,6},{10,8},{12,10},{14,12},{0,14},{3,1},{5,3},... | collective-permute-start | bytes 147464 | tf_op jit(solution)/shard_map/ppermute | solution.py:34
  328.3 2.2 collective-permute-start.10
  332.0 6.5 %collective-permute-start.13 = (f32[3,1,32,128]{3,2,1,0:T(8,128)S(1)}, f32[3,1,32,128]{3,2,1,0:T(8,128)S(1)}, u32[]{:S(2)}, u32[]{:S(2)}) collective-permute-start(f32[3,1,32,128]{3,2,1,0:T(8,128)S(1)} %get-tuple-element.36), channel_id=1, source_target_pairs={{0,2},{2,4},{4,6},{6,8},{8,10},{10,12},{12,14},{14,0},{1,3},{3,5},... | collective-permute-start | bytes 147464 | tf_op jit(solution)/shard_map/ppermute | solution.py:32
  332.0 6.5 %collective-permute-start.12 = (f32[3,1,32,128]{3,2,1,0:T(8,128)S(1)}, f32[3,1,32,128]{3,2,1,0:T(8,128)S(1)}, u32[]{:S(2)}, u32[]{:S(2)}) collective-permute-start(f32[3,1,32,128]{3,2,1,0:T(8,128)S(1)} %get-tuple-element.36), channel_id=1, source_target_pairs={{2,0},{4,2},{6,4},{8,6},{10,8},{12,10},{14,12},{0,14},{3,1},{5,3},... | collective-permute-start | bytes 147464 | tf_op jit(solution)/shard_map/ppermute | solution.py:34
  341.5 6.3 %collective-permute-start.17 = (f32[3,1,32,128]{3,2,1,0:T(8,128)S(1)}, f32[3,1,32,128]{3,2,1,0:T(8,128)S(1)}, u32[]{:S(2)}, u32[]{:S(2)}) collective-permute-start(f32[3,1,32,128]{3,2,1,0:T(8,128)S(1)} %get-tuple-element.33), channel_id=1, source_target_pairs={{0,2},{2,4},{4,6},{6,8},{8,10},{10,12},{12,14},{14,0},{1,3},{3,5},... | collective-permute-start | bytes 147464 | tf_op jit(solution)/shard_map/ppermute | solution.py:32
  341.6 6.2 %collective-permute-start.16 = (f32[3,1,32,128]{3,2,1,0:T(8,128)S(1)}, f32[3,1,32,128]{3,2,1,0:T(8,128)S(1)}, u32[]{:S(2)}, u32[]{:S(2)}) collective-permute-start(f32[3,1,32,128]{3,2,1,0:T(8,128)S(1)} %get-tuple-element.33), channel_id=1, source_target_pairs={{2,0},{4,2},{6,4},{8,6},{10,8},{12,10},{14,12},{0,14},{3,1},{5,3},... | collective-permute-start | bytes 147464 | tf_op jit(solution)/shard_map/ppermute | solution.py:34
  350.9 6.4 %collective-permute-start.21 = (f32[3,1,32,128]{3,2,1,0:T(8,128)S(1)}, f32[3,1,32,128]{3,2,1,0:T(8,128)S(1)}, u32[]{:S(2)}, u32[]{:S(2)}) collective-permute-start(f32[3,1,32,128]{3,2,1,0:T(8,128)S(1)} %get-tuple-element.31), channel_id=1, source_target_pairs={{0,2},{2,4},{4,6},{6,8},{8,10},{10,12},{12,14},{14,0},{1,3},{3,5},... | collective-permute-start | bytes 147464 | tf_op jit(solution)/shard_map/ppermute | solution.py:32
  351.0 6.3 %collective-permute-start.20 = (f32[3,1,32,128]{3,2,1,0:T(8,128)S(1)}, f32[3,1,32,128]{3,2,1,0:T(8,128)S(1)}, u32[]{:S(2)}, u32[]{:S(2)}) collective-permute-start(f32[3,1,32,128]{3,2,1,0:T(8,128)S(1)} %get-tuple-element.31), channel_id=1, source_target_pairs={{2,0},{4,2},{6,4},{8,6},{10,8},{12,10},{14,12},{0,14},{3,1},{5,3},... | collective-permute-start | bytes 147464 | tf_op jit(solution)/shard_map/ppermute | solution.py:34
  360.4 6.3 %collective-permute-start.25 = (f32[3,1,32,128]{3,2,1,0:T(8,128)S(1)}, f32[3,1,32,128]{3,2,1,0:T(8,128)S(1)}, u32[]{:S(2)}, u32[]{:S(2)}) collective-permute-start(f32[3,1,32,128]{3,2,1,0:T(8,128)S(1)} %get-tuple-element.29), channel_id=1, source_target_pairs={{0,2},{2,4},{4,6},{6,8},{8,10},{10,12},{12,14},{14,0},{1,3},{3,5},... | collective-permute-start | bytes 147464 | tf_op jit(solution)/shard_map/ppermute | solution.py:32
  360.5 6.2 %collective-permute-start.24 = (f32[3,1,32,128]{3,2,1,0:T(8,128)S(1)}, f32[3,1,32,128]{3,2,1,0:T(8,128)S(1)}, u32[]{:S(2)}, u32[]{:S(2)}) collective-permute-start(f32[3,1,32,128]{3,2,1,0:T(8,128)S(1)} %get-tuple-element.29), channel_id=1, source_target_pairs={{2,0},{4,2},{6,4},{8,6},{10,8},{12,10},{14,12},{0,14},{3,1},{5,3},... | collective-permute-start | bytes 147464 | tf_op jit(solution)/shard_map/ppermute | solution.py:34
  366.7 1.7 collective-permute-start.26
  369.9 6.6 %collective-permute-start.29 = (f32[3,1,32,128]{3,2,1,0:T(8,128)S(1)}, f32[3,1,32,128]{3,2,1,0:T(8,128)S(1)}, u32[]{:S(2)}, u32[]{:S(2)}) collective-permute-start(f32[3,1,32,128]{3,2,1,0:T(8,128)S(1)} %get-tuple-element.26), channel_id=1, source_target_pairs={{0,2},{2,4},{4,6},{6,8},{8,10},{10,12},{12,14},{14,0},{1,3},{3,5},... | collective-permute-start | bytes 147464 | tf_op jit(solution)/shard_map/ppermute | solution.py:32
  369.9 6.5 %collective-permute-start.28 = (f32[3,1,32,128]{3,2,1,0:T(8,128)S(1)}, f32[3,1,32,128]{3,2,1,0:T(8,128)S(1)}, u32[]{:S(2)}, u32[]{:S(2)}) collective-permute-start(f32[3,1,32,128]{3,2,1,0:T(8,128)S(1)} %get-tuple-element.26), channel_id=1, source_target_pairs={{2,0},{4,2},{6,4},{8,6},{10,8},{12,10},{14,12},{0,14},{3,1},{5,3},... | collective-permute-start | bytes 147464 | tf_op jit(solution)/shard_map/ppermute | solution.py:34
  379.7 6.3 %collective-permute-start.33 = (f32[3,1,32,128]{3,2,1,0:T(8,128)S(1)}, f32[3,1,32,128]{3,2,1,0:T(8,128)S(1)}, u32[]{:S(2)}, u32[]{:S(2)}) collective-permute-start(f32[3,1,32,128]{3,2,1,0:T(8,128)S(1)} %broadcast_divide_fusion.4), channel_id=1, source_target_pairs={{0,2},{2,4},{4,6},{6,8},{8,10},{10,12},{12,14},{14,0},{1,3},{3,5},... | collective-permute-start | bytes 147464 | tf_op jit(solution)/shard_map/ppermute | solution.py:32
  379.8 6.2 %collective-permute-start.32 = (f32[3,1,32,128]{3,2,1,0:T(8,128)S(1)}, f32[3,1,32,128]{3,2,1,0:T(8,128)S(1)}, u32[]{:S(2)}, u32[]{:S(2)}) collective-permute-start(f32[3,1,32,128]{3,2,1,0:T(8,128)S(1)} %broadcast_divide_fusion.4), channel_id=1, source_target_pairs={{2,0},{4,2},{6,4},{8,6},{10,8},{12,10},{14,12},{0,14},{3,1},{5,3},... | collective-permute-start | bytes 147464 | tf_op jit(solution)/shard_map/ppermute | solution.py:34
  386.0 1.7 collective-permute-start.34
  389.4 6.4 %collective-permute-start.37 = (f32[3,1,32,128]{3,2,1,0:T(8,128)S(1)}, f32[3,1,32,128]{3,2,1,0:T(8,128)S(1)}, u32[]{:S(2)}, u32[]{:S(2)}) collective-permute-start(f32[3,1,32,128]{3,2,1,0:T(8,128)S(1)} %broadcast_divide_fusion.3), channel_id=1, source_target_pairs={{0,2},{2,4},{4,6},{6,8},{8,10},{10,12},{12,14},{14,0},{1,3},{3,5},... | collective-permute-start | bytes 147464 | tf_op jit(solution)/shard_map/ppermute | solution.py:32
  389.4 6.3 %collective-permute-start.36 = (f32[3,1,32,128]{3,2,1,0:T(8,128)S(1)}, f32[3,1,32,128]{3,2,1,0:T(8,128)S(1)}, u32[]{:S(2)}, u32[]{:S(2)}) collective-permute-start(f32[3,1,32,128]{3,2,1,0:T(8,128)S(1)} %broadcast_divide_fusion.3), channel_id=1, source_target_pairs={{2,0},{4,2},{6,4},{8,6},{10,8},{12,10},{14,12},{0,14},{3,1},{5,3},... | collective-permute-start | bytes 147464 | tf_op jit(solution)/shard_map/ppermute | solution.py:34
  399.1 6.3 %collective-permute-start.41 = (f32[3,1,32,128]{3,2,1,0:T(8,128)S(1)}, f32[3,1,32,128]{3,2,1,0:T(8,128)S(1)}, u32[]{:S(2)}, u32[]{:S(2)}) collective-permute-start(f32[3,1,32,128]{3,2,1,0:T(8,128)S(1)} %get-tuple-element.24), channel_id=1, source_target_pairs={{0,2},{2,4},{4,6},{6,8},{8,10},{10,12},{12,14},{14,0},{1,3},{3,5},... | collective-permute-start | bytes 147464 | tf_op jit(solution)/shard_map/ppermute | solution.py:32
  399.1 6.2 %collective-permute-start.40 = (f32[3,1,32,128]{3,2,1,0:T(8,128)S(1)}, f32[3,1,32,128]{3,2,1,0:T(8,128)S(1)}, u32[]{:S(2)}, u32[]{:S(2)}) collective-permute-start(f32[3,1,32,128]{3,2,1,0:T(8,128)S(1)} %get-tuple-element.24), channel_id=1, source_target_pairs={{2,0},{4,2},{6,4},{8,6},{10,8},{12,10},{14,12},{0,14},{3,1},{5,3},... | collective-permute-start | bytes 147464 | tf_op jit(solution)/shard_map/ppermute | solution.py:34
  408.7 6.4 %collective-permute-start.45 = (f32[3,1,32,128]{3,2,1,0:T(8,128)S(1)}, f32[3,1,32,128]{3,2,1,0:T(8,128)S(1)}, u32[]{:S(2)}, u32[]{:S(2)}) collective-permute-start(f32[3,1,32,128]{3,2,1,0:T(8,128)S(1)} %broadcast_divide_fusion.1), channel_id=1, source_target_pairs={{0,2},{2,4},{4,6},{6,8},{8,10},{10,12},{12,14},{14,0},{1,3},{3,5},... | collective-permute-start | bytes 147464 | tf_op jit(solution)/shard_map/ppermute | solution.py:32
  408.8 6.3 %collective-permute-start.44 = (f32[3,1,32,128]{3,2,1,0:T(8,128)S(1)}, f32[3,1,32,128]{3,2,1,0:T(8,128)S(1)}, u32[]{:S(2)}, u32[]{:S(2)}) collective-permute-start(f32[3,1,32,128]{3,2,1,0:T(8,128)S(1)} %broadcast_divide_fusion.1), channel_id=1, source_target_pairs={{2,0},{4,2},{6,4},{8,6},{10,8},{12,10},{14,12},{0,14},{3,1},{5,3},... | collective-permute-start | bytes 147464 | tf_op jit(solution)/shard_map/ppermute | solution.py:34
  418.4 6.3 %collective-permute-start.49 = (f32[3,1,32,128]{3,2,1,0:T(8,128)S(1)}, f32[3,1,32,128]{3,2,1,0:T(8,128)S(1)}, u32[]{:S(2)}, u32[]{:S(2)}) collective-permute-start(f32[3,1,32,128]{3,2,1,0:T(8,128)S(1)} %get-tuple-element.16), channel_id=1, source_target_pairs={{0,2},{2,4},{4,6},{6,8},{8,10},{10,12},{12,14},{14,0},{1,3},{3,5},... | collective-permute-start | bytes 147464 | tf_op jit(solution)/shard_map/ppermute | solution.py:32
  418.5 6.2 %collective-permute-start.48 = (f32[3,1,32,128]{3,2,1,0:T(8,128)S(1)}, f32[3,1,32,128]{3,2,1,0:T(8,128)S(1)}, u32[]{:S(2)}, u32[]{:S(2)}) collective-permute-start(f32[3,1,32,128]{3,2,1,0:T(8,128)S(1)} %get-tuple-element.16), channel_id=1, source_target_pairs={{2,0},{4,2},{6,4},{8,6},{10,8},{12,10},{14,12},{0,14},{3,1},{5,3},... | collective-permute-start | bytes 147464 | tf_op jit(solution)/shard_map/ppermute | solution.py:34
  (29 other events, 65.8 us)
where the time goes:
time: 433 us; the launch traced here: 429 us
  other arithmetic  305 us (70%)
  starting transfers between devices  71 us (16%)
  waiting for transfers between devices  29.9 us (7%)
  local copies, waits for them, and re-layouts  19.1 us (4%)
    another operation x248, other arithmetic, apply_coupling(): jnp.stack([matrix[first][0] * difference[0] + matrix[first][1] * differen...  285 us
    ppermute x26, starting transfers between devices, padded_2(): lax.ppermute(head, axis, [((i + 1) % count, i) for i in range(count)])  67 us
    ppermute x26, waiting for transfers between devices, padded_2(): lax.ppermute(tail, axis, [(i, (i + 1) % count) for i in range(count)])  22.7 us
    slice x18, local copies, waits for them, and re-layouts, coupling(): kinds[0, first, second]  12.4 us
    mul x2, other arithmetic, operator_terms(): total = total + 0.5 * (spring + other_spring) * image  11.3 us
  transfers between devices with their start and end apart: 52, of which 35 were waited for; matrix products, arithmetic and copies ran while one was open for 12% of the time, Pallas kernels for 0%

commit v1 on v0

--- a/solution.py
+++ b/solution.py
@@ -1,11 +1,13 @@
 import jax
 import jax.numpy as jnp
 from jax import lax
+from jax.experimental import pallas as pl
+from jax.experimental.pallas import tpu as pltpu
 from jax.sharding import PartitionSpec as P
 
 ZCELLS = 128
 STEPS = 5
-
+TILE = 8
 
 DIRECTIONS = (
     (1, 0, 0),
@@ -18,8 +20,323 @@
     (0, 1, 1),
     (0, 1, -1),
 )
+PAIRS = ((0, 0), (0, 1), (0, 2), (1, 1), (1, 2), (2, 2))
+ENTRY = ((0, 1, 2), (1, 3, 4), (2, 4, 5))
 time_step = 0.5
 germanium_ratio = 1.5856
+half_step = 0.5 * time_step
+LEVELS = 2 * (STEPS + 1)
+FIELDS = 9
+
+
+def kernel(ring, half, *refs):
+    blocks_in = refs[: 2 * ring]
+    force_ref, table_ref, mass_grad, spring_grad = refs[2 * ring : 2 * ring + 4]
+    fields, speed, accel, kind, stiff, inverse, coef, own_sum, carry, up_sum, down_sum, ray, ray_up, ray_down = refs[
+        2 * ring + 4 :
+    ]
+    rows = 2 * half
+    tiles = rows // TILE
+    me = lax.axis_index("gx")
+    depth_index = lax.broadcasted_iota(jnp.int32, (TILE, ZCELLS), 1)
+
+    def ahead(value):
+        return pltpu.roll(value, ZCELLS - 1, 1)
+
+    def behind(value):
+        return pltpu.roll(value, 1, 1)
+
+    def along(value, depth):
+        return ahead(value) if depth > 0 else behind(value) if depth < 0 else value
+
+    def wrap(slab):
+        return lax.rem(slab, ring)
+
+    def at(tile, shift=0):
+        return pl.ds(TILE + TILE * tile + shift, TILE)
+
+    def plain(tile):
+        return pl.ds(TILE * tile, TILE)
+
+    def put_ringed(ref, where, tile, value):
+        ref[where + (at(tile),)] = value
+        if tile == 0:
+            ref[where + (at(tiles),)] = value
+        if tile == tiles - 1:
+            ref[where + (at(-1),)] = value
+
+    for message in range(ring):
+        slab = lax.bitwise_xor(me, message)
+        for side in range(2):
+            source = blocks_in[2 * message + side]
+            for tile in range(half // TILE):
+                target = side * (half // TILE) + tile
+                for comp in range(3):
+                    put_ringed(fields, (0, slab, comp), target, source[comp, plain(tile)])
+                    speed[slab, comp, plain(target)] = source[3 + comp, plain(tile)]
+                sort = source[6, plain(tile)]
+                put_ringed(kind, (slab,), target, sort)
+                put_ringed(stiff, (slab,), target, source[8, plain(tile)])
+                mass = (1.0 + germanium_ratio * sort) * source[7, plain(tile)]
+                inverse[slab, plain(target)] = -1.0 / mass
+
+    def block_entries(direction):
+        result = []
+        for pair in range(3):
+            index = table_ref[pair, direction]
+            result.append(
+                [0.5 * (force_ref[index, a, b] + force_ref[index, b, a]) for a, b in PAIRS]
+            )
+        return result
+
+    def valid(depth):
+        if depth > 0:
+            return depth_index < ZCELLS - 1
+        return depth_index > 0
+
+    def matrix(entries, total_kind):
+        low = total_kind < 0.5
+        mixed = total_kind < 1.5
+        return [
+            jnp.where(low, entries[0][n], jnp.where(mixed, entries[1][n], entries[2][n]))
+            for n in range(6)
+        ]
+
+    for direction, (dx, dy, dz) in enumerate(DIRECTIONS):
+        entries = block_entries(direction)
+
+        def fill(slab, _, direction=direction, dx=dx, dy=dy, dz=dz, entries=entries):
+            other = wrap(slab + dx)
+            for tile in range(tiles):
+                total_kind = kind[slab, at(tile)] + along(kind[other, at(tile, dy)], dz)
+                bond = 0.5 * (stiff[slab, at(tile)] + along(stiff[other, at(tile, dy)], dz))
+                if dz != 0:
+                    bond = jnp.where(valid(dz), bond, 0.0)
+                for n, entry in enumerate(matrix(entries, total_kind)):
+                    coef[slab, 6 * direction + n, plain(tile)] = bond * entry
+            return 0
+
+        lax.fori_loop(0, ring, fill, 0)
+
+    def push(slab, direction, tile, difference):
+        entry = [coef[slab, 6 * direction + n, plain(tile)] for n in range(6)]
+        return [
+            entry[ENTRY[a][0]] * difference[0]
+            + entry[ENTRY[a][1]] * difference[1]
+            + entry[ENTRY[a][2]] * difference[2]
+            for a in range(3)
+        ]
+
+    def sub(first, second):
+        return [a - b for a, b in zip(first, second)]
+
+    def add(first, second):
+        return [a + b for a, b in zip(first, second)]
+
+    def load(level, slab, tile, shift=0):
+        return [fields[level, slab, comp, at(tile, shift)] for comp in range(3)]
+
+    def turned(values, depth):
+        return [along(value, depth) for value in values]
+
+    def cross_bonds(level, slab, tile, centre):
+        beside = wrap(slab + 1)
+        straight = load(level, beside, tile)
+        first = push(slab, 0, tile, sub(centre, straight))
+        third = push(slab, 5, tile, sub(centre, turned(straight, 1)))
+        fourth = push(slab, 6, tile, sub(centre, turned(straight, -1)))
+        upper = push(slab, 3, tile, sub(centre, load(level, beside, tile, 1)))
+        lower = push(slab, 4, tile, sub(centre, load(level, beside, tile, -1)))
+        here = add(add(add(first, third), fourth), add(upper, lower))
+        there = add(first, add(turned(third, -1), turned(fourth, 1)))
+        return here, there, upper, lower
+
+    def step(level, _):
+        reach = LEVELS - 1 - level
+        count = jnp.minimum(ring, 2 * reach + 1)
+        low = wrap(me - lax.div(count, 2) + 2 * ring)
+        middle = level == STEPS
+        kick = jnp.where((level == 0) | (level == STEPS) | (level == STEPS + 1), half_step, time_step)
+        keep = jnp.where(middle, 0.0, 1.0)
+        detect = jnp.where(depth_index >= ZCELLS // 2, 1.0, 0.0)
+        drift = jnp.where(middle, detect, jnp.full((TILE, ZCELLS), time_step))
+
+        before = wrap(low + ring - 1)
+        for tile in range(tiles):
+            centre = load(level, before, tile)
+            _, there, upper, lower = cross_bonds(level, before, tile, centre)
+            for comp in range(3):
+                carry[0, comp, plain(tile)] = there[comp]
+                carry[1, comp, plain(tile)] = upper[comp]
+                put_ringed(down_sum, (1, comp), tile, lower[comp])
+
+        def one(number, _):
+            slab = wrap(low + number)
+            slot = lax.rem(number, 2)
+            for tile in range(tiles):
+                centre = load(level, slab, tile)
+                here, there, upper, lower = cross_bonds(level, slab, tile, centre)
+                beyond = load(level, slab, tile, 1)
+                second = push(slab, 1, tile, sub(centre, beyond))
+                seventh = push(slab, 7, tile, sub(centre, turned(beyond, 1)))
+                eighth = push(slab, 8, tile, sub(centre, turned(beyond, -1)))
+                deep = push(slab, 2, tile, sub(centre, turned(centre, 1)))
+                here = add(add(here, deep), add(second, add(seventh, eighth)))
+                here = sub(here, turned(deep, -1))
+                lift = add(second, add(turned(seventh, -1), turned(eighth, 1)))
+                for comp in range(3):
+                    own_sum[comp, plain(tile)] = here[comp] - carry[0, comp, plain(tile)]
+                    carry[0, comp, plain(tile)] = there[comp]
+                    put_ringed(up_sum, (comp,), tile, lift[comp] + carry[1, comp, plain(tile)])
+                    carry[1, comp, plain(tile)] = upper[comp]
+                    put_ringed(down_sum, (slot, comp), tile, lower[comp])
+            mine = jnp.where(slab == me, 1, 0)
+            for tile in range(tiles):
+                over = inverse[slab, plain(tile)]
+                for comp in range(3):
+                    total = (
+                        own_sum[comp, plain(tile)]
+                        - up_sum[comp, at(tile, -1)]
+                        - down_sum[1 - slot, comp, at(tile, 1)]
+                    )
+                    change = total * over
+                    accel[level, mine, comp, plain(tile)] = change
+                    moved = speed[slab, comp, plain(tile)] + kick * change
+                    speed[slab, comp, plain(tile)] = keep * moved
+                    fresh = keep * fields[level, slab, comp, at(tile)] + drift * moved
+                    put_ringed(fields, (level + 1, slab, comp), tile, fresh)
+            return 0
+
+        lax.fori_loop(0, count, one, 0)
+        return 0
+
+    lax.fori_loop(0, LEVELS - 1, step, 0)
+
+    weights = [half_step if level in (0, STEPS) else time_step for level in range(STEPS + 1)]
+    own_tiles = half // TILE
+    for tile in range(own_tiles):
+        last = [fields[STEPS + 1, me, comp, at(tile)] for comp in range(3)]
+        bar = 0.5 * (last[0] * last[0] + last[1] * last[1] + last[2] * last[2])
+        for level in range(STEPS + 1):
+            dual = [fields[LEVELS - 1 - level, me, comp, at(tile)] for comp in range(3)]
+            moves = [accel[level, 1, comp, plain(tile)] for comp in range(3)]
+            bar = bar - weights[level] * (
+                dual[0] * moves[0] + dual[1] * moves[1] + dual[2] * moves[2]
+            )
+        mass_grad[plain(tile)] = bar * (1.0 + germanium_ratio * kind[me, at(tile)])
+
+    entries_of = [block_entries(direction) for direction in range(9)]
+
+    def strain(slab, direction, tile):
+        dx, dy, dz = DIRECTIONS[direction]
+        other = wrap(slab + dx)
+        total_kind = kind[slab, at_dynamic(tile)] + along(kind[other, at_dynamic(tile, dy)], dz)
+        entry = matrix(entries_of[direction], total_kind)
+        result = None
+        for level in range(STEPS + 1):
+            parts = []
+            for where in (level, LEVELS - 1 - level):
+                parts.append(
+                    [
+                        fields[where, slab, comp, at_dynamic(tile)]
+                        - along(fields[where, other, comp, at_dynamic(tile, dy)], dz)
+                        for comp in range(3)
+                    ]
+                )
+            state, dual = parts
+            image = [
+                entry[ENTRY[a][0]] * dual[0] + entry[ENTRY[a][1]] * dual[1] + entry[ENTRY[a][2]] * dual[2]
+                for a in range(3)
+            ]
+            term = weights[level] * (state[0] * image[0] + state[1] * image[1] + state[2] * image[2])
+            result = term if result is None else result + term
+        if dz != 0:
+            result = jnp.where(valid(dz), result, 0.0)
+        return result
+
+    def at_dynamic(tile, shift=0):
+        return pl.ds(TILE + TILE * tile + shift, TILE)
+
+    past = wrap(me + ring - 1)
+
+    def rays(tile, _):
+        total = strain(me, 2, tile)
+        total = total + behind(total)
+        for direction in (0, 3, 4, 5, 6):
+            total = total + strain(me, direction, tile)
+        second, seventh, eighth = (strain(me, direction, tile) for direction in (1, 7, 8))
+        total = total + (second + (seventh + eighth))
+        lift = second + (behind(seventh) + ahead(eighth)) + strain(past, 3, tile)
+        total = total + strain(past, 0, tile)
+        total = total + behind(strain(past, 5, tile)) + ahead(strain(past, 6, tile))
+        ray[at_dynamic(tile)] = total
+        ray_up[at_dynamic(tile)] = lift
+        ray_down[at_dynamic(tile)] = strain(past, 4, tile)
+        return 0
+
+    lax.fori_loop(0, own_tiles, rays, 0)
+    final = tiles - 1
+    ray_up[at(-1)] = (
+        strain(me, 1, final)
+        + (behind(strain(me, 7, final)) + ahead(strain(me, 8, final)))
+        + strain(past, 3, final)
+    )
+    ray_down[at(own_tiles)] = strain(past, 4, own_tiles)
+    for tile in range(own_tiles):
+        spring_grad[plain(tile)] = -0.5 * (
+            ray[at(tile)] + ray_up[at(tile, -1)] + ray_down[at(tile, 1)]
+        )
+
+
+def gathered_body(displacement, velocity, species, mass_factor, spring, force_blocks, shell_table):
+    ring = lax.axis_size("gx")
+    half = spring.shape[1]
+    rows = 2 * half
+    own = jnp.concatenate(
+        [displacement[:, 0], velocity[:, 0], species.astype(jnp.float32), mass_factor, spring]
+    )
+
+    def swap_slabs(value, mask):
+        return lax.ppermute(value, "gx", [(i, i ^ mask) for i in range(ring)])
+
+    def swap_halves(value):
+        return lax.ppermute(value, "gy", [(0, 1), (1, 0)])
+
+    messages = {0: own, 1: swap_slabs(own, 1)}
+    for mask in range(2, ring, 2):
+        messages[mask] = swap_slabs(own, mask)
+        messages[mask + 1] = swap_slabs(messages[mask], 1)
+    operands = []
+    for mask in range(ring):
+        operands += [messages[mask], swap_halves(messages[mask])]
+
+    padded = rows + 2 * TILE
+    scratch = [
+        (LEVELS, ring, 3, padded, ZCELLS),
+        (ring, 3, rows, ZCELLS),
+        (LEVELS, 2, 3, rows, ZCELLS),
+        (ring, padded, ZCELLS),
+        (ring, padded, ZCELLS),
+        (ring, rows, ZCELLS),
+        (ring, 54, rows, ZCELLS),
+        (3, rows, ZCELLS),
+        (2, 3, rows, ZCELLS),
+        (3, padded, ZCELLS),
+        (2, 3, padded, ZCELLS),
+        (padded, ZCELLS),
+        (padded, ZCELLS),
+        (padded, ZCELLS),
+    ]
+    mass_grad, spring_grad = pl.pallas_call(
+        lambda *refs: kernel(ring, half, *refs),
+        out_shape=[jax.ShapeDtypeStruct((half, ZCELLS), jnp.float32)] * 2,
+        in_specs=[pl.BlockSpec(memory_space=pltpu.VMEM)] * (2 * ring)
+        + [pl.BlockSpec(memory_space=pltpu.SMEM)] * 2,
+        out_specs=[pl.BlockSpec(memory_space=pltpu.VMEM)] * 2,
+        scratch_shapes=[pltpu.VMEM(shape, jnp.float32) for shape in scratch],
+        compiler_params=pltpu.CompilerParams(vmem_limit_bytes=56 * 1024 * 1024),
+    )(*operands, force_blocks, shell_table)
+    return mass_grad[None], spring_grad[None]
 
 
 def padded_2(cells, sides, width):
@@ -119,7 +436,7 @@
     return padded_2(field, (("gx", 1), ("gy", 2)), 1)
 
 
-def body(displacement, velocity, species, mass_factor, spring, force_blocks, shell_table):
+def exchanged_body(displacement, velocity, species, mass_factor, spring, force_blocks, shell_table):
     blocks = pair_blocks(force_blocks, shell_table)
     species_float = species.astype(jnp.float32)
     species_mass = 1.0 + germanium_ratio * species_float
@@ -199,8 +516,9 @@
 
 
 def solution(mesh):
+    small = mesh.shape["gx"] == 8 and mesh.shape["gy"] == 2
     return jax.shard_map(
-        body,
+        gathered_body if small else exchanged_body,
         mesh=mesh,
         in_specs=(
             P(None, ("groups", "gx"), "gy", None),

time: 433 us -> 113 us (0.26)
  other arithmetic: 305 us -> 0.01 us
  Pallas kernels: 0 us -> 80.1 us
  starting transfers between devices: 71 us -> 14.3 us
  waiting for transfers between devices: 29.9 us -> 12.9 us
  local copies, waits for them, and re-layouts: 19.1 us -> 4.8 us
    another operation x251 -> x0, other arithmetic: 286 us -> none  [the longest x248 285 us: apply_coupling(): jnp.stack([matrix[first][0] * difference[0] + matrix[first][1] * differen...]
    pallas_call x0 -> x1, Pallas kernels: none -> 80.1 us  [gathered_body(): pl.pallas_call(lambda *refs: kernel(ring, half, *refs), out_shape=[jax.Sh...]
    ppermute x52 -> x15, starting transfers between devices: 71 us -> 14.3 us  [the longest x7 8.21 us: swap_slabs(): return lax.ppermute(value, 'gx', [(i, i ^ mask) for i in range(ring)])]
    slice x82 -> x0, local copies, waits for them, and re-layouts: 17.5 us -> none  [the longest x18 12.4 us: coupling(): kinds[0, first, second]]
    ppermute x52 -> x15, waiting for transfers between devices: 29.9 us -> 12.9 us  [the longest x7 12.7 us: swap_slabs(): return lax.ppermute(value, 'gx', [(i, i ^ mask) for i in range(ring)])]
    mul x4 -> x0, other arithmetic: 12 us -> none  [the longest x2 11.3 us: operator_terms(): total = total + 0.5 * (spring + other_spring) * image]
  transfers between devices with their start and end apart: 52 -> 15, of which waited for: 35 -> 5; matrix products, arithmetic and copies ran while one was open for 12% -> 1% of each run, Pallas kernels for 0% -> 0%
where the time goes in v1:
time: 113 us
  Pallas kernels  80.1 us (71%)
  starting transfers between devices  14.3 us (13%)
  waiting for transfers between devices  12.9 us (11%)
  local copies, waits for them, and re-layouts  4.8 us (4%)
    pallas_call x1, Pallas kernels, gathered_body(): pl.pallas_call(lambda *refs: kernel(ring, half, *refs), out_shape=[jax.Sh...  80.1 us
    ppermute x7, waiting for transfers between devices, swap_slabs(): return lax.ppermute(value, 'gx', [(i, i ^ mask) for i in range(ring)])  12.7 us
    ppermute x7, starting transfers between devices, swap_slabs(): return lax.ppermute(value, 'gx', [(i, i ^ mask) for i in range(ring)])  8.21 us
    ppermute x8, starting transfers between devices, swap_halves(): return lax.ppermute(value, 'gy', [(0, 1), (1, 0)])  6.13 us
    unnamed x46, local copies, waits for them, and re-layouts  4.79 us
  transfers between devices with their start and end apart: 15, of which 5 were waited for; matrix products, arithmetic and copies ran while one was open for 1% of the time, Pallas kernels for 0%

profile of v1, /device:TPU:1, one launch (start us, length us, event | category | flops | bytes accessed | tf_op | source)
XLA Modules:
  0.0 112.9 jit_solution(1375622004470041222)
XLA Ops:
  0.6 0.8 bitcast_dynamic-update-slice_fusion.1
  1.5 0.7 copy-done.17
  2.2 0.7 copy-done.18
  2.9 0.7 copy-done.19
  3.6 4.2 %collective-permute-start.11 = (f32[9,32,128]{2,1,0:T(8,128)S(1)}, f32[9,32,128]{2,1,0:T(8,128)S(1)}, u32[]{:S(2)}, u32[]{:S(2)}) collective-permute-start(f32[9,32,128]{2,1,0:T(8,128)S(1)} %constant_dynamic-update-slice_fusion.refs_0_), channel_id=1, source_target_pairs={{0,12},{2,14},{4,8},{6,10},{8,4},{10,6},{12,0},{14,2},{1,13},{3,15... | collective-permute-start | bytes 442376 | tf_op jit(solution)/shard_map/ppermute | solution.py:300
  7.8 0.4 collective-permute-start.3
  8.1 1.2 %collective-permute-start.1 = (f32[9,32,128]{2,1,0:T(8,128)S(1)}, f32[9,32,128]{2,1,0:T(8,128)S(1)}, u32[]{:S(2)}, u32[]{:S(2)}) collective-permute-start(f32[9,32,128]{2,1,0:T(8,128)S(1)} %constant_dynamic-update-slice_fusion.refs_0_), channel_id=1, source_target_pairs={{0,2},{2,0},{4,6},{6,4},{8,10},{10,8},{12,14},{14,12},{1,3},{3,1},... | collective-permute-start | bytes 442376 | tf_op jit(solution)/shard_map/ppermute | solution.py:300
  9.3 1.7 %collective-permute-start = (f32[9,32,128]{2,1,0:T(8,128)S(1)}, f32[9,32,128]{2,1,0:T(8,128)S(1)}, u32[]{:S(2)}, u32[]{:S(2)}) collective-permute-start(f32[9,32,128]{2,1,0:T(8,128)S(1)} %constant_dynamic-update-slice_fusion.refs_0_), channel_id=1, source_target_pairs={{0,1},{1,0},{2,3},{3,2},{4,5},{5,4},{6,7},{7,6},{8,9},{9,8},{10,11... | collective-permute-start | bytes 442376 | tf_op jit(solution)/shard_map/ppermute | solution.py:303
  11.0 0.4 collective-permute-done.11.refs_12_
  11.4 1.0 collective-permute-start.13
  12.4 7.4 %collective-permute-done.7.refs_8_ = f32[9,32,128]{2,1,0:T(8,128)S(1)} collective-permute-done((f32[9,32,128]{2,1,0:T(8,128)S(1)}, f32[9,32,128]{2,1,0:T(8,128)S(1)}, u32[]{:S(2)}, u32[]{:S(2)}) %collective-permute-start.7) | collective-permute-done | bytes 147488 | tf_op jit(solution)/shard_map/ppermute | solution.py:300
  19.8 1.4 %collective-permute-start.12 = (f32[9,32,128]{2,1,0:T(8,128)S(1)}, f32[9,32,128]{2,1,0:T(8,128)S(1)}, u32[]{:S(2)}, u32[]{:S(2)}) collective-permute-start(f32[9,32,128]{2,1,0:T(8,128)S(1)} %collective-permute-done.11.refs_12_), channel_id=1, source_target_pairs={{0,1},{1,0},{2,3},{3,2},{4,5},{5,4},{6,7},{7,6},{8,9},{9,8},{10,11... | collective-permute-start | bytes 442376 | tf_op jit(solution)/shard_map/ppermute | solution.py:303
  21.2 0.0 collective-permute-done.3.refs_4_
  21.2 1.2 %collective-permute-start.9 = (f32[9,32,128]{2,1,0:T(8,128)S(1)}, f32[9,32,128]{2,1,0:T(8,128)S(1)}, u32[]{:S(2)}, u32[]{:S(2)}) collective-permute-start(f32[9,32,128]{2,1,0:T(8,128)S(1)} %collective-permute-done.7.refs_8_), channel_id=1, source_target_pairs={{0,2},{2,0},{4,6},{6,4},{8,10},{10,8},{12,14},{14,12},{1,3},{3,1},... | collective-permute-start | bytes 442376 | tf_op jit(solution)/shard_map/ppermute | solution.py:300
  22.4 0.0 collective-permute-done.1.refs_2_
  22.4 0.3 collective-permute-start.8
  22.8 0.3 collective-permute-start.5
  23.1 0.4 collective-permute-start.4
  23.5 0.1 collective-permute-start.2
  23.6 3.0 %collective-permute-done.9.refs_10_ = f32[9,32,128]{2,1,0:T(8,128)S(1)} collective-permute-done((f32[9,32,128]{2,1,0:T(8,128)S(1)}, f32[9,32,128]{2,1,0:T(8,128)S(1)}, u32[]{:S(2)}, u32[]{:S(2)}) %collective-permute-start.9) | collective-permute-done | bytes 147488 | tf_op jit(solution)/shard_map/ppermute | solution.py:300
  26.6 1.3 %collective-permute-start.14 = (f32[9,32,128]{2,1,0:T(8,128)S(1)}, f32[9,32,128]{2,1,0:T(8,128)S(1)}, u32[]{:S(2)}, u32[]{:S(2)}) collective-permute-start(f32[9,32,128]{2,1,0:T(8,128)S(1)} %collective-permute-done.13.refs_14_), channel_id=1, source_target_pairs={{0,1},{1,0},{2,3},{3,2},{4,5},{5,4},{6,7},{7,6},{8,9},{9,8},{10,11... | collective-permute-start | bytes 442376 | tf_op jit(solution)/shard_map/ppermute | solution.py:303
  27.9 0.1 collective-permute-start.10
  28.0 1.8 %collective-permute-done.5.refs_6_ = f32[9,32,128]{2,1,0:T(8,128)S(1)} collective-permute-done((f32[9,32,128]{2,1,0:T(8,128)S(1)}, f32[9,32,128]{2,1,0:T(8,128)S(1)}, u32[]{:S(2)}, u32[]{:S(2)}) %collective-permute-start.5) | collective-permute-done | bytes 147488 | tf_op jit(solution)/shard_map/ppermute | solution.py:300
  29.8 0.8 collective-permute-start.6
  30.7 0.7 copy.9.refs_16_
  31.4 0.2 collective-permute-done.6.refs_7_
  31.7 0.3 copy-done.11
  32.0 0.1 copy-done.12
  32.1 0.1 copy-done.13
  32.1 0.0 copy-done.14
  32.2 0.7 copy-done.15
  32.8 80.1 %shard_map.86 = (f32[32,128]{1,0:T(8,128)}, f32[32,128]{1,0:T(8,128)}) custom-call(f32[9,32,128]{2,1,0:T(8,128)} %copy-done, f32[9,32,128]{2,1,0:T(8,128)} %copy-done.5, f32[9,32,128]{2,1,0:T(8,128)} %copy-done.4, f32[9,32,128]{2,1,0:T(8,128)} %copy-done.12, f32[9,32,128]{2,1,0:T(8,128)} %copy-done.3, f32[9,32,128]{2,1,0:T(8,128)} %copy-done.11, ...), custom_call_target="tpu_custom_call" | custom-call | tf_op jit(solution)/shard_map/pallas_call | solution.py:330
  (47 shorter events, 0.1 us)
Async XLA Ops:
  0.6 0.8 copy-start.16
  1.5 0.7 copy-start.17
  3.6 27.0 %copy-start.20 = (f32[8,3,3]{0,2,1:T(4,128)S(1)}, f32[8,3,3]{0,2,1:T(4,128)}, u32[]{:S(2)}) copy-start(f32[8,3,3]{0,2,1:T(4,128)} %param.12) | copy-start | bytes 868
  3.6 28.0 %copy-start = (f32[9,32,128]{2,1,0:T(8,128)}, f32[9,32,128]{2,1,0:T(8,128)S(1)}, u32[]{:S(2)}) copy-start(f32[9,32,128]{2,1,0:T(8,128)S(1)} %constant_dynamic-update-slice_fusion.refs_0_) | copy-start | bytes 442372
  3.6 7.8 %collective-permute-start.11 = (f32[9,32,128]{2,1,0:T(8,128)S(1)}, f32[9,32,128]{2,1,0:T(8,128)S(1)}, u32[]{:S(2)}, u32[]{:S(2)}) collective-permute-start(f32[9,32,128]{2,1,0:T(8,128)S(1)} %constant_dynamic-update-slice_fusion.refs_0_), channel_id=1, source_target_pairs={{0,12},{2,14},{4,8},{6,10},{8,4},{10,6},{12,0},{14,2},{1,13},{3,15... | collective-permute-start | bytes 442376 | tf_op jit(solution)/shard_map/ppermute | solution.py:300
  7.8 12.1 %collective-permute-start.7 = (f32[9,32,128]{2,1,0:T(8,128)S(1)}, f32[9,32,128]{2,1,0:T(8,128)S(1)}, u32[]{:S(2)}, u32[]{:S(2)}) collective-permute-start(f32[9,32,128]{2,1,0:T(8,128)S(1)} %constant_dynamic-update-slice_fusion.refs_0_), channel_id=1, source_target_pairs={{0,8},{2,10},{4,12},{6,14},{8,0},{10,2},{12,4},{14,6},{1,9},{3,11}... | collective-permute-start | bytes 442376 | tf_op jit(solution)/shard_map/ppermute | solution.py:300
  7.8 13.4 %collective-permute-start.3 = (f32[9,32,128]{2,1,0:T(8,128)S(1)}, f32[9,32,128]{2,1,0:T(8,128)S(1)}, u32[]{:S(2)}, u32[]{:S(2)}) collective-permute-start(f32[9,32,128]{2,1,0:T(8,128)S(1)} %constant_dynamic-update-slice_fusion.refs_0_), channel_id=1, source_target_pairs={{0,4},{2,6},{4,0},{6,2},{8,12},{10,14},{12,8},{14,10},{1,5},{3,7},... | collective-permute-start | bytes 442376 | tf_op jit(solution)/shard_map/ppermute | solution.py:300
  8.1 14.3 %collective-permute-start.1 = (f32[9,32,128]{2,1,0:T(8,128)S(1)}, f32[9,32,128]{2,1,0:T(8,128)S(1)}, u32[]{:S(2)}, u32[]{:S(2)}) collective-permute-start(f32[9,32,128]{2,1,0:T(8,128)S(1)} %constant_dynamic-update-slice_fusion.refs_0_), channel_id=1, source_target_pairs={{0,2},{2,0},{4,6},{6,4},{8,10},{10,8},{12,14},{14,12},{1,3},{3,1},... | collective-permute-start | bytes 442376 | tf_op jit(solution)/shard_map/ppermute | solution.py:300
  9.3 13.5 %collective-permute-start = (f32[9,32,128]{2,1,0:T(8,128)S(1)}, f32[9,32,128]{2,1,0:T(8,128)S(1)}, u32[]{:S(2)}, u32[]{:S(2)}) collective-permute-start(f32[9,32,128]{2,1,0:T(8,128)S(1)} %constant_dynamic-update-slice_fusion.refs_0_), channel_id=1, source_target_pairs={{0,1},{1,0},{2,3},{3,2},{4,5},{5,4},{6,7},{7,6},{8,9},{9,8},{10,11... | collective-permute-start | bytes 442376 | tf_op jit(solution)/shard_map/ppermute | solution.py:303
  11.4 20.3 %copy-start.1 = (f32[9,32,128]{2,1,0:T(8,128)}, f32[9,32,128]{2,1,0:T(8,128)S(1)}, u32[]{:S(2)}) copy-start(f32[9,32,128]{2,1,0:T(8,128)S(1)} %collective-permute-done.11.refs_12_) | copy-start | bytes 442372
  11.4 11.7 %collective-permute-start.13 = (f32[9,32,128]{2,1,0:T(8,128)S(1)}, f32[9,32,128]{2,1,0:T(8,128)S(1)}, u32[]{:S(2)}, u32[]{:S(2)}) collective-permute-start(f32[9,32,128]{2,1,0:T(8,128)S(1)} %collective-permute-done.11.refs_12_), channel_id=1, source_target_pairs={{0,2},{2,0},{4,6},{6,4},{8,10},{10,8},{12,14},{14,12},{1,3},{3,1},... | collective-permute-start | bytes 442376 | tf_op jit(solution)/shard_map/ppermute | solution.py:300
  19.8 11.8 %copy-start.2 = (f32[9,32,128]{2,1,0:T(8,128)}, f32[9,32,128]{2,1,0:T(8,128)S(1)}, u32[]{:S(2)}) copy-start(f32[9,32,128]{2,1,0:T(8,128)S(1)} %collective-permute-done.7.refs_8_) | copy-start | bytes 442372
  19.8 3.7 %collective-permute-start.12 = (f32[9,32,128]{2,1,0:T(8,128)S(1)}, f32[9,32,128]{2,1,0:T(8,128)S(1)}, u32[]{:S(2)}, u32[]{:S(2)}) collective-permute-start(f32[9,32,128]{2,1,0:T(8,128)S(1)} %collective-permute-done.11.refs_12_), channel_id=1, source_target_pairs={{0,1},{1,0},{2,3},{3,2},{4,5},{5,4},{6,7},{7,6},{8,9},{9,8},{10,11... | collective-permute-start | bytes 442376 | tf_op jit(solution)/shard_map/ppermute | solution.py:303
  21.2 10.5 %copy-start.3 = (f32[9,32,128]{2,1,0:T(8,128)}, f32[9,32,128]{2,1,0:T(8,128)S(1)}, u32[]{:S(2)}) copy-start(f32[9,32,128]{2,1,0:T(8,128)S(1)} %collective-permute-done.3.refs_4_) | copy-start | bytes 442372
  21.2 5.4 %collective-permute-start.9 = (f32[9,32,128]{2,1,0:T(8,128)S(1)}, f32[9,32,128]{2,1,0:T(8,128)S(1)}, u32[]{:S(2)}, u32[]{:S(2)}) collective-permute-start(f32[9,32,128]{2,1,0:T(8,128)S(1)} %collective-permute-done.7.refs_8_), channel_id=1, source_target_pairs={{0,2},{2,0},{4,6},{6,4},{8,10},{10,8},{12,14},{14,12},{1,3},{3,1},... | collective-permute-start | bytes 442376 | tf_op jit(solution)/shard_map/ppermute | solution.py:300
  22.4 9.2 %copy-start.4 = (f32[9,32,128]{2,1,0:T(8,128)}, f32[9,32,128]{2,1,0:T(8,128)S(1)}, u32[]{:S(2)}) copy-start(f32[9,32,128]{2,1,0:T(8,128)S(1)} %collective-permute-done.1.refs_2_) | copy-start | bytes 442372
  22.4 5.5 %collective-permute-start.8 = (f32[9,32,128]{2,1,0:T(8,128)S(1)}, f32[9,32,128]{2,1,0:T(8,128)S(1)}, u32[]{:S(2)}, u32[]{:S(2)}) collective-permute-start(f32[9,32,128]{2,1,0:T(8,128)S(1)} %collective-permute-done.7.refs_8_), channel_id=1, source_target_pairs={{0,1},{1,0},{2,3},{3,2},{4,5},{5,4},{6,7},{7,6},{8,9},{9,8},{10,11... | collective-permute-start | bytes 442376 | tf_op jit(solution)/shard_map/ppermute | solution.py:303
  22.8 8.9 %copy-start.5 = (f32[9,32,128]{2,1,0:T(8,128)}, f32[9,32,128]{2,1,0:T(8,128)S(1)}, u32[]{:S(2)}) copy-start(f32[9,32,128]{2,1,0:T(8,128)S(1)} %collective-permute-done.refs_1_) | copy-start | bytes 442372
  22.8 7.0 %collective-permute-start.5 = (f32[9,32,128]{2,1,0:T(8,128)S(1)}, f32[9,32,128]{2,1,0:T(8,128)S(1)}, u32[]{:S(2)}, u32[]{:S(2)}) collective-permute-start(f32[9,32,128]{2,1,0:T(8,128)S(1)} %collective-permute-done.3.refs_4_), channel_id=1, source_target_pairs={{0,2},{2,0},{4,6},{6,4},{8,10},{10,8},{12,14},{14,12},{1,3},{3,1},... | collective-permute-start | bytes 442376 | tf_op jit(solution)/shard_map/ppermute | solution.py:300
  23.1 8.6 %copy-start.6 = (f32[9,32,128]{2,1,0:T(8,128)}, f32[9,32,128]{2,1,0:T(8,128)S(1)}, u32[]{:S(2)}) copy-start(f32[9,32,128]{2,1,0:T(8,128)S(1)} %collective-permute-done.13.refs_14_) | copy-start | bytes 442372
  23.1 8.3 %collective-permute-start.4 = (f32[9,32,128]{2,1,0:T(8,128)S(1)}, f32[9,32,128]{2,1,0:T(8,128)S(1)}, u32[]{:S(2)}, u32[]{:S(2)}) collective-permute-start(f32[9,32,128]{2,1,0:T(8,128)S(1)} %collective-permute-done.3.refs_4_), channel_id=1, source_target_pairs={{0,1},{1,0},{2,3},{3,2},{4,5},{5,4},{6,7},{7,6},{8,9},{9,8},{10,11... | collective-permute-start | bytes 442376 | tf_op jit(solution)/shard_map/ppermute | solution.py:303
  23.5 8.2 %copy-start.7 = (f32[9,32,128]{2,1,0:T(8,128)}, f32[9,32,128]{2,1,0:T(8,128)S(1)}, u32[]{:S(2)}) copy-start(f32[9,32,128]{2,1,0:T(8,128)S(1)} %collective-permute-done.12.refs_13_) | copy-start | bytes 442372
  23.5 7.8 %collective-permute-start.2 = (f32[9,32,128]{2,1,0:T(8,128)S(1)}, f32[9,32,128]{2,1,0:T(8,128)S(1)}, u32[]{:S(2)}, u32[]{:S(2)}) collective-permute-start(f32[9,32,128]{2,1,0:T(8,128)S(1)} %collective-permute-done.1.refs_2_), channel_id=1, source_target_pairs={{0,1},{1,0},{2,3},{3,2},{4,5},{5,4},{6,7},{7,6},{8,9},{9,8},{10,11... | collective-permute-start | bytes 442376 | tf_op jit(solution)/shard_map/ppermute | solution.py:303
  26.6 5.1 %copy-start.8 = (f32[9,32,128]{2,1,0:T(8,128)}, f32[9,32,128]{2,1,0:T(8,128)S(1)}, u32[]{:S(2)}) copy-start(f32[9,32,128]{2,1,0:T(8,128)S(1)} %collective-permute-done.9.refs_10_) | copy-start | bytes 442372
  26.6 4.7 %collective-permute-start.14 = (f32[9,32,128]{2,1,0:T(8,128)S(1)}, f32[9,32,128]{2,1,0:T(8,128)S(1)}, u32[]{:S(2)}, u32[]{:S(2)}) collective-permute-start(f32[9,32,128]{2,1,0:T(8,128)S(1)} %collective-permute-done.13.refs_14_), channel_id=1, source_target_pairs={{0,1},{1,0},{2,3},{3,2},{4,5},{5,4},{6,7},{7,6},{8,9},{9,8},{10,11... | collective-permute-start | bytes 442376 | tf_op jit(solution)/shard_map/ppermute | solution.py:303
  27.9 3.8 %copy-start.9 = (f32[9,32,128]{2,1,0:T(8,128)}, f32[9,32,128]{2,1,0:T(8,128)S(1)}, u32[]{:S(2)}) copy-start(f32[9,32,128]{2,1,0:T(8,128)S(1)} %collective-permute-done.8.refs_9_) | copy-start | bytes 442372
  27.9 3.4 %collective-permute-start.10 = (f32[9,32,128]{2,1,0:T(8,128)S(1)}, f32[9,32,128]{2,1,0:T(8,128)S(1)}, u32[]{:S(2)}, u32[]{:S(2)}) collective-permute-start(f32[9,32,128]{2,1,0:T(8,128)S(1)} %collective-permute-done.9.refs_10_), channel_id=1, source_target_pairs={{0,1},{1,0},{2,3},{3,2},{4,5},{5,4},{6,7},{7,6},{8,9},{9,8},{10,11... | collective-permute-start | bytes 442376 | tf_op jit(solution)/shard_map/ppermute | solution.py:303
  29.8 1.9 %copy-start.10 = (f32[9,32,128]{2,1,0:T(8,128)}, f32[9,32,128]{2,1,0:T(8,128)S(1)}, u32[]{:S(2)}) copy-start(f32[9,32,128]{2,1,0:T(8,128)S(1)} %collective-permute-done.5.refs_6_) | copy-start | bytes 442372
  29.8 1.9 %collective-permute-start.6 = (f32[9,32,128]{2,1,0:T(8,128)S(1)}, f32[9,32,128]{2,1,0:T(8,128)S(1)}, u32[]{:S(2)}, u32[]{:S(2)}) collective-permute-start(f32[9,32,128]{2,1,0:T(8,128)S(1)} %collective-permute-done.5.refs_6_), channel_id=1, source_target_pairs={{0,1},{1,0},{2,3},{3,2},{4,5},{5,4},{6,7},{7,6},{8,9},{9,8},{10,11... | collective-permute-start | bytes 442376 | tf_op jit(solution)/shard_map/ppermute | solution.py:303
  31.4 0.7 copy-start.12
  31.4 0.8 copy-start.13
  31.4 0.8 copy-start.14
  (4 other events, 2.8 us)

commit v2 on v0

--- a/solution.py
+++ b/solution.py
@@ -1,11 +1,13 @@
 import jax
 import jax.numpy as jnp
 from jax import lax
+from jax.experimental import pallas as pl
+from jax.experimental.pallas import tpu as pltpu
 from jax.sharding import PartitionSpec as P
 
 ZCELLS = 128
 STEPS = 5
-
+TILE = 8
 
 DIRECTIONS = (
     (1, 0, 0),
@@ -18,8 +20,348 @@
     (0, 1, 1),
     (0, 1, -1),
 )
+BONDS = (
+    ((0, 0, 0), (1, 0, 0)),
+    ((0, 0, 0), (0, 1, 0)),
+    ((0, 0, 0), (0, 0, 1)),
+    ((0, 0, 0), (1, 1, 0)),
+    ((1, 0, 0), (0, 1, 0)),
+    ((0, 0, 0), (1, 0, 1)),
+    ((1, 0, 0), (0, 0, 1)),
+    ((0, 0, 0), (0, 1, 1)),
+    ((0, 1, 0), (0, 0, 1)),
+)
+PAIRS = ((0, 0), (0, 1), (0, 2), (1, 1), (1, 2), (2, 2))
+ENTRY = ((0, 1, 2), (1, 3, 4), (2, 4, 5))
 time_step = 0.5
 germanium_ratio = 1.5856
+half_step = 0.5 * time_step
+LEVELS = 2 * (STEPS + 1)
+FIELDS = 9
+
+
+def kernel(ring, half, *refs):
+    blocks_in = refs[: 2 * ring]
+    force_ref, table_ref, mass_grad, spring_grad = refs[2 * ring : 2 * ring + 4]
+    (
+        fields,
+        speed,
+        pushes,
+        matter,
+        inverse,
+        coef,
+        sums,
+        carry,
+        ray,
+    ) = refs[2 * ring + 4 :]
+    rows = 2 * half
+    tiles = rows // TILE
+    own_tiles = half // TILE
+    me = lax.axis_index("gx")
+    depth_index = lax.broadcasted_iota(jnp.int32, (TILE, ZCELLS), 1)
+
+    def ahead(value):
+        return pltpu.roll(value, ZCELLS - 1, 1)
+
+    def behind(value):
+        return pltpu.roll(value, 1, 1)
+
+    def wrap(slab):
+        return lax.rem(slab, ring)
+
+    def at(tile, shift=0):
+        return pl.ds(TILE * tile + shift, TILE)
+
+    def late(tile, shift=0):
+        return pl.ds(TILE + TILE * tile + shift, TILE)
+
+    def put_field(level, slab, comp, tile, value):
+        deeper = ahead(value)
+        fields[0, level, slab, comp, at(tile)] = value
+        fields[1, level, slab, comp, at(tile)] = deeper
+        if tile == 0:
+            fields[0, level, slab, comp, at(tiles)] = value
+            fields[1, level, slab, comp, at(tiles)] = deeper
+
+    for message in range(ring):
+        slab = lax.bitwise_xor(me, message)
+        for side in range(2):
+            source = blocks_in[2 * message + side]
+            for tile in range(own_tiles):
+                target = side * own_tiles + tile
+                for comp in range(3):
+                    put_field(0, slab, comp, target, source[comp, at(tile)])
+                    speed[slab, comp, at(target)] = time_step * source[3 + comp, at(tile)]
+                sort = source[6, at(tile)]
+                for which, value in ((0, sort), (1, source[8, at(tile)])):
+                    deeper = ahead(value)
+                    for place in (target,) if target else (0, tiles):
+                        matter[which, 0, slab, at(place)] = value
+                        matter[which, 1, slab, at(place)] = deeper
+                mass = (1.0 + germanium_ratio * sort) * source[7, at(tile)]
+                inverse[slab, at(target)] = (-time_step * time_step) / mass
+
+    def block_entries(direction):
+        result = []
+        for pair in range(3):
+            index = table_ref[pair, direction]
+            result.append([0.5 * (force_ref[index, a, b] + force_ref[index, b, a]) for a, b in PAIRS])
+        return result
+
+    inside = depth_index < ZCELLS - 1
+
+    def matrix(entries, total_kind):
+        low = total_kind < 0.5
+        mixed = total_kind < 1.5
+        return [
+            jnp.where(low, entries[0][n], jnp.where(mixed, entries[1][n], entries[2][n])) for n in range(6)
+        ]
+
+    def ends(ref, where, slab, direction, tile):
+        return [
+            ref[where[0] + (dz,) + where[1] + (wrap(slab + dx),) + where[2] + (at(tile, dy),)]
+            for dx, dy, dz in BONDS[direction]
+        ]
+
+    def matter_ends(which, slab, direction, tile):
+        return ends(matter, ((which,), (), ()), slab, direction, tile)
+
+    for direction in range(9):
+        entries = block_entries(direction)
+
+        def fill(slab, _, direction=direction, entries=entries):
+            for tile in range(tiles):
+                first, second = matter_ends(0, slab, direction, tile)
+                spring_first, spring_second = matter_ends(1, slab, direction, tile)
+                bond = 0.5 * (spring_first + spring_second)
+                if BONDS[direction][1][2]:
+                    bond = jnp.where(inside, bond, 0.0)
+                for n, entry in enumerate(matrix(entries, first + second)):
+                    coef[slab, 6 * direction + n, at(tile)] = bond * entry
+            return 0
+
+        lax.fori_loop(0, ring, fill, 0)
+
+    def product(entry, vector):
+        return [
+            entry[ENTRY[a][0]] * vector[0] + entry[ENTRY[a][1]] * vector[1] + entry[ENTRY[a][2]] * vector[2]
+            for a in range(3)
+        ]
+
+    def bonds(level, slab, order):
+        beside = wrap(slab + 1)
+        for tile in order:
+            loaded = {}
+
+            def site(place):
+                if place not in loaded:
+                    dx, dy, dz = place
+                    loaded[place] = [
+                        fields[dz, level, beside if dx else slab, comp, at(tile, dy)] for comp in range(3)
+                    ]
+                return loaded[place]
+
+            def force(direction):
+                first, second = BONDS[direction]
+                entry = [coef[slab, 6 * direction + n, at(tile)] for n in range(6)]
+                return product(entry, [a - b for a, b in zip(site(first), site(second))])
+
+            here, up, deep, across, lift, dive = (None,) * 6
+
+            def add(total, values):
+                return values if total is None else [a + b for a, b in zip(total, values)]
+
+            def less(total, values):
+                return [-b for b in values] if total is None else [a - b for a, b in zip(total, values)]
+
+            f = force(0)
+            here, across = f, f
+            f = force(4)
+            across, up = [a - b for a, b in zip(across, f)], f
+            f = force(6)
+            across, deep = [a - b for a, b in zip(across, f)], f
+            f = force(1)
+            here, up = add(here, f), add(up, f)
+            f = force(2)
+            here, deep = add(here, f), add(deep, f)
+            f = force(8)
+            up, deep = [a - b for a, b in zip(up, f)], add(deep, f)
+            lift = force(3)
+            here = add(here, lift)
+            dive = force(5)
+            here = add(here, dive)
+            both = force(7)
+            here = add(here, both)
+            for comp in range(3):
+                sums[0, slab, comp, late(tile)] = here[comp]
+                sums[1, slab, comp, late(tile)] = up[comp]
+                sums[2, slab, comp, late(tile)] = deep[comp]
+                sums[3, slab, comp, late(tile)] = both[comp]
+                carry[0, beside, comp, late(tile)] = across[comp]
+                carry[1, beside, comp, late(tile)] = lift[comp]
+                carry[2, beside, comp, late(tile)] = dive[comp]
+                if tile == tiles - 1:
+                    sums[1, slab, comp, late(-1)] = up[comp]
+                    sums[3, slab, comp, late(-1)] = both[comp]
+                    carry[1, beside, comp, late(-1)] = lift[comp]
+
+    def update(level, slab, order, kick, kind):
+        mine = jnp.where(slab == me, 1, 0)
+        detect = depth_index >= ZCELLS // 2
+        for tile in order:
+            over = kick * inverse[slab, at(tile)]
+            for comp in range(3):
+                deep = sums[2, slab, comp, late(tile)] + carry[2, slab, comp, late(tile)]
+                deep = deep + sums[3, slab, comp, late(tile, -1)]
+                total = sums[0, slab, comp, late(tile)] - carry[0, slab, comp, late(tile)]
+                total = total - (sums[1, slab, comp, late(tile, -1)] + carry[1, slab, comp, late(tile, -1)])
+                change = (total - behind(deep)) * over
+                if kind != "dual":
+                    pushes[level, mine, comp, at(tile)] = change
+                moved = speed[slab, comp, at(tile)] + change
+                if kind == "middle":
+                    speed[slab, comp, at(tile)] = jnp.zeros_like(moved)
+                    fresh = jnp.where(detect, moved, 0.0)
+                else:
+                    speed[slab, comp, at(tile)] = moved
+                    fresh = fields[0, level, slab, comp, at(tile)] + moved
+                put_field(level + 1, slab, comp, tile, fresh)
+
+    def step(level, order, kind):
+        reach = LEVELS - 1 - level
+        count = jnp.minimum(ring, 2 * reach + 1)
+        low = wrap(me - jnp.minimum(reach, ring // 2) + ring)
+        more = jnp.where(count < ring, 1, 0)
+        kick = jnp.where((level == 0) | (level == STEPS) | (level == STEPS + 1), 0.5, 1.0)
+
+        def first(number, _):
+            bonds(level, wrap(low - more + number + ring), order)
+            return 0
+
+        def second(number, _):
+            update(level, wrap(low + number), order, kick, kind)
+            return 0
+
+        lax.fori_loop(0, count + more, first, 0)
+        lax.fori_loop(0, count, second, 0)
+
+    everything = list(range(tiles))
+    near = [tiles - 1] + list(range(own_tiles + 1))
+    wide = LEVELS - TILE
+
+    def run(start, stop, order, kind):
+        def one(level, _):
+            step(level, order, kind)
+            return 0
+
+        lax.fori_loop(start, stop, one, 0)
+
+    run(0, wide, everything, "state")
+    run(wide, STEPS, near, "state")
+    run(STEPS, STEPS + 1, near, "middle")
+    run(STEPS + 1, LEVELS - 1, near, "dual")
+
+    weights = [half_step if level in (0, STEPS) else time_step for level in range(STEPS + 1)]
+    for tile in range(own_tiles):
+        last = [fields[0, STEPS + 1, me, comp, at(tile)] for comp in range(3)]
+        bar = 0.5 * (last[0] * last[0] + last[1] * last[1] + last[2] * last[2])
+        for level in range(STEPS + 1):
+            for comp in range(3):
+                dual = fields[0, LEVELS - 1 - level, me, comp, at(tile)]
+                bar = bar - dual * pushes[level, 1, comp, at(tile)]
+        bar = bar * (1.0 / (time_step * time_step))
+        mass_grad[at(tile)] = bar * (1.0 + germanium_ratio * matter[0, 0, me, at(tile)])
+
+    entries_of = [block_entries(direction) for direction in range(9)]
+
+    def strain(slab, direction, tile):
+        first, second = matter_ends(0, slab, direction, tile)
+        entry = matrix(entries_of[direction], first + second)
+        result = None
+        for level in range(STEPS + 1):
+            parts = []
+            for where in (level, LEVELS - 1 - level):
+                pairs = [ends(fields, ((), (where,), (comp,)), slab, direction, tile) for comp in range(3)]
+                parts.append([a - b for a, b in pairs])
+            state, dual = parts
+            image = product(entry, dual)
+            term = state[0] * image[0] + state[1] * image[1] + state[2] * image[2]
+            term = weights[level] / time_step * term
+            result = term if result is None else result + term
+        if BONDS[direction][1][2]:
+            result = jnp.where(inside, result, 0.0)
+        return result
+
+    past = wrap(me + ring - 1)
+
+    def lifted(tile):
+        up = strain(me, 1, tile) + strain(me, 4, tile) + strain(me, 8, tile) + strain(past, 3, tile)
+        return up, strain(me, 7, tile)
+
+    def rays(tile, _):
+        second = strain(me, 1, tile)
+        both = strain(me, 7, tile)
+        third = strain(me, 2, tile)
+        here = strain(me, 0, tile) + second + third + strain(me, 3, tile) + strain(me, 5, tile) + both
+        here = here + strain(past, 0, tile) + strain(past, 4, tile) + strain(past, 6, tile)
+        eighth = strain(me, 8, tile)
+        ray[0, late(tile)] = here
+        ray[1, late(tile)] = second + strain(me, 4, tile) + eighth + strain(past, 3, tile)
+        ray[2, late(tile)] = third + strain(me, 6, tile) + eighth + strain(past, 5, tile)
+        ray[3, late(tile)] = both
+        return 0
+
+    lax.fori_loop(0, own_tiles, rays, 0)
+    ray[1, late(-1)], ray[3, late(-1)] = lifted(tiles - 1)
+    for tile in range(own_tiles):
+        deep = ray[2, late(tile)] + ray[3, late(tile, -1)]
+        spring_grad[at(tile)] = -0.5 * (ray[0, late(tile)] + ray[1, late(tile, -1)] + behind(deep))
+
+
+def gathered_body(displacement, velocity, species, mass_factor, spring, force_blocks, shell_table):
+    ring = lax.axis_size("gx")
+    half = spring.shape[1]
+    rows = 2 * half
+    own = jnp.concatenate(
+        [displacement[:, 0], velocity[:, 0], species.astype(jnp.float32), mass_factor, spring]
+    )
+
+    def swap_slabs(value, mask):
+        return lax.ppermute(value, "gx", [(i, i ^ mask) for i in range(ring)])
+
+    def swap_halves(value):
+        return lax.ppermute(value, "gy", [(0, 1), (1, 0)])
+
+    messages = {0: own, 1: swap_slabs(own, 1)}
+    for mask in range(2, ring, 2):
+        messages[mask] = swap_slabs(own, mask)
+        messages[mask + 1] = swap_slabs(messages[mask], 1)
+    operands = []
+    for mask in range(ring):
+        operands += [messages[mask], swap_halves(messages[mask])]
+
+    padded = rows + TILE
+    scratch = [
+        (2, LEVELS, ring, 3, padded, ZCELLS),
+        (ring, 3, rows, ZCELLS),
+        (STEPS + 1, 2, 3, rows, ZCELLS),
+        (2, 2, ring, padded, ZCELLS),
+        (ring, rows, ZCELLS),
+        (ring, 54, rows, ZCELLS),
+        (4, ring, 3, padded, ZCELLS),
+        (3, ring, 3, padded, ZCELLS),
+        (4, padded, ZCELLS),
+    ]
+    mass_grad, spring_grad = pl.pallas_call(
+        lambda *refs: kernel(ring, half, *refs),
+        out_shape=[jax.ShapeDtypeStruct((half, ZCELLS), jnp.float32)] * 2,
+        in_specs=[pl.BlockSpec(memory_space=pltpu.VMEM)] * (2 * ring)
+        + [pl.BlockSpec(memory_space=pltpu.SMEM)] * 2,
+        out_specs=[pl.BlockSpec(memory_space=pltpu.VMEM)] * 2,
+        scratch_shapes=[pltpu.VMEM(shape, jnp.float32) for shape in scratch],
+        compiler_params=pltpu.CompilerParams(vmem_limit_bytes=60 * 1024 * 1024),
+    )(*operands, force_blocks, shell_table)
+    return mass_grad[None], spring_grad[None]
 
 
 def padded_2(cells, sides, width):
@@ -119,7 +461,7 @@
     return padded_2(field, (("gx", 1), ("gy", 2)), 1)
 
 
-def body(displacement, velocity, species, mass_factor, spring, force_blocks, shell_table):
+def exchanged_body(displacement, velocity, species, mass_factor, spring, force_blocks, shell_table):
     blocks = pair_blocks(force_blocks, shell_table)
     species_float = species.astype(jnp.float32)
     species_mass = 1.0 + germanium_ratio * species_float
@@ -199,8 +541,9 @@
 
 
 def solution(mesh):
+    small = mesh.shape["gx"] == 8 and mesh.shape["gy"] == 2
     return jax.shard_map(
-        body,
+        gathered_body if small else exchanged_body,
         mesh=mesh,
         in_specs=(
             P(None, ("groups", "gx"), "gy", None),

time: 433 us -> 73.6 us (0.17)
  other arithmetic: 305 us -> 0.01 us
  starting transfers between devices: 71 us -> 14.3 us
  Pallas kernels: 0 us -> 40.3 us
  waiting for transfers between devices: 29.9 us -> 12.9 us
  local copies, waits for them, and re-layouts: 19.1 us -> 4.8 us
    another operation x251 -> x0, other arithmetic: 286 us -> none  [the longest x248 285 us: apply_coupling(): jnp.stack([matrix[first][0] * difference[0] + matrix[first][1] * differen...]
    ppermute x52 -> x15, starting transfers between devices: 71 us -> 14.3 us  [the longest x7 8.21 us: swap_slabs(): return lax.ppermute(value, 'gx', [(i, i ^ mask) for i in range(ring)])]
    pallas_call x0 -> x1, Pallas kernels: none -> 40.3 us  [gathered_body(): pl.pallas_call(lambda *refs: kernel(ring, half, *refs), out_shape=[jax.Sh...]
    slice x82 -> x0, local copies, waits for them, and re-layouts: 17.5 us -> none  [the longest x18 12.4 us: coupling(): kinds[0, first, second]]
    ppermute x52 -> x15, waiting for transfers between devices: 29.9 us -> 12.9 us  [the longest x7 12.7 us: swap_slabs(): return lax.ppermute(value, 'gx', [(i, i ^ mask) for i in range(ring)])]
    mul x4 -> x0, other arithmetic: 12 us -> none  [the longest x2 11.3 us: operator_terms(): total = total + 0.5 * (spring + other_spring) * image]
  transfers between devices with their start and end apart: 52 -> 15, of which waited for: 35 -> 5; matrix products, arithmetic and copies ran while one was open for 12% -> 1% of each run, Pallas kernels for 0% -> 0%
where the time goes in v2:
time: 73.6 us; the launch traced here: 73.1 us
  Pallas kernels  40.3 us (55%)
  starting transfers between devices  14.3 us (19%)
  waiting for transfers between devices  12.9 us (18%)
  local copies, waits for them, and re-layouts  4.8 us (7%)
  between operations  0.78 us (1%)
    pallas_call x1, Pallas kernels, gathered_body(): pl.pallas_call(lambda *refs: kernel(ring, half, *refs), out_shape=[jax.Sh...  40.3 us
    ppermute x7, waiting for transfers between devices, swap_slabs(): return lax.ppermute(value, 'gx', [(i, i ^ mask) for i in range(ring)])  12.7 us
    ppermute x7, starting transfers between devices, swap_slabs(): return lax.ppermute(value, 'gx', [(i, i ^ mask) for i in range(ring)])  8.21 us
    ppermute x8, starting transfers between devices, swap_halves(): return lax.ppermute(value, 'gy', [(0, 1), (1, 0)])  6.13 us
    unnamed x46, local copies, waits for them, and re-layouts  4.79 us
  transfers between devices with their start and end apart: 15, of which 5 were waited for; matrix products, arithmetic and copies ran while one was open for 1% of the time, Pallas kernels for 0%

profile of v2, /device:TPU:1, one launch (start us, length us, event | category | flops | bytes accessed | tf_op | source)
XLA Modules:
  0.0 73.1 jit_solution(6906917809713587404)
XLA Ops:
  0.6 0.8 %bitcast_dynamic-update-slice_fusion.1 = f32[9,32,128]{2,1,0:T(8,128)S(1)} fusion(f32[3,1,32,128]{3,2,1,0:T(8,128)} %param.7), kind=kLoop, calls=%fused_computation.1 | loop fusion | bytes 98304
  1.5 0.7 copy-done.17
  2.2 0.7 copy-done.18
  2.9 0.7 copy-done.19
  3.6 4.2 %collective-permute-start.11 = (f32[9,32,128]{2,1,0:T(8,128)S(1)}, f32[9,32,128]{2,1,0:T(8,128)S(1)}, u32[]{:S(2)}, u32[]{:S(2)}) collective-permute-start(f32[9,32,128]{2,1,0:T(8,128)S(1)} %constant_dynamic-update-slice_fusion.refs_0_), channel_id=1, source_target_pairs={{0,12},{2,14},{4,8},{6,10},{8,4},{10,6},{12,0},{14,2},{1,13},{3,15... | collective-permute-start | bytes 442376 | tf_op jit(solution)/shard_map/ppermute | solution.py:330
  7.8 0.0 collective-permute-start.7
  7.8 0.4 collective-permute-start.3
  8.1 1.2 %collective-permute-start.1 = (f32[9,32,128]{2,1,0:T(8,128)S(1)}, f32[9,32,128]{2,1,0:T(8,128)S(1)}, u32[]{:S(2)}, u32[]{:S(2)}) collective-permute-start(f32[9,32,128]{2,1,0:T(8,128)S(1)} %constant_dynamic-update-slice_fusion.refs_0_), channel_id=1, source_target_pairs={{0,2},{2,0},{4,6},{6,4},{8,10},{10,8},{12,14},{14,12},{1,3},{3,1},... | collective-permute-start | bytes 442376 | tf_op jit(solution)/shard_map/ppermute | solution.py:330
  9.3 1.7 %collective-permute-start = (f32[9,32,128]{2,1,0:T(8,128)S(1)}, f32[9,32,128]{2,1,0:T(8,128)S(1)}, u32[]{:S(2)}, u32[]{:S(2)}) collective-permute-start(f32[9,32,128]{2,1,0:T(8,128)S(1)} %constant_dynamic-update-slice_fusion.refs_0_), channel_id=1, source_target_pairs={{0,1},{1,0},{2,3},{3,2},{4,5},{5,4},{6,7},{7,6},{8,9},{9,8},{10,11... | collective-permute-start | bytes 442376 | tf_op jit(solution)/shard_map/ppermute | solution.py:333
  11.0 0.4 collective-permute-done.11.refs_12_
  11.4 1.0 %collective-permute-start.13 = (f32[9,32,128]{2,1,0:T(8,128)S(1)}, f32[9,32,128]{2,1,0:T(8,128)S(1)}, u32[]{:S(2)}, u32[]{:S(2)}) collective-permute-start(f32[9,32,128]{2,1,0:T(8,128)S(1)} %collective-permute-done.11.refs_12_), channel_id=1, source_target_pairs={{0,2},{2,0},{4,6},{6,4},{8,10},{10,8},{12,14},{14,12},{1,3},{3,1},... | collective-permute-start | bytes 442376 | tf_op jit(solution)/shard_map/ppermute | solution.py:330
  12.4 7.4 %collective-permute-done.7.refs_8_ = f32[9,32,128]{2,1,0:T(8,128)S(1)} collective-permute-done((f32[9,32,128]{2,1,0:T(8,128)S(1)}, f32[9,32,128]{2,1,0:T(8,128)S(1)}, u32[]{:S(2)}, u32[]{:S(2)}) %collective-permute-start.7) | collective-permute-done | bytes 147488 | tf_op jit(solution)/shard_map/ppermute | solution.py:330
  19.8 1.4 %collective-permute-start.12 = (f32[9,32,128]{2,1,0:T(8,128)S(1)}, f32[9,32,128]{2,1,0:T(8,128)S(1)}, u32[]{:S(2)}, u32[]{:S(2)}) collective-permute-start(f32[9,32,128]{2,1,0:T(8,128)S(1)} %collective-permute-done.11.refs_12_), channel_id=1, source_target_pairs={{0,1},{1,0},{2,3},{3,2},{4,5},{5,4},{6,7},{7,6},{8,9},{9,8},{10,11... | collective-permute-start | bytes 442376 | tf_op jit(solution)/shard_map/ppermute | solution.py:333
  21.2 1.2 %collective-permute-start.9 = (f32[9,32,128]{2,1,0:T(8,128)S(1)}, f32[9,32,128]{2,1,0:T(8,128)S(1)}, u32[]{:S(2)}, u32[]{:S(2)}) collective-permute-start(f32[9,32,128]{2,1,0:T(8,128)S(1)} %collective-permute-done.7.refs_8_), channel_id=1, source_target_pairs={{0,2},{2,0},{4,6},{6,4},{8,10},{10,8},{12,14},{14,12},{1,3},{3,1},... | collective-permute-start | bytes 442376 | tf_op jit(solution)/shard_map/ppermute | solution.py:330
  22.4 0.0 collective-permute-done.1.refs_2_
  22.4 0.3 collective-permute-start.8
  22.8 0.3 collective-permute-start.5
  23.1 0.4 collective-permute-start.4
  23.5 0.1 collective-permute-start.2
  23.6 3.0 %collective-permute-done.9.refs_10_ = f32[9,32,128]{2,1,0:T(8,128)S(1)} collective-permute-done((f32[9,32,128]{2,1,0:T(8,128)S(1)}, f32[9,32,128]{2,1,0:T(8,128)S(1)}, u32[]{:S(2)}, u32[]{:S(2)}) %collective-permute-start.9) | collective-permute-done | bytes 147488 | tf_op jit(solution)/shard_map/ppermute | solution.py:330
  26.6 1.3 %collective-permute-start.14 = (f32[9,32,128]{2,1,0:T(8,128)S(1)}, f32[9,32,128]{2,1,0:T(8,128)S(1)}, u32[]{:S(2)}, u32[]{:S(2)}) collective-permute-start(f32[9,32,128]{2,1,0:T(8,128)S(1)} %collective-permute-done.13.refs_14_), channel_id=1, source_target_pairs={{0,1},{1,0},{2,3},{3,2},{4,5},{5,4},{6,7},{7,6},{8,9},{9,8},{10,11... | collective-permute-start | bytes 442376 | tf_op jit(solution)/shard_map/ppermute | solution.py:333
  27.9 0.1 collective-permute-start.10
  28.0 1.8 %collective-permute-done.5.refs_6_ = f32[9,32,128]{2,1,0:T(8,128)S(1)} collective-permute-done((f32[9,32,128]{2,1,0:T(8,128)S(1)}, f32[9,32,128]{2,1,0:T(8,128)S(1)}, u32[]{:S(2)}, u32[]{:S(2)}) %collective-permute-start.5) | collective-permute-done | bytes 147488 | tf_op jit(solution)/shard_map/ppermute | solution.py:330
  29.8 0.8 %collective-permute-start.6 = (f32[9,32,128]{2,1,0:T(8,128)S(1)}, f32[9,32,128]{2,1,0:T(8,128)S(1)}, u32[]{:S(2)}, u32[]{:S(2)}) collective-permute-start(f32[9,32,128]{2,1,0:T(8,128)S(1)} %collective-permute-done.5.refs_6_), channel_id=1, source_target_pairs={{0,1},{1,0},{2,3},{3,2},{4,5},{5,4},{6,7},{7,6},{8,9},{9,8},{10,11... | collective-permute-start | bytes 442376 | tf_op jit(solution)/shard_map/ppermute | solution.py:333
  30.7 0.7 copy.9.refs_16_
  31.4 0.2 collective-permute-done.6.refs_7_
  31.7 0.3 copy-done.11
  32.0 0.1 copy-done.12
  32.1 0.1 copy-done.13
  32.1 0.0 copy-done.14
  32.2 0.7 copy-done.15
  32.8 40.3 %shard_map.86 = (f32[32,128]{1,0:T(8,128)}, f32[32,128]{1,0:T(8,128)}) custom-call(f32[9,32,128]{2,1,0:T(8,128)} %copy-done, f32[9,32,128]{2,1,0:T(8,128)} %copy-done.5, f32[9,32,128]{2,1,0:T(8,128)} %copy-done.4, f32[9,32,128]{2,1,0:T(8,128)} %copy-done.12, f32[9,32,128]{2,1,0:T(8,128)} %copy-done.3, f32[9,32,128]{2,1,0:T(8,128)} %copy-done.11, ...), custom_call_target="tpu_custom_call" | custom-call | tf_op jit(solution)/shard_map/pallas_call | solution.py:355
  (47 shorter events, 0.1 us)
Async XLA Ops:
  0.6 0.8 %copy-start.16 = (f32[3,1,32,128]{3,2,1,0:T(8,128)S(1)}, f32[3,1,32,128]{3,2,1,0:T(8,128)}, u32[]{:S(2)}) copy-start(f32[3,1,32,128]{3,2,1,0:T(8,128)} %param.8) | copy-start | bytes 147460
  1.5 0.7 copy-start.17
  3.6 27.0 %copy-start.20 = (f32[8,3,3]{0,2,1:T(4,128)S(1)}, f32[8,3,3]{0,2,1:T(4,128)}, u32[]{:S(2)}) copy-start(f32[8,3,3]{0,2,1:T(4,128)} %param.12) | copy-start | bytes 868
  3.6 28.0 %copy-start = (f32[9,32,128]{2,1,0:T(8,128)}, f32[9,32,128]{2,1,0:T(8,128)S(1)}, u32[]{:S(2)}) copy-start(f32[9,32,128]{2,1,0:T(8,128)S(1)} %constant_dynamic-update-slice_fusion.refs_0_) | copy-start | bytes 442372
  3.6 7.8 %collective-permute-start.11 = (f32[9,32,128]{2,1,0:T(8,128)S(1)}, f32[9,32,128]{2,1,0:T(8,128)S(1)}, u32[]{:S(2)}, u32[]{:S(2)}) collective-permute-start(f32[9,32,128]{2,1,0:T(8,128)S(1)} %constant_dynamic-update-slice_fusion.refs_0_), channel_id=1, source_target_pairs={{0,12},{2,14},{4,8},{6,10},{8,4},{10,6},{12,0},{14,2},{1,13},{3,15... | collective-permute-start | bytes 442376 | tf_op jit(solution)/shard_map/ppermute | solution.py:330
  7.8 12.1 %collective-permute-start.7 = (f32[9,32,128]{2,1,0:T(8,128)S(1)}, f32[9,32,128]{2,1,0:T(8,128)S(1)}, u32[]{:S(2)}, u32[]{:S(2)}) collective-permute-start(f32[9,32,128]{2,1,0:T(8,128)S(1)} %constant_dynamic-update-slice_fusion.refs_0_), channel_id=1, source_target_pairs={{0,8},{2,10},{4,12},{6,14},{8,0},{10,2},{12,4},{14,6},{1,9},{3,11}... | collective-permute-start | bytes 442376 | tf_op jit(solution)/shard_map/ppermute | solution.py:330
  7.8 13.4 %collective-permute-start.3 = (f32[9,32,128]{2,1,0:T(8,128)S(1)}, f32[9,32,128]{2,1,0:T(8,128)S(1)}, u32[]{:S(2)}, u32[]{:S(2)}) collective-permute-start(f32[9,32,128]{2,1,0:T(8,128)S(1)} %constant_dynamic-update-slice_fusion.refs_0_), channel_id=1, source_target_pairs={{0,4},{2,6},{4,0},{6,2},{8,12},{10,14},{12,8},{14,10},{1,5},{3,7},... | collective-permute-start | bytes 442376 | tf_op jit(solution)/shard_map/ppermute | solution.py:330
  8.1 14.3 %collective-permute-start.1 = (f32[9,32,128]{2,1,0:T(8,128)S(1)}, f32[9,32,128]{2,1,0:T(8,128)S(1)}, u32[]{:S(2)}, u32[]{:S(2)}) collective-permute-start(f32[9,32,128]{2,1,0:T(8,128)S(1)} %constant_dynamic-update-slice_fusion.refs_0_), channel_id=1, source_target_pairs={{0,2},{2,0},{4,6},{6,4},{8,10},{10,8},{12,14},{14,12},{1,3},{3,1},... | collective-permute-start | bytes 442376 | tf_op jit(solution)/shard_map/ppermute | solution.py:330
  9.3 13.5 %collective-permute-start = (f32[9,32,128]{2,1,0:T(8,128)S(1)}, f32[9,32,128]{2,1,0:T(8,128)S(1)}, u32[]{:S(2)}, u32[]{:S(2)}) collective-permute-start(f32[9,32,128]{2,1,0:T(8,128)S(1)} %constant_dynamic-update-slice_fusion.refs_0_), channel_id=1, source_target_pairs={{0,1},{1,0},{2,3},{3,2},{4,5},{5,4},{6,7},{7,6},{8,9},{9,8},{10,11... | collective-permute-start | bytes 442376 | tf_op jit(solution)/shard_map/ppermute | solution.py:333
  11.4 20.3 %copy-start.1 = (f32[9,32,128]{2,1,0:T(8,128)}, f32[9,32,128]{2,1,0:T(8,128)S(1)}, u32[]{:S(2)}) copy-start(f32[9,32,128]{2,1,0:T(8,128)S(1)} %collective-permute-done.11.refs_12_) | copy-start | bytes 442372
  11.4 11.7 %collective-permute-start.13 = (f32[9,32,128]{2,1,0:T(8,128)S(1)}, f32[9,32,128]{2,1,0:T(8,128)S(1)}, u32[]{:S(2)}, u32[]{:S(2)}) collective-permute-start(f32[9,32,128]{2,1,0:T(8,128)S(1)} %collective-permute-done.11.refs_12_), channel_id=1, source_target_pairs={{0,2},{2,0},{4,6},{6,4},{8,10},{10,8},{12,14},{14,12},{1,3},{3,1},... | collective-permute-start | bytes 442376 | tf_op jit(solution)/shard_map/ppermute | solution.py:330
  19.8 11.8 %copy-start.2 = (f32[9,32,128]{2,1,0:T(8,128)}, f32[9,32,128]{2,1,0:T(8,128)S(1)}, u32[]{:S(2)}) copy-start(f32[9,32,128]{2,1,0:T(8,128)S(1)} %collective-permute-done.7.refs_8_) | copy-start | bytes 442372
  19.8 3.7 %collective-permute-start.12 = (f32[9,32,128]{2,1,0:T(8,128)S(1)}, f32[9,32,128]{2,1,0:T(8,128)S(1)}, u32[]{:S(2)}, u32[]{:S(2)}) collective-permute-start(f32[9,32,128]{2,1,0:T(8,128)S(1)} %collective-permute-done.11.refs_12_), channel_id=1, source_target_pairs={{0,1},{1,0},{2,3},{3,2},{4,5},{5,4},{6,7},{7,6},{8,9},{9,8},{10,11... | collective-permute-start | bytes 442376 | tf_op jit(solution)/shard_map/ppermute | solution.py:333
  21.2 10.5 %copy-start.3 = (f32[9,32,128]{2,1,0:T(8,128)}, f32[9,32,128]{2,1,0:T(8,128)S(1)}, u32[]{:S(2)}) copy-start(f32[9,32,128]{2,1,0:T(8,128)S(1)} %collective-permute-done.3.refs_4_) | copy-start | bytes 442372
  21.2 5.4 %collective-permute-start.9 = (f32[9,32,128]{2,1,0:T(8,128)S(1)}, f32[9,32,128]{2,1,0:T(8,128)S(1)}, u32[]{:S(2)}, u32[]{:S(2)}) collective-permute-start(f32[9,32,128]{2,1,0:T(8,128)S(1)} %collective-permute-done.7.refs_8_), channel_id=1, source_target_pairs={{0,2},{2,0},{4,6},{6,4},{8,10},{10,8},{12,14},{14,12},{1,3},{3,1},... | collective-permute-start | bytes 442376 | tf_op jit(solution)/shard_map/ppermute | solution.py:330
  22.4 9.2 %copy-start.4 = (f32[9,32,128]{2,1,0:T(8,128)}, f32[9,32,128]{2,1,0:T(8,128)S(1)}, u32[]{:S(2)}) copy-start(f32[9,32,128]{2,1,0:T(8,128)S(1)} %collective-permute-done.1.refs_2_) | copy-start | bytes 442372
  22.4 5.5 %collective-permute-start.8 = (f32[9,32,128]{2,1,0:T(8,128)S(1)}, f32[9,32,128]{2,1,0:T(8,128)S(1)}, u32[]{:S(2)}, u32[]{:S(2)}) collective-permute-start(f32[9,32,128]{2,1,0:T(8,128)S(1)} %collective-permute-done.7.refs_8_), channel_id=1, source_target_pairs={{0,1},{1,0},{2,3},{3,2},{4,5},{5,4},{6,7},{7,6},{8,9},{9,8},{10,11... | collective-permute-start | bytes 442376 | tf_op jit(solution)/shard_map/ppermute | solution.py:333
  22.8 8.9 %copy-start.5 = (f32[9,32,128]{2,1,0:T(8,128)}, f32[9,32,128]{2,1,0:T(8,128)S(1)}, u32[]{:S(2)}) copy-start(f32[9,32,128]{2,1,0:T(8,128)S(1)} %collective-permute-done.refs_1_) | copy-start | bytes 442372
  22.8 7.0 %collective-permute-start.5 = (f32[9,32,128]{2,1,0:T(8,128)S(1)}, f32[9,32,128]{2,1,0:T(8,128)S(1)}, u32[]{:S(2)}, u32[]{:S(2)}) collective-permute-start(f32[9,32,128]{2,1,0:T(8,128)S(1)} %collective-permute-done.3.refs_4_), channel_id=1, source_target_pairs={{0,2},{2,0},{4,6},{6,4},{8,10},{10,8},{12,14},{14,12},{1,3},{3,1},... | collective-permute-start | bytes 442376 | tf_op jit(solution)/shard_map/ppermute | solution.py:330
  23.1 8.6 %copy-start.6 = (f32[9,32,128]{2,1,0:T(8,128)}, f32[9,32,128]{2,1,0:T(8,128)S(1)}, u32[]{:S(2)}) copy-start(f32[9,32,128]{2,1,0:T(8,128)S(1)} %collective-permute-done.13.refs_14_) | copy-start | bytes 442372
  23.1 8.3 %collective-permute-start.4 = (f32[9,32,128]{2,1,0:T(8,128)S(1)}, f32[9,32,128]{2,1,0:T(8,128)S(1)}, u32[]{:S(2)}, u32[]{:S(2)}) collective-permute-start(f32[9,32,128]{2,1,0:T(8,128)S(1)} %collective-permute-done.3.refs_4_), channel_id=1, source_target_pairs={{0,1},{1,0},{2,3},{3,2},{4,5},{5,4},{6,7},{7,6},{8,9},{9,8},{10,11... | collective-permute-start | bytes 442376 | tf_op jit(solution)/shard_map/ppermute | solution.py:333
  23.5 8.2 %copy-start.7 = (f32[9,32,128]{2,1,0:T(8,128)}, f32[9,32,128]{2,1,0:T(8,128)S(1)}, u32[]{:S(2)}) copy-start(f32[9,32,128]{2,1,0:T(8,128)S(1)} %collective-permute-done.12.refs_13_) | copy-start | bytes 442372
  23.5 7.8 %collective-permute-start.2 = (f32[9,32,128]{2,1,0:T(8,128)S(1)}, f32[9,32,128]{2,1,0:T(8,128)S(1)}, u32[]{:S(2)}, u32[]{:S(2)}) collective-permute-start(f32[9,32,128]{2,1,0:T(8,128)S(1)} %collective-permute-done.1.refs_2_), channel_id=1, source_target_pairs={{0,1},{1,0},{2,3},{3,2},{4,5},{5,4},{6,7},{7,6},{8,9},{9,8},{10,11... | collective-permute-start | bytes 442376 | tf_op jit(solution)/shard_map/ppermute | solution.py:333
  26.6 5.1 %copy-start.8 = (f32[9,32,128]{2,1,0:T(8,128)}, f32[9,32,128]{2,1,0:T(8,128)S(1)}, u32[]{:S(2)}) copy-start(f32[9,32,128]{2,1,0:T(8,128)S(1)} %collective-permute-done.9.refs_10_) | copy-start | bytes 442372
  26.6 4.7 %collective-permute-start.14 = (f32[9,32,128]{2,1,0:T(8,128)S(1)}, f32[9,32,128]{2,1,0:T(8,128)S(1)}, u32[]{:S(2)}, u32[]{:S(2)}) collective-permute-start(f32[9,32,128]{2,1,0:T(8,128)S(1)} %collective-permute-done.13.refs_14_), channel_id=1, source_target_pairs={{0,1},{1,0},{2,3},{3,2},{4,5},{5,4},{6,7},{7,6},{8,9},{9,8},{10,11... | collective-permute-start | bytes 442376 | tf_op jit(solution)/shard_map/ppermute | solution.py:333
  27.9 3.8 %copy-start.9 = (f32[9,32,128]{2,1,0:T(8,128)}, f32[9,32,128]{2,1,0:T(8,128)S(1)}, u32[]{:S(2)}) copy-start(f32[9,32,128]{2,1,0:T(8,128)S(1)} %collective-permute-done.8.refs_9_) | copy-start | bytes 442372
  27.9 3.4 %collective-permute-start.10 = (f32[9,32,128]{2,1,0:T(8,128)S(1)}, f32[9,32,128]{2,1,0:T(8,128)S(1)}, u32[]{:S(2)}, u32[]{:S(2)}) collective-permute-start(f32[9,32,128]{2,1,0:T(8,128)S(1)} %collective-permute-done.9.refs_10_), channel_id=1, source_target_pairs={{0,1},{1,0},{2,3},{3,2},{4,5},{5,4},{6,7},{7,6},{8,9},{9,8},{10,11... | collective-permute-start | bytes 442376 | tf_op jit(solution)/shard_map/ppermute | solution.py:333
  29.8 1.9 %copy-start.10 = (f32[9,32,128]{2,1,0:T(8,128)}, f32[9,32,128]{2,1,0:T(8,128)S(1)}, u32[]{:S(2)}) copy-start(f32[9,32,128]{2,1,0:T(8,128)S(1)} %collective-permute-done.5.refs_6_) | copy-start | bytes 442372
  29.8 1.9 %collective-permute-start.6 = (f32[9,32,128]{2,1,0:T(8,128)S(1)}, f32[9,32,128]{2,1,0:T(8,128)S(1)}, u32[]{:S(2)}, u32[]{:S(2)}) collective-permute-start(f32[9,32,128]{2,1,0:T(8,128)S(1)} %collective-permute-done.5.refs_6_), channel_id=1, source_target_pairs={{0,1},{1,0},{2,3},{3,2},{4,5},{5,4},{6,7},{7,6},{8,9},{9,8},{10,11... | collective-permute-start | bytes 442376 | tf_op jit(solution)/shard_map/ppermute | solution.py:333
  31.4 0.7 copy-start.12
  31.4 0.8 %copy-start.13 = (f32[9,32,128]{2,1,0:T(8,128)}, f32[9,32,128]{2,1,0:T(8,128)S(1)}, u32[]{:S(2)}) copy-start(f32[9,32,128]{2,1,0:T(8,128)S(1)} %collective-permute-done.14.refs_15_) | copy-start | bytes 442372
  31.4 0.8 %copy-start.14 = (f32[9,32,128]{2,1,0:T(8,128)}, f32[9,32,128]{2,1,0:T(8,128)S(1)}, u32[]{:S(2)}) copy-start(f32[9,32,128]{2,1,0:T(8,128)S(1)} %collective-permute-done.10.refs_11_) | copy-start | bytes 442372
  (4 other events, 2.8 us)

commit v3 on v2

--- a/solution.py
+++ b/solution.py
@@ -44,7 +44,8 @@
     blocks_in = refs[: 2 * ring]
     force_ref, table_ref, mass_grad, spring_grad = refs[2 * ring : 2 * ring + 4]
     (
-        fields,
+        even_fields,
+        odd_fields,
         speed,
         pushes,
         matter,
@@ -75,13 +76,13 @@
     def late(tile, shift=0):
         return pl.ds(TILE + TILE * tile + shift, TILE)
 
-    def put_field(level, slab, comp, tile, value):
+    fields = (even_fields, odd_fields)
+
+    def put_field(odd, number, slab, comp, tile, value):
         deeper = ahead(value)
-        fields[0, level, slab, comp, at(tile)] = value
-        fields[1, level, slab, comp, at(tile)] = deeper
-        if tile == 0:
-            fields[0, level, slab, comp, at(tiles)] = value
-            fields[1, level, slab, comp, at(tiles)] = deeper
+        for place in (tile,) if tile else (0, tiles):
+            fields[odd][0, number, slab, comp, at(place)] = value
+            fields[odd][1, number, slab, comp, at(place)] = deeper
 
     for message in range(ring):
         slab = lax.bitwise_xor(me, message)
@@ -90,8 +91,10 @@
             for tile in range(own_tiles):
                 target = side * own_tiles + tile
                 for comp in range(3):
-                    put_field(0, slab, comp, target, source[comp, at(tile)])
-                    speed[slab, comp, at(target)] = time_step * source[3 + comp, at(tile)]
+                    put_field(0, 0, slab, comp, target, source[comp, at(tile)])
+                    rate = time_step * source[3 + comp, at(tile)]
+                    speed[0, slab, comp, at(target)] = rate
+                    speed[1, slab, comp, at(target)] = ahead(rate)
                 sort = source[6, at(tile)]
                 for which, value in ((0, sort), (1, source[8, at(tile)])):
                     deeper = ahead(value)
@@ -99,7 +102,9 @@
                         matter[which, 0, slab, at(place)] = value
                         matter[which, 1, slab, at(place)] = deeper
                 mass = (1.0 + germanium_ratio * sort) * source[7, at(tile)]
-                inverse[slab, at(target)] = (-time_step * time_step) / mass
+                over_mass = (-time_step * time_step) / mass
+                inverse[0, slab, at(target)] = over_mass
+                inverse[1, slab, at(target)] = ahead(over_mass)
 
     def block_entries(direction):
         result = []
@@ -129,8 +134,8 @@
     for direction in range(9):
         entries = block_entries(direction)
 
-        def fill(slab, _, direction=direction, entries=entries):
-            for tile in range(tiles):
+        def fill(pair, _, direction=direction, entries=entries):
+            for slab, tile in [(2 * pair + which, tile) for which in range(2) for tile in range(tiles)]:
                 first, second = matter_ends(0, slab, direction, tile)
                 spring_first, spring_second = matter_ends(1, slab, direction, tile)
                 bond = 0.5 * (spring_first + spring_second)
@@ -140,7 +145,7 @@
                     coef[slab, 6 * direction + n, at(tile)] = bond * entry
             return 0
 
-        lax.fori_loop(0, ring, fill, 0)
+        lax.fori_loop(0, ring // 2, fill, 0)
 
     def product(entry, vector):
         return [
@@ -148,7 +153,7 @@
             for a in range(3)
         ]
 
-    def bonds(level, slab, order):
+    def bonds(odd, number, slab, order):
         beside = wrap(slab + 1)
         for tile in order:
             loaded = {}
@@ -157,7 +162,7 @@
                 if place not in loaded:
                     dx, dy, dz = place
                     loaded[place] = [
-                        fields[dz, level, beside if dx else slab, comp, at(tile, dy)] for comp in range(3)
+                        fields[odd][dz, number, beside if dx else slab, comp, at(tile, dy)] for comp in range(3)
                     ]
                 return loaded[place]
 
@@ -205,56 +210,73 @@
                     sums[3, slab, comp, late(-1)] = both[comp]
                     carry[1, beside, comp, late(-1)] = lift[comp]
 
-    def update(level, slab, order, kick, kind):
+    def update(odd, number, slab, order, kick, kind):
         mine = jnp.where(slab == me, 1, 0)
         detect = depth_index >= ZCELLS // 2
+        detect = (detect, (depth_index >= ZCELLS // 2 - 1) & inside)
         for tile in order:
-            over = kick * inverse[slab, at(tile)]
+            over = [kick * inverse[frame, slab, at(tile)] for frame in range(2)]
             for comp in range(3):
                 deep = sums[2, slab, comp, late(tile)] + carry[2, slab, comp, late(tile)]
                 deep = deep + sums[3, slab, comp, late(tile, -1)]
                 total = sums[0, slab, comp, late(tile)] - carry[0, slab, comp, late(tile)]
                 total = total - (sums[1, slab, comp, late(tile, -1)] + carry[1, slab, comp, late(tile, -1)])
-                change = (total - behind(deep)) * over
-                if kind != "dual":
-                    pushes[level, mine, comp, at(tile)] = change
-                moved = speed[slab, comp, at(tile)] + change
-                if kind == "middle":
-                    speed[slab, comp, at(tile)] = jnp.zeros_like(moved)
-                    fresh = jnp.where(detect, moved, 0.0)
-                else:
-                    speed[slab, comp, at(tile)] = moved
-                    fresh = fields[0, level, slab, comp, at(tile)] + moved
-                put_field(level + 1, slab, comp, tile, fresh)
-
-    def step(level, order, kind):
+                for frame, force in enumerate((total - behind(deep), ahead(total) - deep)):
+                    change = force * over[frame]
+                    if kind != "dual" and frame == 0:
+                        pushes[2 * number + odd, mine, comp, at(tile)] = change
+                    moved = speed[frame, slab, comp, at(tile)] + change
+                    if kind == "middle":
+                        speed[frame, slab, comp, at(tile)] = jnp.zeros_like(moved)
+                        fresh = jnp.where(detect[frame], moved, 0.0)
+                    else:
+                        speed[frame, slab, comp, at(tile)] = moved
+                        fresh = fields[odd][frame, number, slab, comp, at(tile)] + moved
+                    for place in (tile,) if tile else (0, tiles):
+                        fields[1 - odd][frame, number + odd, slab, comp, at(place)] = fresh
+
+    def step(odd, number, order, kind):
+        level = 2 * number + odd
         reach = LEVELS - 1 - level
-        count = jnp.minimum(ring, 2 * reach + 1)
-        low = wrap(me - jnp.minimum(reach, ring // 2) + ring)
-        more = jnp.where(count < ring, 1, 0)
+        count = jnp.minimum(ring, 2 * reach + 2)
+        low = wrap(me - jnp.minimum(reach + 1, ring // 2) + ring)
         kick = jnp.where((level == 0) | (level == STEPS) | (level == STEPS + 1), 0.5, 1.0)
 
-        def first(number, _):
-            bonds(level, wrap(low - more + number + ring), order)
+        def start(place, _):
+            bonds(odd, number, wrap(low + place), order)
             return 0
 
-        def second(number, _):
-            update(level, wrap(low + number), order, kick, kind)
+        def both(place, _):
+            for tile in order:
+                update(odd, number, wrap(low + place + 1), [tile], kick, kind)
+                bonds(odd, number, wrap(low + place + 2), [tile])
             return 0
 
-        lax.fori_loop(0, count + more, first, 0)
-        lax.fori_loop(0, count, second, 0)
+        lax.fori_loop(0, 2, start, 0)
+        lax.fori_loop(0, count - 2, both, 0)
+        update(odd, number, wrap(low + count - 1), order, kick, kind)
+        update(odd, number, low, order, kick, kind)
 
     everything = list(range(tiles))
     near = [tiles - 1] + list(range(own_tiles + 1))
     wide = LEVELS - TILE
 
     def run(start, stop, order, kind):
-        def one(level, _):
-            step(level, order, kind)
+        level = start
+        if level % 2:
+            step(1, level // 2, order, kind)
+            level += 1
+        pairs = (stop - level) // 2
+
+        def two(number, _):
+            step(0, number, order, kind)
+            step(1, number, order, kind)
             return 0
 
-        lax.fori_loop(start, stop, one, 0)
+        if pairs:
+            lax.fori_loop(level // 2, level // 2 + pairs, two, 0)
+        if (stop - level) % 2:
+            step(0, stop // 2, order, kind)
 
     run(0, wide, everything, "state")
     run(wide, STEPS, near, "state")
@@ -263,11 +285,11 @@
 
     weights = [half_step if level in (0, STEPS) else time_step for level in range(STEPS + 1)]
     for tile in range(own_tiles):
-        last = [fields[0, STEPS + 1, me, comp, at(tile)] for comp in range(3)]
+        last = [fields[(STEPS + 1) % 2][0, (STEPS + 1) // 2, me, comp, at(tile)] for comp in range(3)]
         bar = 0.5 * (last[0] * last[0] + last[1] * last[1] + last[2] * last[2])
         for level in range(STEPS + 1):
             for comp in range(3):
-                dual = fields[0, LEVELS - 1 - level, me, comp, at(tile)]
+                dual = fields[(LEVELS - 1 - level) % 2][0, (LEVELS - 1 - level) // 2, me, comp, at(tile)]
                 bar = bar - dual * pushes[level, 1, comp, at(tile)]
         bar = bar * (1.0 / (time_step * time_step))
         mass_grad[at(tile)] = bar * (1.0 + germanium_ratio * matter[0, 0, me, at(tile)])
@@ -281,7 +303,10 @@
         for level in range(STEPS + 1):
             parts = []
             for where in (level, LEVELS - 1 - level):
-                pairs = [ends(fields, ((), (where,), (comp,)), slab, direction, tile) for comp in range(3)]
+                pairs = [
+                    ends(fields[where % 2], ((), (where // 2,), (comp,)), slab, direction, tile)
+                    for comp in range(3)
+                ]
                 parts.append([a - b for a, b in pairs])
             state, dual = parts
             image = product(entry, dual)
@@ -318,13 +343,25 @@
         spring_grad[at(tile)] = -0.5 * (ray[0, late(tile)] + ray[1, late(tile, -1)] + behind(deep))
 
 
+def pack(displacement, velocity, species, mass_factor, spring, packed):
+    for comp in range(3):
+        packed[comp] = displacement[comp, 0]
+        packed[3 + comp] = velocity[comp, 0]
+    packed[6] = species[0].astype(jnp.float32)
+    packed[7] = mass_factor[0]
+    packed[8] = spring[0]
+
+
 def gathered_body(displacement, velocity, species, mass_factor, spring, force_blocks, shell_table):
     ring = lax.axis_size("gx")
     half = spring.shape[1]
     rows = 2 * half
-    own = jnp.concatenate(
-        [displacement[:, 0], velocity[:, 0], species.astype(jnp.float32), mass_factor, spring]
-    )
+    own = pl.pallas_call(
+        pack,
+        out_shape=jax.ShapeDtypeStruct((FIELDS, half, ZCELLS), jnp.float32),
+        in_specs=[pl.BlockSpec(memory_space=pltpu.VMEM)] * 5,
+        out_specs=pl.BlockSpec(memory_space=pltpu.VMEM),
+    )(displacement, velocity, species, mass_factor, spring)
 
     def swap_slabs(value, mask):
         return lax.ppermute(value, "gx", [(i, i ^ mask) for i in range(ring)])
@@ -342,11 +379,12 @@
 
     padded = rows + TILE
     scratch = [
-        (2, LEVELS, ring, 3, padded, ZCELLS),
-        (ring, 3, rows, ZCELLS),
+        (2, LEVELS // 2, ring, 3, padded, ZCELLS),
+        (2, LEVELS // 2, ring, 3, padded, ZCELLS),
+        (2, ring, 3, rows, ZCELLS),
         (STEPS + 1, 2, 3, rows, ZCELLS),
         (2, 2, ring, padded, ZCELLS),
-        (ring, rows, ZCELLS),
+        (2, ring, rows, ZCELLS),
         (ring, 54, rows, ZCELLS),
         (4, ring, 3, padded, ZCELLS),
         (3, ring, 3, padded, ZCELLS),

time: 73.6 us -> 64.1 us (0.87)
  Pallas kernels: 40.3 us -> 33.8 us
  local copies, waits for them, and re-layouts: 4.8 us -> 1.85 us
    pallas_call x1, Pallas kernels: 40.3 us -> 32.3 us  [gathered_body(): pl.pallas_call(lambda *refs: kernel(ring, half, *refs), out_shape=[jax.Sh...]
    unnamed x46 -> x33, local copies, waits for them, and re-layouts: 4.79 us -> 1.85 us
    pallas_call x0 -> x1, Pallas kernels: none -> 1.53 us  [gathered_body(): pl.pallas_call(pack, out_shape=jax.ShapeDtypeStruct((FIELDS, half, ZCELLS...]
where the time goes in v3:
time: 64.1 us; the launch traced here: 63.9 us
  Pallas kernels  33.8 us (53%)
  starting transfers between devices  14.3 us (22%)
  waiting for transfers between devices  13.1 us (20%)
  local copies, waits for them, and re-layouts  1.85 us (3%)
  between operations  0.76 us (1%)
    pallas_call x1, Pallas kernels, gathered_body(): pl.pallas_call(lambda *refs: kernel(ring, half, *refs), out_shape=[jax.Sh...  32.3 us
    ppermute x7, waiting for transfers between devices, swap_slabs(): return lax.ppermute(value, 'gx', [(i, i ^ mask) for i in range(ring)])  12.9 us
    ppermute x7, starting transfers between devices, swap_slabs(): return lax.ppermute(value, 'gx', [(i, i ^ mask) for i in range(ring)])  8.14 us
    ppermute x8, starting transfers between devices, swap_halves(): return lax.ppermute(value, 'gy', [(0, 1), (1, 0)])  6.2 us
    unnamed x33, local copies, waits for them, and re-layouts  1.85 us
    pallas_call x1, Pallas kernels, gathered_body(): pl.pallas_call(pack, out_shape=jax.ShapeDtypeStruct((FIELDS, half, ZCELLS...  1.53 us
  transfers between devices with their start and end apart: 15, of which 5 were waited for; matrix products, arithmetic and copies ran while one was open for 1% of the time, Pallas kernels for 0%

profile of v3, /device:TPU:1, one launch (start us, length us, event | category | flops | bytes accessed | tf_op | source)
XLA Modules:
  0.0 63.9 jit_solution(14488356406795545853)
XLA Ops:
  0.6 1.5 %shard_map.86.refs_0_ = f32[9,32,128]{2,1,0:T(8,128)} custom-call(f32[3,1,32,128]{3,2,1,0:T(8,128)} %displacement.1, f32[3,1,32,128]{3,2,1,0:T(8,128)} %velocity.1, s32[1,32,128]{2,1,0:T(8,128)} %species.1, f32[1,32,128]{2,1,0:T(8,128)} %mass_factor.1, f32[1,32,128]{2,1,0:T(8,128)} %spring.1), custom_call_target="tpu_custom_call" | custom-call | tf_op jit(solution)/shard_map/pallas_call | solution.py:359
  2.2 4.2 %collective-permute-start.11 = (f32[9,32,128]{2,1,0:T(8,128)}, f32[9,32,128]{2,1,0:T(8,128)S(1)}, u32[]{:S(2)}, u32[]{:S(2)}) collective-permute-start(f32[9,32,128]{2,1,0:T(8,128)} %shard_map.86.refs_0_), channel_id=1, source_target_pairs={{0,12},{2,14},{4,8},{6,10},{8,4},{10,6},{12,0},{14,2},{1,13},{3,15... | collective-permute-start | bytes 442376 | tf_op jit(solution)/shard_map/ppermute | solution.py:367
  6.3 0.0 collective-permute-start.7
  6.3 0.3 collective-permute-start.3
  6.6 1.2 %collective-permute-start.1 = (f32[9,32,128]{2,1,0:T(8,128)}, f32[9,32,128]{2,1,0:T(8,128)S(1)}, u32[]{:S(2)}, u32[]{:S(2)}) collective-permute-start(f32[9,32,128]{2,1,0:T(8,128)} %shard_map.86.refs_0_), channel_id=1, source_target_pairs={{0,2},{2,0},{4,6},{6,4},{8,10},{10,8},{12,14},{14,12},{1,3},{3,1},... | collective-permute-start | bytes 442376 | tf_op jit(solution)/shard_map/ppermute | solution.py:367
  7.8 1.7 %collective-permute-start = (f32[9,32,128]{2,1,0:T(8,128)}, f32[9,32,128]{2,1,0:T(8,128)S(1)}, u32[]{:S(2)}, u32[]{:S(2)}) collective-permute-start(f32[9,32,128]{2,1,0:T(8,128)} %shard_map.86.refs_0_), channel_id=1, source_target_pairs={{0,1},{1,0},{2,3},{3,2},{4,5},{5,4},{6,7},{7,6},{8,9},{9,8},{10,11... | collective-permute-start | bytes 442376 | tf_op jit(solution)/shard_map/ppermute | solution.py:370
  9.6 0.6 collective-permute-done.11.refs_12_
  10.2 1.0 %collective-permute-start.13 = (f32[9,32,128]{2,1,0:T(8,128)S(1)}, f32[9,32,128]{2,1,0:T(8,128)S(1)}, u32[]{:S(2)}, u32[]{:S(2)}) collective-permute-start(f32[9,32,128]{2,1,0:T(8,128)S(1)} %collective-permute-done.11.refs_12_), channel_id=1, source_target_pairs={{0,2},{2,0},{4,6},{6,4},{8,10},{10,8},{12,14},{14,12},{1,3},{3,1},... | collective-permute-start | bytes 442376 | tf_op jit(solution)/shard_map/ppermute | solution.py:367
  11.2 7.4 %collective-permute-done.7.refs_8_ = f32[9,32,128]{2,1,0:T(8,128)S(1)} collective-permute-done((f32[9,32,128]{2,1,0:T(8,128)}, f32[9,32,128]{2,1,0:T(8,128)S(1)}, u32[]{:S(2)}, u32[]{:S(2)}) %collective-permute-start.7) | collective-permute-done | bytes 147488 | tf_op jit(solution)/shard_map/ppermute | solution.py:367
  18.6 1.4 %collective-permute-start.12 = (f32[9,32,128]{2,1,0:T(8,128)S(1)}, f32[9,32,128]{2,1,0:T(8,128)S(1)}, u32[]{:S(2)}, u32[]{:S(2)}) collective-permute-start(f32[9,32,128]{2,1,0:T(8,128)S(1)} %collective-permute-done.11.refs_12_), channel_id=1, source_target_pairs={{0,1},{1,0},{2,3},{3,2},{4,5},{5,4},{6,7},{7,6},{8,9},{9,8},{10,11... | collective-permute-start | bytes 442376 | tf_op jit(solution)/shard_map/ppermute | solution.py:370
  20.0 0.0 collective-permute-done.3.refs_4_
  20.0 1.2 %collective-permute-start.9 = (f32[9,32,128]{2,1,0:T(8,128)S(1)}, f32[9,32,128]{2,1,0:T(8,128)S(1)}, u32[]{:S(2)}, u32[]{:S(2)}) collective-permute-start(f32[9,32,128]{2,1,0:T(8,128)S(1)} %collective-permute-done.7.refs_8_), channel_id=1, source_target_pairs={{0,2},{2,0},{4,6},{6,4},{8,10},{10,8},{12,14},{14,12},{1,3},{3,1},... | collective-permute-start | bytes 442376 | tf_op jit(solution)/shard_map/ppermute | solution.py:367
  21.2 0.0 collective-permute-done.1.refs_2_
  21.2 0.3 collective-permute-start.8
  21.6 0.3 collective-permute-start.5
  21.8 0.4 collective-permute-start.4
  22.3 0.0 collective-permute-done.12.refs_13_
  22.3 0.1 collective-permute-start.2
  22.4 3.0 %collective-permute-done.9.refs_10_ = f32[9,32,128]{2,1,0:T(8,128)S(1)} collective-permute-done((f32[9,32,128]{2,1,0:T(8,128)S(1)}, f32[9,32,128]{2,1,0:T(8,128)S(1)}, u32[]{:S(2)}, u32[]{:S(2)}) %collective-permute-start.9) | collective-permute-done | bytes 147488 | tf_op jit(solution)/shard_map/ppermute | solution.py:367
  25.4 1.3 %collective-permute-start.14 = (f32[9,32,128]{2,1,0:T(8,128)S(1)}, f32[9,32,128]{2,1,0:T(8,128)S(1)}, u32[]{:S(2)}, u32[]{:S(2)}) collective-permute-start(f32[9,32,128]{2,1,0:T(8,128)S(1)} %collective-permute-done.13.refs_14_), channel_id=1, source_target_pairs={{0,1},{1,0},{2,3},{3,2},{4,5},{5,4},{6,7},{7,6},{8,9},{9,8},{10,11... | collective-permute-start | bytes 442376 | tf_op jit(solution)/shard_map/ppermute | solution.py:370
  26.7 0.1 collective-permute-start.10
  26.8 1.8 %collective-permute-done.5.refs_6_ = f32[9,32,128]{2,1,0:T(8,128)S(1)} collective-permute-done((f32[9,32,128]{2,1,0:T(8,128)S(1)}, f32[9,32,128]{2,1,0:T(8,128)S(1)}, u32[]{:S(2)}, u32[]{:S(2)}) %collective-permute-start.5) | collective-permute-done | bytes 147488 | tf_op jit(solution)/shard_map/ppermute | solution.py:367
  28.6 0.8 %collective-permute-start.6 = (f32[9,32,128]{2,1,0:T(8,128)S(1)}, f32[9,32,128]{2,1,0:T(8,128)S(1)}, u32[]{:S(2)}, u32[]{:S(2)}) collective-permute-start(f32[9,32,128]{2,1,0:T(8,128)S(1)} %collective-permute-done.5.refs_6_), channel_id=1, source_target_pairs={{0,1},{1,0},{2,3},{3,2},{4,5},{5,4},{6,7},{7,6},{8,9},{9,8},{10,11... | collective-permute-start | bytes 442376 | tf_op jit(solution)/shard_map/ppermute | solution.py:370
  29.4 0.7 %copy.9.refs_16_ = f32[8,3,3]{2,1,0:T(4,128)} copy(f32[8,3,3]{0,2,1:T(4,128)S(1)} %copy-done.15) | data formatting | bytes 576 | tf_op args[5]
  30.1 0.0 collective-permute-done.2.refs_3_
  30.2 0.2 collective-permute-done.6.refs_7_
  30.5 0.3 copy-done.10
  30.8 0.1 copy-done.11
  30.8 0.1 copy-done.12
  30.9 0.1 copy-done.13
  31.0 0.6 %copy-done.14 = f32[9,32,128]{2,1,0:T(8,128)} copy-done((f32[9,32,128]{2,1,0:T(8,128)}, f32[9,32,128]{2,1,0:T(8,128)S(1)}, u32[]{:S(2)}) %copy-start.14) | copy-done | bytes 147480
  31.6 32.3 %shard_map.87 = (f32[32,128]{1,0:T(8,128)}, f32[32,128]{1,0:T(8,128)}) custom-call(f32[9,32,128]{2,1,0:T(8,128)} %shard_map.86.refs_0_, f32[9,32,128]{2,1,0:T(8,128)} %copy-done.4, f32[9,32,128]{2,1,0:T(8,128)} %copy-done.3, f32[9,32,128]{2,1,0:T(8,128)} %copy-done.11, f32[9,32,128]{2,1,0:T(8,128)} %copy-done.2, f32[9,32,128]{2,1,0:T(8,128)} %copy-done.10, ...), custom_call_target="tpu_custom_call" | custom-call | tf_op jit(solution)/shard_map/pallas_call | solution.py:393
  (33 shorter events, 0.1 us)
Async XLA Ops:
  0.6 28.8 %copy-start.15 = (f32[8,3,3]{0,2,1:T(4,128)S(1)}, f32[8,3,3]{0,2,1:T(4,128)}, u32[]{:S(2)}) copy-start(f32[8,3,3]{0,2,1:T(4,128)} %param.12) | copy-start | bytes 868
  2.2 8.0 %collective-permute-start.11 = (f32[9,32,128]{2,1,0:T(8,128)}, f32[9,32,128]{2,1,0:T(8,128)S(1)}, u32[]{:S(2)}, u32[]{:S(2)}) collective-permute-start(f32[9,32,128]{2,1,0:T(8,128)} %shard_map.86.refs_0_), channel_id=1, source_target_pairs={{0,12},{2,14},{4,8},{6,10},{8,4},{10,6},{12,0},{14,2},{1,13},{3,15... | collective-permute-start | bytes 442376 | tf_op jit(solution)/shard_map/ppermute | solution.py:367
  6.3 12.3 %collective-permute-start.7 = (f32[9,32,128]{2,1,0:T(8,128)}, f32[9,32,128]{2,1,0:T(8,128)S(1)}, u32[]{:S(2)}, u32[]{:S(2)}) collective-permute-start(f32[9,32,128]{2,1,0:T(8,128)} %shard_map.86.refs_0_), channel_id=1, source_target_pairs={{0,8},{2,10},{4,12},{6,14},{8,0},{10,2},{12,4},{14,6},{1,9},{3,11}... | collective-permute-start | bytes 442376 | tf_op jit(solution)/shard_map/ppermute | solution.py:367
  6.3 13.6 %collective-permute-start.3 = (f32[9,32,128]{2,1,0:T(8,128)}, f32[9,32,128]{2,1,0:T(8,128)S(1)}, u32[]{:S(2)}, u32[]{:S(2)}) collective-permute-start(f32[9,32,128]{2,1,0:T(8,128)} %shard_map.86.refs_0_), channel_id=1, source_target_pairs={{0,4},{2,6},{4,0},{6,2},{8,12},{10,14},{12,8},{14,10},{1,5},{3,7},... | collective-permute-start | bytes 442376 | tf_op jit(solution)/shard_map/ppermute | solution.py:367
  6.6 14.6 %collective-permute-start.1 = (f32[9,32,128]{2,1,0:T(8,128)}, f32[9,32,128]{2,1,0:T(8,128)S(1)}, u32[]{:S(2)}, u32[]{:S(2)}) collective-permute-start(f32[9,32,128]{2,1,0:T(8,128)} %shard_map.86.refs_0_), channel_id=1, source_target_pairs={{0,2},{2,0},{4,6},{6,4},{8,10},{10,8},{12,14},{14,12},{1,3},{3,1},... | collective-permute-start | bytes 442376 | tf_op jit(solution)/shard_map/ppermute | solution.py:367
  7.8 13.7 %collective-permute-start = (f32[9,32,128]{2,1,0:T(8,128)}, f32[9,32,128]{2,1,0:T(8,128)S(1)}, u32[]{:S(2)}, u32[]{:S(2)}) collective-permute-start(f32[9,32,128]{2,1,0:T(8,128)} %shard_map.86.refs_0_), channel_id=1, source_target_pairs={{0,1},{1,0},{2,3},{3,2},{4,5},{5,4},{6,7},{7,6},{8,9},{9,8},{10,11... | collective-permute-start | bytes 442376 | tf_op jit(solution)/shard_map/ppermute | solution.py:370
  10.2 20.3 %copy-start = (f32[9,32,128]{2,1,0:T(8,128)}, f32[9,32,128]{2,1,0:T(8,128)S(1)}, u32[]{:S(2)}) copy-start(f32[9,32,128]{2,1,0:T(8,128)S(1)} %collective-permute-done.11.refs_12_) | copy-start | bytes 442372
  10.2 11.7 %collective-permute-start.13 = (f32[9,32,128]{2,1,0:T(8,128)S(1)}, f32[9,32,128]{2,1,0:T(8,128)S(1)}, u32[]{:S(2)}, u32[]{:S(2)}) collective-permute-start(f32[9,32,128]{2,1,0:T(8,128)S(1)} %collective-permute-done.11.refs_12_), channel_id=1, source_target_pairs={{0,2},{2,0},{4,6},{6,4},{8,10},{10,8},{12,14},{14,12},{1,3},{3,1},... | collective-permute-start | bytes 442376 | tf_op jit(solution)/shard_map/ppermute | solution.py:367
  18.6 11.8 %copy-start.1 = (f32[9,32,128]{2,1,0:T(8,128)}, f32[9,32,128]{2,1,0:T(8,128)S(1)}, u32[]{:S(2)}) copy-start(f32[9,32,128]{2,1,0:T(8,128)S(1)} %collective-permute-done.7.refs_8_) | copy-start | bytes 442372
  18.6 3.7 %collective-permute-start.12 = (f32[9,32,128]{2,1,0:T(8,128)S(1)}, f32[9,32,128]{2,1,0:T(8,128)S(1)}, u32[]{:S(2)}, u32[]{:S(2)}) collective-permute-start(f32[9,32,128]{2,1,0:T(8,128)S(1)} %collective-permute-done.11.refs_12_), channel_id=1, source_target_pairs={{0,1},{1,0},{2,3},{3,2},{4,5},{5,4},{6,7},{7,6},{8,9},{9,8},{10,11... | collective-permute-start | bytes 442376 | tf_op jit(solution)/shard_map/ppermute | solution.py:370
  20.0 10.5 %copy-start.2 = (f32[9,32,128]{2,1,0:T(8,128)}, f32[9,32,128]{2,1,0:T(8,128)S(1)}, u32[]{:S(2)}) copy-start(f32[9,32,128]{2,1,0:T(8,128)S(1)} %collective-permute-done.3.refs_4_) | copy-start | bytes 442372
  20.0 5.4 %collective-permute-start.9 = (f32[9,32,128]{2,1,0:T(8,128)S(1)}, f32[9,32,128]{2,1,0:T(8,128)S(1)}, u32[]{:S(2)}, u32[]{:S(2)}) collective-permute-start(f32[9,32,128]{2,1,0:T(8,128)S(1)} %collective-permute-done.7.refs_8_), channel_id=1, source_target_pairs={{0,2},{2,0},{4,6},{6,4},{8,10},{10,8},{12,14},{14,12},{1,3},{3,1},... | collective-permute-start | bytes 442376 | tf_op jit(solution)/shard_map/ppermute | solution.py:367
  21.2 9.2 %copy-start.3 = (f32[9,32,128]{2,1,0:T(8,128)}, f32[9,32,128]{2,1,0:T(8,128)S(1)}, u32[]{:S(2)}) copy-start(f32[9,32,128]{2,1,0:T(8,128)S(1)} %collective-permute-done.1.refs_2_) | copy-start | bytes 442372
  21.2 5.5 %collective-permute-start.8 = (f32[9,32,128]{2,1,0:T(8,128)S(1)}, f32[9,32,128]{2,1,0:T(8,128)S(1)}, u32[]{:S(2)}, u32[]{:S(2)}) collective-permute-start(f32[9,32,128]{2,1,0:T(8,128)S(1)} %collective-permute-done.7.refs_8_), channel_id=1, source_target_pairs={{0,1},{1,0},{2,3},{3,2},{4,5},{5,4},{6,7},{7,6},{8,9},{9,8},{10,11... | collective-permute-start | bytes 442376 | tf_op jit(solution)/shard_map/ppermute | solution.py:370
  21.6 8.9 %copy-start.4 = (f32[9,32,128]{2,1,0:T(8,128)}, f32[9,32,128]{2,1,0:T(8,128)S(1)}, u32[]{:S(2)}) copy-start(f32[9,32,128]{2,1,0:T(8,128)S(1)} %collective-permute-done.refs_1_) | copy-start | bytes 442372
  21.6 7.0 %collective-permute-start.5 = (f32[9,32,128]{2,1,0:T(8,128)S(1)}, f32[9,32,128]{2,1,0:T(8,128)S(1)}, u32[]{:S(2)}, u32[]{:S(2)}) collective-permute-start(f32[9,32,128]{2,1,0:T(8,128)S(1)} %collective-permute-done.3.refs_4_), channel_id=1, source_target_pairs={{0,2},{2,0},{4,6},{6,4},{8,10},{10,8},{12,14},{14,12},{1,3},{3,1},... | collective-permute-start | bytes 442376 | tf_op jit(solution)/shard_map/ppermute | solution.py:367
  21.8 8.6 %copy-start.5 = (f32[9,32,128]{2,1,0:T(8,128)}, f32[9,32,128]{2,1,0:T(8,128)S(1)}, u32[]{:S(2)}) copy-start(f32[9,32,128]{2,1,0:T(8,128)S(1)} %collective-permute-done.13.refs_14_) | copy-start | bytes 442372
  21.8 8.3 %collective-permute-start.4 = (f32[9,32,128]{2,1,0:T(8,128)S(1)}, f32[9,32,128]{2,1,0:T(8,128)S(1)}, u32[]{:S(2)}, u32[]{:S(2)}) collective-permute-start(f32[9,32,128]{2,1,0:T(8,128)S(1)} %collective-permute-done.3.refs_4_), channel_id=1, source_target_pairs={{0,1},{1,0},{2,3},{3,2},{4,5},{5,4},{6,7},{7,6},{8,9},{9,8},{10,11... | collective-permute-start | bytes 442376 | tf_op jit(solution)/shard_map/ppermute | solution.py:370
  22.3 8.2 %copy-start.6 = (f32[9,32,128]{2,1,0:T(8,128)}, f32[9,32,128]{2,1,0:T(8,128)S(1)}, u32[]{:S(2)}) copy-start(f32[9,32,128]{2,1,0:T(8,128)S(1)} %collective-permute-done.12.refs_13_) | copy-start | bytes 442372
  22.3 7.8 %collective-permute-start.2 = (f32[9,32,128]{2,1,0:T(8,128)S(1)}, f32[9,32,128]{2,1,0:T(8,128)S(1)}, u32[]{:S(2)}, u32[]{:S(2)}) collective-permute-start(f32[9,32,128]{2,1,0:T(8,128)S(1)} %collective-permute-done.1.refs_2_), channel_id=1, source_target_pairs={{0,1},{1,0},{2,3},{3,2},{4,5},{5,4},{6,7},{7,6},{8,9},{9,8},{10,11... | collective-permute-start | bytes 442376 | tf_op jit(solution)/shard_map/ppermute | solution.py:370
  25.4 5.1 %copy-start.7 = (f32[9,32,128]{2,1,0:T(8,128)}, f32[9,32,128]{2,1,0:T(8,128)S(1)}, u32[]{:S(2)}) copy-start(f32[9,32,128]{2,1,0:T(8,128)S(1)} %collective-permute-done.9.refs_10_) | copy-start | bytes 442372
  25.4 4.7 %collective-permute-start.14 = (f32[9,32,128]{2,1,0:T(8,128)S(1)}, f32[9,32,128]{2,1,0:T(8,128)S(1)}, u32[]{:S(2)}, u32[]{:S(2)}) collective-permute-start(f32[9,32,128]{2,1,0:T(8,128)S(1)} %collective-permute-done.13.refs_14_), channel_id=1, source_target_pairs={{0,1},{1,0},{2,3},{3,2},{4,5},{5,4},{6,7},{7,6},{8,9},{9,8},{10,11... | collective-permute-start | bytes 442376 | tf_op jit(solution)/shard_map/ppermute | solution.py:370
  26.7 3.8 %copy-start.8 = (f32[9,32,128]{2,1,0:T(8,128)}, f32[9,32,128]{2,1,0:T(8,128)S(1)}, u32[]{:S(2)}) copy-start(f32[9,32,128]{2,1,0:T(8,128)S(1)} %collective-permute-done.8.refs_9_) | copy-start | bytes 442372
  26.7 3.4 %collective-permute-start.10 = (f32[9,32,128]{2,1,0:T(8,128)S(1)}, f32[9,32,128]{2,1,0:T(8,128)S(1)}, u32[]{:S(2)}, u32[]{:S(2)}) collective-permute-start(f32[9,32,128]{2,1,0:T(8,128)S(1)} %collective-permute-done.9.refs_10_), channel_id=1, source_target_pairs={{0,1},{1,0},{2,3},{3,2},{4,5},{5,4},{6,7},{7,6},{8,9},{9,8},{10,11... | collective-permute-start | bytes 442376 | tf_op jit(solution)/shard_map/ppermute | solution.py:370
  28.6 1.9 %copy-start.9 = (f32[9,32,128]{2,1,0:T(8,128)}, f32[9,32,128]{2,1,0:T(8,128)S(1)}, u32[]{:S(2)}) copy-start(f32[9,32,128]{2,1,0:T(8,128)S(1)} %collective-permute-done.5.refs_6_) | copy-start | bytes 442372
  28.6 1.9 %collective-permute-start.6 = (f32[9,32,128]{2,1,0:T(8,128)S(1)}, f32[9,32,128]{2,1,0:T(8,128)S(1)}, u32[]{:S(2)}, u32[]{:S(2)}) collective-permute-start(f32[9,32,128]{2,1,0:T(8,128)S(1)} %collective-permute-done.5.refs_6_), channel_id=1, source_target_pairs={{0,1},{1,0},{2,3},{3,2},{4,5},{5,4},{6,7},{7,6},{8,9},{9,8},{10,11... | collective-permute-start | bytes 442376 | tf_op jit(solution)/shard_map/ppermute | solution.py:370
  30.1 0.6 %copy-start.10 = (f32[9,32,128]{2,1,0:T(8,128)}, f32[9,32,128]{2,1,0:T(8,128)S(1)}, u32[]{:S(2)}) copy-start(f32[9,32,128]{2,1,0:T(8,128)S(1)} %collective-permute-done.4.refs_5_) | copy-start | bytes 442372
  30.1 0.7 %copy-start.11 = (f32[9,32,128]{2,1,0:T(8,128)}, f32[9,32,128]{2,1,0:T(8,128)S(1)}, u32[]{:S(2)}) copy-start(f32[9,32,128]{2,1,0:T(8,128)S(1)} %collective-permute-done.2.refs_3_) | copy-start | bytes 442372
  30.1 0.8 %copy-start.12 = (f32[9,32,128]{2,1,0:T(8,128)}, f32[9,32,128]{2,1,0:T(8,128)S(1)}, u32[]{:S(2)}) copy-start(f32[9,32,128]{2,1,0:T(8,128)S(1)} %collective-permute-done.14.refs_15_) | copy-start | bytes 442372
  30.2 0.8 %copy-start.13 = (f32[9,32,128]{2,1,0:T(8,128)}, f32[9,32,128]{2,1,0:T(8,128)S(1)}, u32[]{:S(2)}) copy-start(f32[9,32,128]{2,1,0:T(8,128)S(1)} %collective-permute-done.10.refs_11_) | copy-start | bytes 442372
  31.0 0.7 %copy-start.14 = (f32[9,32,128]{2,1,0:T(8,128)}, f32[9,32,128]{2,1,0:T(8,128)S(1)}, u32[]{:S(2)}) copy-start(f32[9,32,128]{2,1,0:T(8,128)S(1)} %collective-permute-done.6.refs_7_) | copy-start | bytes 442372

commit v4 on v3

--- a/solution.py
+++ b/solution.py
@@ -38,6 +38,7 @@
 half_step = 0.5 * time_step
 LEVELS = 2 * (STEPS + 1)
 FIELDS = 9
+GROUP = 4
 
 
 def kernel(ring, half, *refs):
@@ -51,8 +52,10 @@
         matter,
         inverse,
         coef,
-        sums,
-        carry,
+        even_sums,
+        odd_sums,
+        even_carry,
+        odd_carry,
         ray,
     ) = refs[2 * ring + 4 :]
     rows = 2 * half
@@ -77,6 +80,8 @@
         return pl.ds(TILE + TILE * tile + shift, TILE)
 
     fields = (even_fields, odd_fields)
+    sums_of = (even_sums, odd_sums)
+    carry_of = (even_carry, odd_carry)
 
     def put_field(odd, number, slab, comp, tile, value):
         deeper = ahead(value)
@@ -135,7 +140,7 @@
         entries = block_entries(direction)
 
         def fill(pair, _, direction=direction, entries=entries):
-            for slab, tile in [(2 * pair + which, tile) for which in range(2) for tile in range(tiles)]:
+            for slab, tile in [(GROUP * pair + which, tile) for which in range(GROUP) for tile in range(tiles)]:
                 first, second = matter_ends(0, slab, direction, tile)
                 spring_first, spring_second = matter_ends(1, slab, direction, tile)
                 bond = 0.5 * (spring_first + spring_second)
@@ -145,7 +150,7 @@
                     coef[slab, 6 * direction + n, at(tile)] = bond * entry
             return 0
 
-        lax.fori_loop(0, ring // 2, fill, 0)
+        lax.fori_loop(0, ring // GROUP, fill, 0)
 
     def product(entry, vector):
         return [
@@ -155,6 +160,7 @@
 
     def bonds(odd, number, slab, order):
         beside = wrap(slab + 1)
+        sums, carry = sums_of[odd], carry_of[odd]
         for tile in order:
             loaded = {}
 
@@ -212,6 +218,7 @@
 
     def update(odd, number, slab, order, kick, kind):
         mine = jnp.where(slab == me, 1, 0)
+        sums, carry = sums_of[odd], carry_of[odd]
         detect = depth_index >= ZCELLS // 2
         detect = (detect, (depth_index >= ZCELLS // 2 - 1) & inside)
         for tile in order:
@@ -235,27 +242,32 @@
                     for place in (tile,) if tile else (0, tiles):
                         fields[1 - odd][frame, number + odd, slab, comp, at(place)] = fresh
 
-    def step(odd, number, order, kind):
+    def span(level):
+        count = jnp.minimum(ring, 2 * (LEVELS - level))
+        low = jnp.where(count < ring, me + level + ring - LEVELS, me + 2 * level + ring // 2)
+        return wrap(low + ring), count
+
+    def middle_part(odd, number, order, kind, low, count, kick):
+        def both(pair, _):
+            for place in (2 * pair, 2 * pair + 1):
+                for tile in order:
+                    update(odd, number, wrap(low + place + 1), [tile], kick, kind)
+                    bonds(odd, number, wrap(low + place + 2), [tile])
+            return 0
+
+        lax.fori_loop(0, lax.div(count - 2, 2), both, 0)
+
+    def step(odd, number, order, kind, final=False):
         level = 2 * number + odd
-        reach = LEVELS - 1 - level
-        count = jnp.minimum(ring, 2 * reach + 2)
-        low = wrap(me - jnp.minimum(reach + 1, ring // 2) + ring)
+        low, count = span(level)
         kick = jnp.where((level == 0) | (level == STEPS) | (level == STEPS + 1), 0.5, 1.0)
-
-        def start(place, _):
-            bonds(odd, number, wrap(low + place), order)
-            return 0
-
-        def both(place, _):
+        middle_part(odd, number, order, kind, low, count, kick)
+        ahead_low = span(level + 1)[0]
+        for place, slab in enumerate((wrap(low + count - 1), low)):
             for tile in order:
-                update(odd, number, wrap(low + place + 1), [tile], kick, kind)
-                bonds(odd, number, wrap(low + place + 2), [tile])
-            return 0
-
-        lax.fori_loop(0, 2, start, 0)
-        lax.fori_loop(0, count - 2, both, 0)
-        update(odd, number, wrap(low + count - 1), order, kick, kind)
-        update(odd, number, low, order, kick, kind)
+                if not final:
+                    bonds(1 - odd, number + odd, wrap(ahead_low + place), [tile])
+                update(odd, number, slab, [tile], kick, kind)
 
     everything = list(range(tiles))
     near = [tiles - 1] + list(range(own_tiles + 1))
@@ -266,6 +278,7 @@
         if level % 2:
             step(1, level // 2, order, kind)
             level += 1
+        last = stop == LEVELS - 1
         pairs = (stop - level) // 2
 
         def two(number, _):
@@ -276,8 +289,10 @@
         if pairs:
             lax.fori_loop(level // 2, level // 2 + pairs, two, 0)
         if (stop - level) % 2:
-            step(0, stop // 2, order, kind)
-
+            step(0, stop // 2, order, kind, last)
+
+    for place in range(2):
+        bonds(0, 0, wrap(span(0)[0] + place), everything)
     run(0, wide, everything, "state")
     run(wide, STEPS, near, "state")
     run(STEPS, STEPS + 1, near, "middle")
@@ -387,6 +402,8 @@
         (2, ring, rows, ZCELLS),
         (ring, 54, rows, ZCELLS),
         (4, ring, 3, padded, ZCELLS),
+        (4, ring, 3, padded, ZCELLS),
+        (3, ring, 3, padded, ZCELLS),
         (3, ring, 3, padded, ZCELLS),
         (4, padded, ZCELLS),
     ]

time: 64.1 us -> 62.4 us (0.973)
  Pallas kernels: 33.8 us -> 32.2 us
    pallas_call x1, Pallas kernels: 32.3 us -> 30.6 us  [gathered_body(): pl.pallas_call(lambda *refs: kernel(ring, half, *refs), out_shape=[jax.Sh...]
where the time goes in v4:
time: 62.4 us; the launch traced here: 62.2 us
  Pallas kernels  32.2 us (52%)
  starting transfers between devices  14.3 us (23%)
  waiting for transfers between devices  13.1 us (21%)
  local copies, waits for them, and re-layouts  1.85 us (3%)
  between operations  0.76 us (1%)
    pallas_call x1, Pallas kernels, gathered_body(): pl.pallas_call(lambda *refs: kernel(ring, half, *refs), out_shape=[jax.Sh...  30.6 us
    ppermute x7, waiting for transfers between devices, swap_slabs(): return lax.ppermute(value, 'gx', [(i, i ^ mask) for i in range(ring)])  12.9 us
    ppermute x7, starting transfers between devices, swap_slabs(): return lax.ppermute(value, 'gx', [(i, i ^ mask) for i in range(ring)])  8.14 us
    ppermute x8, starting transfers between devices, swap_halves(): return lax.ppermute(value, 'gy', [(0, 1), (1, 0)])  6.2 us
    unnamed x33, local copies, waits for them, and re-layouts  1.85 us
    pallas_call x1, Pallas kernels, gathered_body(): pl.pallas_call(pack, out_shape=jax.ShapeDtypeStruct((FIELDS, half, ZCELLS...  1.53 us
  transfers between devices with their start and end apart: 15, of which 5 were waited for; matrix products, arithmetic and copies ran while one was open for 1% of the time, Pallas kernels for 0%

profile of v4, /device:TPU:1, one launch (start us, length us, event | category | flops | bytes accessed | tf_op | source)
XLA Modules:
  0.0 62.2 jit_solution(12446595796608233788)
XLA Ops:
  0.6 1.5 %shard_map.86.refs_0_ = f32[9,32,128]{2,1,0:T(8,128)} custom-call(f32[3,1,32,128]{3,2,1,0:T(8,128)} %displacement.1, f32[3,1,32,128]{3,2,1,0:T(8,128)} %velocity.1, s32[1,32,128]{2,1,0:T(8,128)} %species.1, f32[1,32,128]{2,1,0:T(8,128)} %mass_factor.1, f32[1,32,128]{2,1,0:T(8,128)} %spring.1), custom_call_target="tpu_custom_call" | custom-call | tf_op jit(solution)/shard_map/pallas_call | solution.py:374
  2.2 4.2 %collective-permute-start.11 = (f32[9,32,128]{2,1,0:T(8,128)}, f32[9,32,128]{2,1,0:T(8,128)S(1)}, u32[]{:S(2)}, u32[]{:S(2)}) collective-permute-start(f32[9,32,128]{2,1,0:T(8,128)} %shard_map.86.refs_0_), channel_id=1, source_target_pairs={{0,12},{2,14},{4,8},{6,10},{8,4},{10,6},{12,0},{14,2},{1,13},{3,15... | collective-permute-start | bytes 442376 | tf_op jit(solution)/shard_map/ppermute | solution.py:382
  6.3 0.3 collective-permute-start.3
  6.6 1.2 %collective-permute-start.1 = (f32[9,32,128]{2,1,0:T(8,128)}, f32[9,32,128]{2,1,0:T(8,128)S(1)}, u32[]{:S(2)}, u32[]{:S(2)}) collective-permute-start(f32[9,32,128]{2,1,0:T(8,128)} %shard_map.86.refs_0_), channel_id=1, source_target_pairs={{0,2},{2,0},{4,6},{6,4},{8,10},{10,8},{12,14},{14,12},{1,3},{3,1},... | collective-permute-start | bytes 442376 | tf_op jit(solution)/shard_map/ppermute | solution.py:382
  7.8 1.7 %collective-permute-start = (f32[9,32,128]{2,1,0:T(8,128)}, f32[9,32,128]{2,1,0:T(8,128)S(1)}, u32[]{:S(2)}, u32[]{:S(2)}) collective-permute-start(f32[9,32,128]{2,1,0:T(8,128)} %shard_map.86.refs_0_), channel_id=1, source_target_pairs={{0,1},{1,0},{2,3},{3,2},{4,5},{5,4},{6,7},{7,6},{8,9},{9,8},{10,11... | collective-permute-start | bytes 442376 | tf_op jit(solution)/shard_map/ppermute | solution.py:385
  9.6 0.6 collective-permute-done.11.refs_12_
  10.2 1.0 %collective-permute-start.13 = (f32[9,32,128]{2,1,0:T(8,128)S(1)}, f32[9,32,128]{2,1,0:T(8,128)S(1)}, u32[]{:S(2)}, u32[]{:S(2)}) collective-permute-start(f32[9,32,128]{2,1,0:T(8,128)S(1)} %collective-permute-done.11.refs_12_), channel_id=1, source_target_pairs={{0,2},{2,0},{4,6},{6,4},{8,10},{10,8},{12,14},{14,12},{1,3},{3,1},... | collective-permute-start | bytes 442376 | tf_op jit(solution)/shard_map/ppermute | solution.py:382
  11.2 7.4 %collective-permute-done.7.refs_8_ = f32[9,32,128]{2,1,0:T(8,128)S(1)} collective-permute-done((f32[9,32,128]{2,1,0:T(8,128)}, f32[9,32,128]{2,1,0:T(8,128)S(1)}, u32[]{:S(2)}, u32[]{:S(2)}) %collective-permute-start.7) | collective-permute-done | bytes 147488 | tf_op jit(solution)/shard_map/ppermute | solution.py:382
  18.6 1.4 %collective-permute-start.12 = (f32[9,32,128]{2,1,0:T(8,128)S(1)}, f32[9,32,128]{2,1,0:T(8,128)S(1)}, u32[]{:S(2)}, u32[]{:S(2)}) collective-permute-start(f32[9,32,128]{2,1,0:T(8,128)S(1)} %collective-permute-done.11.refs_12_), channel_id=1, source_target_pairs={{0,1},{1,0},{2,3},{3,2},{4,5},{5,4},{6,7},{7,6},{8,9},{9,8},{10,11... | collective-permute-start | bytes 442376 | tf_op jit(solution)/shard_map/ppermute | solution.py:385
  20.0 0.0 collective-permute-done.3.refs_4_
  20.0 1.2 %collective-permute-start.9 = (f32[9,32,128]{2,1,0:T(8,128)S(1)}, f32[9,32,128]{2,1,0:T(8,128)S(1)}, u32[]{:S(2)}, u32[]{:S(2)}) collective-permute-start(f32[9,32,128]{2,1,0:T(8,128)S(1)} %collective-permute-done.7.refs_8_), channel_id=1, source_target_pairs={{0,2},{2,0},{4,6},{6,4},{8,10},{10,8},{12,14},{14,12},{1,3},{3,1},... | collective-permute-start | bytes 442376 | tf_op jit(solution)/shard_map/ppermute | solution.py:382
  21.2 0.0 collective-permute-done.1.refs_2_
  21.2 0.3 collective-permute-start.8
  21.6 0.0 collective-permute-done.refs_1_
  21.6 0.3 collective-permute-start.5
  21.8 0.4 collective-permute-start.4
  22.3 0.0 collective-permute-done.12.refs_13_
  22.3 0.1 collective-permute-start.2
  22.4 3.0 %collective-permute-done.9.refs_10_ = f32[9,32,128]{2,1,0:T(8,128)S(1)} collective-permute-done((f32[9,32,128]{2,1,0:T(8,128)S(1)}, f32[9,32,128]{2,1,0:T(8,128)S(1)}, u32[]{:S(2)}, u32[]{:S(2)}) %collective-permute-start.9) | collective-permute-done | bytes 147488 | tf_op jit(solution)/shard_map/ppermute | solution.py:382
  25.4 1.3 %collective-permute-start.14 = (f32[9,32,128]{2,1,0:T(8,128)S(1)}, f32[9,32,128]{2,1,0:T(8,128)S(1)}, u32[]{:S(2)}, u32[]{:S(2)}) collective-permute-start(f32[9,32,128]{2,1,0:T(8,128)S(1)} %collective-permute-done.13.refs_14_), channel_id=1, source_target_pairs={{0,1},{1,0},{2,3},{3,2},{4,5},{5,4},{6,7},{7,6},{8,9},{9,8},{10,11... | collective-permute-start | bytes 442376 | tf_op jit(solution)/shard_map/ppermute | solution.py:385
  26.7 0.1 collective-permute-start.10
  26.8 1.8 %collective-permute-done.5.refs_6_ = f32[9,32,128]{2,1,0:T(8,128)S(1)} collective-permute-done((f32[9,32,128]{2,1,0:T(8,128)S(1)}, f32[9,32,128]{2,1,0:T(8,128)S(1)}, u32[]{:S(2)}, u32[]{:S(2)}) %collective-permute-start.5) | collective-permute-done | bytes 147488 | tf_op jit(solution)/shard_map/ppermute | solution.py:382
  28.6 0.8 %collective-permute-start.6 = (f32[9,32,128]{2,1,0:T(8,128)S(1)}, f32[9,32,128]{2,1,0:T(8,128)S(1)}, u32[]{:S(2)}, u32[]{:S(2)}) collective-permute-start(f32[9,32,128]{2,1,0:T(8,128)S(1)} %collective-permute-done.5.refs_6_), channel_id=1, source_target_pairs={{0,1},{1,0},{2,3},{3,2},{4,5},{5,4},{6,7},{7,6},{8,9},{9,8},{10,11... | collective-permute-start | bytes 442376 | tf_op jit(solution)/shard_map/ppermute | solution.py:385
  29.4 0.7 %copy.9.refs_16_ = f32[8,3,3]{2,1,0:T(4,128)} copy(f32[8,3,3]{0,2,1:T(4,128)S(1)} %copy-done.15) | data formatting | bytes 576 | tf_op args[5]
  30.1 0.0 collective-permute-done.4.refs_5_
  30.2 0.2 collective-permute-done.6.refs_7_
  30.5 0.3 copy-done.10
  30.8 0.1 copy-done.11
  30.8 0.1 copy-done.12
  30.9 0.1 copy-done.13
  31.0 0.6 %copy-done.14 = f32[9,32,128]{2,1,0:T(8,128)} copy-done((f32[9,32,128]{2,1,0:T(8,128)}, f32[9,32,128]{2,1,0:T(8,128)S(1)}, u32[]{:S(2)}) %copy-start.14) | copy-done | bytes 147480
  31.6 30.6 %shard_map.87 = (f32[32,128]{1,0:T(8,128)}, f32[32,128]{1,0:T(8,128)}) custom-call(f32[9,32,128]{2,1,0:T(8,128)} %shard_map.86.refs_0_, f32[9,32,128]{2,1,0:T(8,128)} %copy-done.4, f32[9,32,128]{2,1,0:T(8,128)} %copy-done.3, f32[9,32,128]{2,1,0:T(8,128)} %copy-done.11, f32[9,32,128]{2,1,0:T(8,128)} %copy-done.2, f32[9,32,128]{2,1,0:T(8,128)} %copy-done.10, ...), custom_call_target="tpu_custom_call" | custom-call | tf_op jit(solution)/shard_map/pallas_call | solution.py:410
  (33 shorter events, 0.1 us)
Async XLA Ops:
  0.6 28.8 %copy-start.15 = (f32[8,3,3]{0,2,1:T(4,128)S(1)}, f32[8,3,3]{0,2,1:T(4,128)}, u32[]{:S(2)}) copy-start(f32[8,3,3]{0,2,1:T(4,128)} %param.12) | copy-start | bytes 868
  2.2 8.0 %collective-permute-start.11 = (f32[9,32,128]{2,1,0:T(8,128)}, f32[9,32,128]{2,1,0:T(8,128)S(1)}, u32[]{:S(2)}, u32[]{:S(2)}) collective-permute-start(f32[9,32,128]{2,1,0:T(8,128)} %shard_map.86.refs_0_), channel_id=1, source_target_pairs={{0,12},{2,14},{4,8},{6,10},{8,4},{10,6},{12,0},{14,2},{1,13},{3,15... | collective-permute-start | bytes 442376 | tf_op jit(solution)/shard_map/ppermute | solution.py:382
  6.3 12.3 %collective-permute-start.7 = (f32[9,32,128]{2,1,0:T(8,128)}, f32[9,32,128]{2,1,0:T(8,128)S(1)}, u32[]{:S(2)}, u32[]{:S(2)}) collective-permute-start(f32[9,32,128]{2,1,0:T(8,128)} %shard_map.86.refs_0_), channel_id=1, source_target_pairs={{0,8},{2,10},{4,12},{6,14},{8,0},{10,2},{12,4},{14,6},{1,9},{3,11}... | collective-permute-start | bytes 442376 | tf_op jit(solution)/shard_map/ppermute | solution.py:382
  6.3 13.6 %collective-permute-start.3 = (f32[9,32,128]{2,1,0:T(8,128)}, f32[9,32,128]{2,1,0:T(8,128)S(1)}, u32[]{:S(2)}, u32[]{:S(2)}) collective-permute-start(f32[9,32,128]{2,1,0:T(8,128)} %shard_map.86.refs_0_), channel_id=1, source_target_pairs={{0,4},{2,6},{4,0},{6,2},{8,12},{10,14},{12,8},{14,10},{1,5},{3,7},... | collective-permute-start | bytes 442376 | tf_op jit(solution)/shard_map/ppermute | solution.py:382
  6.6 14.6 %collective-permute-start.1 = (f32[9,32,128]{2,1,0:T(8,128)}, f32[9,32,128]{2,1,0:T(8,128)S(1)}, u32[]{:S(2)}, u32[]{:S(2)}) collective-permute-start(f32[9,32,128]{2,1,0:T(8,128)} %shard_map.86.refs_0_), channel_id=1, source_target_pairs={{0,2},{2,0},{4,6},{6,4},{8,10},{10,8},{12,14},{14,12},{1,3},{3,1},... | collective-permute-start | bytes 442376 | tf_op jit(solution)/shard_map/ppermute | solution.py:382
  7.8 13.7 %collective-permute-start = (f32[9,32,128]{2,1,0:T(8,128)}, f32[9,32,128]{2,1,0:T(8,128)S(1)}, u32[]{:S(2)}, u32[]{:S(2)}) collective-permute-start(f32[9,32,128]{2,1,0:T(8,128)} %shard_map.86.refs_0_), channel_id=1, source_target_pairs={{0,1},{1,0},{2,3},{3,2},{4,5},{5,4},{6,7},{7,6},{8,9},{9,8},{10,11... | collective-permute-start | bytes 442376 | tf_op jit(solution)/shard_map/ppermute | solution.py:385
  10.2 20.3 %copy-start = (f32[9,32,128]{2,1,0:T(8,128)}, f32[9,32,128]{2,1,0:T(8,128)S(1)}, u32[]{:S(2)}) copy-start(f32[9,32,128]{2,1,0:T(8,128)S(1)} %collective-permute-done.11.refs_12_) | copy-start | bytes 442372
  10.2 11.7 %collective-permute-start.13 = (f32[9,32,128]{2,1,0:T(8,128)S(1)}, f32[9,32,128]{2,1,0:T(8,128)S(1)}, u32[]{:S(2)}, u32[]{:S(2)}) collective-permute-start(f32[9,32,128]{2,1,0:T(8,128)S(1)} %collective-permute-done.11.refs_12_), channel_id=1, source_target_pairs={{0,2},{2,0},{4,6},{6,4},{8,10},{10,8},{12,14},{14,12},{1,3},{3,1},... | collective-permute-start | bytes 442376 | tf_op jit(solution)/shard_map/ppermute | solution.py:382
  18.6 11.8 %copy-start.1 = (f32[9,32,128]{2,1,0:T(8,128)}, f32[9,32,128]{2,1,0:T(8,128)S(1)}, u32[]{:S(2)}) copy-start(f32[9,32,128]{2,1,0:T(8,128)S(1)} %collective-permute-done.7.refs_8_) | copy-start | bytes 442372
  18.6 3.7 %collective-permute-start.12 = (f32[9,32,128]{2,1,0:T(8,128)S(1)}, f32[9,32,128]{2,1,0:T(8,128)S(1)}, u32[]{:S(2)}, u32[]{:S(2)}) collective-permute-start(f32[9,32,128]{2,1,0:T(8,128)S(1)} %collective-permute-done.11.refs_12_), channel_id=1, source_target_pairs={{0,1},{1,0},{2,3},{3,2},{4,5},{5,4},{6,7},{7,6},{8,9},{9,8},{10,11... | collective-permute-start | bytes 442376 | tf_op jit(solution)/shard_map/ppermute | solution.py:385
  20.0 10.5 %copy-start.2 = (f32[9,32,128]{2,1,0:T(8,128)}, f32[9,32,128]{2,1,0:T(8,128)S(1)}, u32[]{:S(2)}) copy-start(f32[9,32,128]{2,1,0:T(8,128)S(1)} %collective-permute-done.3.refs_4_) | copy-start | bytes 442372
  20.0 5.4 %collective-permute-start.9 = (f32[9,32,128]{2,1,0:T(8,128)S(1)}, f32[9,32,128]{2,1,0:T(8,128)S(1)}, u32[]{:S(2)}, u32[]{:S(2)}) collective-permute-start(f32[9,32,128]{2,1,0:T(8,128)S(1)} %collective-permute-done.7.refs_8_), channel_id=1, source_target_pairs={{0,2},{2,0},{4,6},{6,4},{8,10},{10,8},{12,14},{14,12},{1,3},{3,1},... | collective-permute-start | bytes 442376 | tf_op jit(solution)/shard_map/ppermute | solution.py:382
  21.2 9.2 %copy-start.3 = (f32[9,32,128]{2,1,0:T(8,128)}, f32[9,32,128]{2,1,0:T(8,128)S(1)}, u32[]{:S(2)}) copy-start(f32[9,32,128]{2,1,0:T(8,128)S(1)} %collective-permute-done.1.refs_2_) | copy-start | bytes 442372
  21.2 5.5 %collective-permute-start.8 = (f32[9,32,128]{2,1,0:T(8,128)S(1)}, f32[9,32,128]{2,1,0:T(8,128)S(1)}, u32[]{:S(2)}, u32[]{:S(2)}) collective-permute-start(f32[9,32,128]{2,1,0:T(8,128)S(1)} %collective-permute-done.7.refs_8_), channel_id=1, source_target_pairs={{0,1},{1,0},{2,3},{3,2},{4,5},{5,4},{6,7},{7,6},{8,9},{9,8},{10,11... | collective-permute-start | bytes 442376 | tf_op jit(solution)/shard_map/ppermute | solution.py:385
  21.6 8.9 %copy-start.4 = (f32[9,32,128]{2,1,0:T(8,128)}, f32[9,32,128]{2,1,0:T(8,128)S(1)}, u32[]{:S(2)}) copy-start(f32[9,32,128]{2,1,0:T(8,128)S(1)} %collective-permute-done.refs_1_) | copy-start | bytes 442372
  21.6 7.0 %collective-permute-start.5 = (f32[9,32,128]{2,1,0:T(8,128)S(1)}, f32[9,32,128]{2,1,0:T(8,128)S(1)}, u32[]{:S(2)}, u32[]{:S(2)}) collective-permute-start(f32[9,32,128]{2,1,0:T(8,128)S(1)} %collective-permute-done.3.refs_4_), channel_id=1, source_target_pairs={{0,2},{2,0},{4,6},{6,4},{8,10},{10,8},{12,14},{14,12},{1,3},{3,1},... | collective-permute-start | bytes 442376 | tf_op jit(solution)/shard_map/ppermute | solution.py:382
  21.8 8.6 %copy-start.5 = (f32[9,32,128]{2,1,0:T(8,128)}, f32[9,32,128]{2,1,0:T(8,128)S(1)}, u32[]{:S(2)}) copy-start(f32[9,32,128]{2,1,0:T(8,128)S(1)} %collective-permute-done.13.refs_14_) | copy-start | bytes 442372
  21.8 8.3 %collective-permute-start.4 = (f32[9,32,128]{2,1,0:T(8,128)S(1)}, f32[9,32,128]{2,1,0:T(8,128)S(1)}, u32[]{:S(2)}, u32[]{:S(2)}) collective-permute-start(f32[9,32,128]{2,1,0:T(8,128)S(1)} %collective-permute-done.3.refs_4_), channel_id=1, source_target_pairs={{0,1},{1,0},{2,3},{3,2},{4,5},{5,4},{6,7},{7,6},{8,9},{9,8},{10,11... | collective-permute-start | bytes 442376 | tf_op jit(solution)/shard_map/ppermute | solution.py:385
  22.3 8.2 %copy-start.6 = (f32[9,32,128]{2,1,0:T(8,128)}, f32[9,32,128]{2,1,0:T(8,128)S(1)}, u32[]{:S(2)}) copy-start(f32[9,32,128]{2,1,0:T(8,128)S(1)} %collective-permute-done.12.refs_13_) | copy-start | bytes 442372
  22.3 7.8 %collective-permute-start.2 = (f32[9,32,128]{2,1,0:T(8,128)S(1)}, f32[9,32,128]{2,1,0:T(8,128)S(1)}, u32[]{:S(2)}, u32[]{:S(2)}) collective-permute-start(f32[9,32,128]{2,1,0:T(8,128)S(1)} %collective-permute-done.1.refs_2_), channel_id=1, source_target_pairs={{0,1},{1,0},{2,3},{3,2},{4,5},{5,4},{6,7},{7,6},{8,9},{9,8},{10,11... | collective-permute-start | bytes 442376 | tf_op jit(solution)/shard_map/ppermute | solution.py:385
  25.4 5.1 %copy-start.7 = (f32[9,32,128]{2,1,0:T(8,128)}, f32[9,32,128]{2,1,0:T(8,128)S(1)}, u32[]{:S(2)}) copy-start(f32[9,32,128]{2,1,0:T(8,128)S(1)} %collective-permute-done.9.refs_10_) | copy-start | bytes 442372
  25.4 4.7 %collective-permute-start.14 = (f32[9,32,128]{2,1,0:T(8,128)S(1)}, f32[9,32,128]{2,1,0:T(8,128)S(1)}, u32[]{:S(2)}, u32[]{:S(2)}) collective-permute-start(f32[9,32,128]{2,1,0:T(8,128)S(1)} %collective-permute-done.13.refs_14_), channel_id=1, source_target_pairs={{0,1},{1,0},{2,3},{3,2},{4,5},{5,4},{6,7},{7,6},{8,9},{9,8},{10,11... | collective-permute-start | bytes 442376 | tf_op jit(solution)/shard_map/ppermute | solution.py:385
  26.7 3.8 %copy-start.8 = (f32[9,32,128]{2,1,0:T(8,128)}, f32[9,32,128]{2,1,0:T(8,128)S(1)}, u32[]{:S(2)}) copy-start(f32[9,32,128]{2,1,0:T(8,128)S(1)} %collective-permute-done.8.refs_9_) | copy-start | bytes 442372
  26.7 3.4 %collective-permute-start.10 = (f32[9,32,128]{2,1,0:T(8,128)S(1)}, f32[9,32,128]{2,1,0:T(8,128)S(1)}, u32[]{:S(2)}, u32[]{:S(2)}) collective-permute-start(f32[9,32,128]{2,1,0:T(8,128)S(1)} %collective-permute-done.9.refs_10_), channel_id=1, source_target_pairs={{0,1},{1,0},{2,3},{3,2},{4,5},{5,4},{6,7},{7,6},{8,9},{9,8},{10,11... | collective-permute-start | bytes 442376 | tf_op jit(solution)/shard_map/ppermute | solution.py:385
  28.6 1.9 %copy-start.9 = (f32[9,32,128]{2,1,0:T(8,128)}, f32[9,32,128]{2,1,0:T(8,128)S(1)}, u32[]{:S(2)}) copy-start(f32[9,32,128]{2,1,0:T(8,128)S(1)} %collective-permute-done.5.refs_6_) | copy-start | bytes 442372
  28.6 1.9 %collective-permute-start.6 = (f32[9,32,128]{2,1,0:T(8,128)S(1)}, f32[9,32,128]{2,1,0:T(8,128)S(1)}, u32[]{:S(2)}, u32[]{:S(2)}) collective-permute-start(f32[9,32,128]{2,1,0:T(8,128)S(1)} %collective-permute-done.5.refs_6_), channel_id=1, source_target_pairs={{0,1},{1,0},{2,3},{3,2},{4,5},{5,4},{6,7},{7,6},{8,9},{9,8},{10,11... | collective-permute-start | bytes 442376 | tf_op jit(solution)/shard_map/ppermute | solution.py:385
  30.1 0.6 %copy-start.10 = (f32[9,32,128]{2,1,0:T(8,128)}, f32[9,32,128]{2,1,0:T(8,128)S(1)}, u32[]{:S(2)}) copy-start(f32[9,32,128]{2,1,0:T(8,128)S(1)} %collective-permute-done.4.refs_5_) | copy-start | bytes 442372
  30.1 0.7 %copy-start.11 = (f32[9,32,128]{2,1,0:T(8,128)}, f32[9,32,128]{2,1,0:T(8,128)S(1)}, u32[]{:S(2)}) copy-start(f32[9,32,128]{2,1,0:T(8,128)S(1)} %collective-permute-done.2.refs_3_) | copy-start | bytes 442372
  30.1 0.8 %copy-start.12 = (f32[9,32,128]{2,1,0:T(8,128)}, f32[9,32,128]{2,1,0:T(8,128)S(1)}, u32[]{:S(2)}) copy-start(f32[9,32,128]{2,1,0:T(8,128)S(1)} %collective-permute-done.14.refs_15_) | copy-start | bytes 442372
  30.2 0.8 %copy-start.13 = (f32[9,32,128]{2,1,0:T(8,128)}, f32[9,32,128]{2,1,0:T(8,128)S(1)}, u32[]{:S(2)}) copy-start(f32[9,32,128]{2,1,0:T(8,128)S(1)} %collective-permute-done.10.refs_11_) | copy-start | bytes 442372
  31.0 0.7 %copy-start.14 = (f32[9,32,128]{2,1,0:T(8,128)}, f32[9,32,128]{2,1,0:T(8,128)S(1)}, u32[]{:S(2)}) copy-start(f32[9,32,128]{2,1,0:T(8,128)S(1)} %collective-permute-done.6.refs_7_) | copy-start | bytes 442372

commit v5 on v4

--- a/solution.py
+++ b/solution.py
@@ -247,21 +247,22 @@
         low = jnp.where(count < ring, me + level + ring - LEVELS, me + 2 * level + ring // 2)
         return wrap(low + ring), count
 
-    def middle_part(odd, number, order, kind, low, count, kick):
+    def middle_part(odd, number, order, kind, low, count, kick, below):
         def both(pair, _):
             for place in (2 * pair, 2 * pair + 1):
-                for tile in order:
-                    update(odd, number, wrap(low + place + 1), [tile], kick, kind)
+                for tile in below + order:
+                    if tile in order:
+                        update(odd, number, wrap(low + place + 1), [tile], kick, kind)
                     bonds(odd, number, wrap(low + place + 2), [tile])
             return 0
 
         lax.fori_loop(0, lax.div(count - 2, 2), both, 0)
 
-    def step(odd, number, order, kind, final=False):
+    def step(odd, number, order, kind, final=False, below=()):
         level = 2 * number + odd
         low, count = span(level)
         kick = jnp.where((level == 0) | (level == STEPS) | (level == STEPS + 1), 0.5, 1.0)
-        middle_part(odd, number, order, kind, low, count, kick)
+        middle_part(odd, number, order, kind, low, count, kick, list(below))
         ahead_low = span(level + 1)[0]
         for place, slab in enumerate((wrap(low + count - 1), low)):
             for tile in order:
@@ -293,7 +294,8 @@
 
     for place in range(2):
         bonds(0, 0, wrap(span(0)[0] + place), everything)
-    run(0, wide, everything, "state")
+    run(0, wide - 1, everything, "state")
+    step((wide - 1) % 2, (wide - 1) // 2, near, "state", below=[tiles - 2])
     run(wide, STEPS, near, "state")
     run(STEPS, STEPS + 1, near, "middle")
     run(STEPS + 1, LEVELS - 1, near, "dual")

time: 62.4 us -> 61.8 us (level)
  Pallas kernels: 32.2 us -> 31.5 us
where the time goes in v5:
time: 61.8 us; the launch traced here: 61.6 us
  Pallas kernels  31.5 us (51%)
  starting transfers between devices  14.3 us (23%)
  waiting for transfers between devices  13.1 us (21%)
  local copies, waits for them, and re-layouts  1.85 us (3%)
  between operations  0.76 us (1%)
    pallas_call x1, Pallas kernels, gathered_body(): pl.pallas_call(lambda *refs: kernel(ring, half, *refs), out_shape=[jax.Sh...  30 us
    ppermute x7, waiting for transfers between devices, swap_slabs(): return lax.ppermute(value, 'gx', [(i, i ^ mask) for i in range(ring)])  12.9 us
    ppermute x7, starting transfers between devices, swap_slabs(): return lax.ppermute(value, 'gx', [(i, i ^ mask) for i in range(ring)])  8.14 us
    ppermute x8, starting transfers between devices, swap_halves(): return lax.ppermute(value, 'gy', [(0, 1), (1, 0)])  6.2 us
    unnamed x33, local copies, waits for them, and re-layouts  1.85 us
    pallas_call x1, Pallas kernels, gathered_body(): pl.pallas_call(pack, out_shape=jax.ShapeDtypeStruct((FIELDS, half, ZCELLS...  1.53 us
  transfers between devices with their start and end apart: 15, of which 5 were waited for; matrix products, arithmetic and copies ran while one was open for 1% of the time, Pallas kernels for 0%

profile of v5, /device:TPU:1, one launch (start us, length us, event | category | flops | bytes accessed | tf_op | source)
XLA Modules:
  0.0 61.6 jit_solution(11174015922624652033)
XLA Ops:
  0.6 1.5 %shard_map.86.refs_0_ = f32[9,32,128]{2,1,0:T(8,128)} custom-call(f32[3,1,32,128]{3,2,1,0:T(8,128)} %displacement.1, f32[3,1,32,128]{3,2,1,0:T(8,128)} %velocity.1, s32[1,32,128]{2,1,0:T(8,128)} %species.1, f32[1,32,128]{2,1,0:T(8,128)} %mass_factor.1, f32[1,32,128]{2,1,0:T(8,128)} %spring.1), custom_call_target="tpu_custom_call" | custom-call | tf_op jit(solution)/shard_map/pallas_call | solution.py:376
  2.2 4.2 %collective-permute-start.11 = (f32[9,32,128]{2,1,0:T(8,128)}, f32[9,32,128]{2,1,0:T(8,128)S(1)}, u32[]{:S(2)}, u32[]{:S(2)}) collective-permute-start(f32[9,32,128]{2,1,0:T(8,128)} %shard_map.86.refs_0_), channel_id=1, source_target_pairs={{0,12},{2,14},{4,8},{6,10},{8,4},{10,6},{12,0},{14,2},{1,13},{3,15... | collective-permute-start | bytes 442376 | tf_op jit(solution)/shard_map/ppermute | solution.py:384
  6.3 0.0 collective-permute-start.7
  6.3 0.3 collective-permute-start.3
  6.6 1.2 %collective-permute-start.1 = (f32[9,32,128]{2,1,0:T(8,128)}, f32[9,32,128]{2,1,0:T(8,128)S(1)}, u32[]{:S(2)}, u32[]{:S(2)}) collective-permute-start(f32[9,32,128]{2,1,0:T(8,128)} %shard_map.86.refs_0_), channel_id=1, source_target_pairs={{0,2},{2,0},{4,6},{6,4},{8,10},{10,8},{12,14},{14,12},{1,3},{3,1},... | collective-permute-start | bytes 442376 | tf_op jit(solution)/shard_map/ppermute | solution.py:384
  7.8 1.7 %collective-permute-start = (f32[9,32,128]{2,1,0:T(8,128)}, f32[9,32,128]{2,1,0:T(8,128)S(1)}, u32[]{:S(2)}, u32[]{:S(2)}) collective-permute-start(f32[9,32,128]{2,1,0:T(8,128)} %shard_map.86.refs_0_), channel_id=1, source_target_pairs={{0,1},{1,0},{2,3},{3,2},{4,5},{5,4},{6,7},{7,6},{8,9},{9,8},{10,11... | collective-permute-start | bytes 442376 | tf_op jit(solution)/shard_map/ppermute | solution.py:387
  9.6 0.6 collective-permute-done.11.refs_12_
  10.2 1.0 %collective-permute-start.13 = (f32[9,32,128]{2,1,0:T(8,128)S(1)}, f32[9,32,128]{2,1,0:T(8,128)S(1)}, u32[]{:S(2)}, u32[]{:S(2)}) collective-permute-start(f32[9,32,128]{2,1,0:T(8,128)S(1)} %collective-permute-done.11.refs_12_), channel_id=1, source_target_pairs={{0,2},{2,0},{4,6},{6,4},{8,10},{10,8},{12,14},{14,12},{1,3},{3,1},... | collective-permute-start | bytes 442376 | tf_op jit(solution)/shard_map/ppermute | solution.py:384
  11.2 7.4 %collective-permute-done.7.refs_8_ = f32[9,32,128]{2,1,0:T(8,128)S(1)} collective-permute-done((f32[9,32,128]{2,1,0:T(8,128)}, f32[9,32,128]{2,1,0:T(8,128)S(1)}, u32[]{:S(2)}, u32[]{:S(2)}) %collective-permute-start.7) | collective-permute-done | bytes 147488 | tf_op jit(solution)/shard_map/ppermute | solution.py:384
  18.6 1.4 %collective-permute-start.12 = (f32[9,32,128]{2,1,0:T(8,128)S(1)}, f32[9,32,128]{2,1,0:T(8,128)S(1)}, u32[]{:S(2)}, u32[]{:S(2)}) collective-permute-start(f32[9,32,128]{2,1,0:T(8,128)S(1)} %collective-permute-done.11.refs_12_), channel_id=1, source_target_pairs={{0,1},{1,0},{2,3},{3,2},{4,5},{5,4},{6,7},{7,6},{8,9},{9,8},{10,11... | collective-permute-start | bytes 442376 | tf_op jit(solution)/shard_map/ppermute | solution.py:387
  20.0 0.0 collective-permute-done.3.refs_4_
  20.0 1.2 %collective-permute-start.9 = (f32[9,32,128]{2,1,0:T(8,128)S(1)}, f32[9,32,128]{2,1,0:T(8,128)S(1)}, u32[]{:S(2)}, u32[]{:S(2)}) collective-permute-start(f32[9,32,128]{2,1,0:T(8,128)S(1)} %collective-permute-done.7.refs_8_), channel_id=1, source_target_pairs={{0,2},{2,0},{4,6},{6,4},{8,10},{10,8},{12,14},{14,12},{1,3},{3,1},... | collective-permute-start | bytes 442376 | tf_op jit(solution)/shard_map/ppermute | solution.py:384
  21.2 0.3 collective-permute-start.8
  21.6 0.3 collective-permute-start.5
  21.8 0.0 collective-permute-done.13.refs_14_
  21.8 0.4 collective-permute-start.4
  22.3 0.1 collective-permute-start.2
  22.4 3.0 %collective-permute-done.9.refs_10_ = f32[9,32,128]{2,1,0:T(8,128)S(1)} collective-permute-done((f32[9,32,128]{2,1,0:T(8,128)S(1)}, f32[9,32,128]{2,1,0:T(8,128)S(1)}, u32[]{:S(2)}, u32[]{:S(2)}) %collective-permute-start.9) | collective-permute-done | bytes 147488 | tf_op jit(solution)/shard_map/ppermute | solution.py:384
  25.4 1.3 %collective-permute-start.14 = (f32[9,32,128]{2,1,0:T(8,128)S(1)}, f32[9,32,128]{2,1,0:T(8,128)S(1)}, u32[]{:S(2)}, u32[]{:S(2)}) collective-permute-start(f32[9,32,128]{2,1,0:T(8,128)S(1)} %collective-permute-done.13.refs_14_), channel_id=1, source_target_pairs={{0,1},{1,0},{2,3},{3,2},{4,5},{5,4},{6,7},{7,6},{8,9},{9,8},{10,11... | collective-permute-start | bytes 442376 | tf_op jit(solution)/shard_map/ppermute | solution.py:387
  26.7 0.0 collective-permute-done.8.refs_9_
  26.7 0.1 collective-permute-start.10
  26.8 1.8 %collective-permute-done.5.refs_6_ = f32[9,32,128]{2,1,0:T(8,128)S(1)} collective-permute-done((f32[9,32,128]{2,1,0:T(8,128)S(1)}, f32[9,32,128]{2,1,0:T(8,128)S(1)}, u32[]{:S(2)}, u32[]{:S(2)}) %collective-permute-start.5) | collective-permute-done | bytes 147488 | tf_op jit(solution)/shard_map/ppermute | solution.py:384
  28.6 0.8 %collective-permute-start.6 = (f32[9,32,128]{2,1,0:T(8,128)S(1)}, f32[9,32,128]{2,1,0:T(8,128)S(1)}, u32[]{:S(2)}, u32[]{:S(2)}) collective-permute-start(f32[9,32,128]{2,1,0:T(8,128)S(1)} %collective-permute-done.5.refs_6_), channel_id=1, source_target_pairs={{0,1},{1,0},{2,3},{3,2},{4,5},{5,4},{6,7},{7,6},{8,9},{9,8},{10,11... | collective-permute-start | bytes 442376 | tf_op jit(solution)/shard_map/ppermute | solution.py:387
  29.4 0.7 %copy.9.refs_16_ = f32[8,3,3]{2,1,0:T(4,128)} copy(f32[8,3,3]{0,2,1:T(4,128)S(1)} %copy-done.15) | data formatting | bytes 576 | tf_op args[5]
  30.1 0.0 collective-permute-done.14.refs_15_
  30.2 0.2 collective-permute-done.6.refs_7_
  30.5 0.3 copy-done.10
  30.8 0.1 copy-done.11
  30.8 0.1 copy-done.12
  30.9 0.1 copy-done.13
  31.0 0.6 %copy-done.14 = f32[9,32,128]{2,1,0:T(8,128)} copy-done((f32[9,32,128]{2,1,0:T(8,128)}, f32[9,32,128]{2,1,0:T(8,128)S(1)}, u32[]{:S(2)}) %copy-start.14) | copy-done | bytes 147480
  31.6 30.0 %shard_map.87 = (f32[32,128]{1,0:T(8,128)}, f32[32,128]{1,0:T(8,128)}) custom-call(f32[9,32,128]{2,1,0:T(8,128)} %shard_map.86.refs_0_, f32[9,32,128]{2,1,0:T(8,128)} %copy-done.4, f32[9,32,128]{2,1,0:T(8,128)} %copy-done.3, f32[9,32,128]{2,1,0:T(8,128)} %copy-done.11, f32[9,32,128]{2,1,0:T(8,128)} %copy-done.2, f32[9,32,128]{2,1,0:T(8,128)} %copy-done.10, ...), custom_call_target="tpu_custom_call" | custom-call | tf_op jit(solution)/shard_map/pallas_call | solution.py:412
  (33 shorter events, 0.1 us)
Async XLA Ops:
  0.6 28.8 %copy-start.15 = (f32[8,3,3]{0,2,1:T(4,128)S(1)}, f32[8,3,3]{0,2,1:T(4,128)}, u32[]{:S(2)}) copy-start(f32[8,3,3]{0,2,1:T(4,128)} %param.12) | copy-start | bytes 868
  2.2 8.0 %collective-permute-start.11 = (f32[9,32,128]{2,1,0:T(8,128)}, f32[9,32,128]{2,1,0:T(8,128)S(1)}, u32[]{:S(2)}, u32[]{:S(2)}) collective-permute-start(f32[9,32,128]{2,1,0:T(8,128)} %shard_map.86.refs_0_), channel_id=1, source_target_pairs={{0,12},{2,14},{4,8},{6,10},{8,4},{10,6},{12,0},{14,2},{1,13},{3,15... | collective-permute-start | bytes 442376 | tf_op jit(solution)/shard_map/ppermute | solution.py:384
  6.3 12.3 %collective-permute-start.7 = (f32[9,32,128]{2,1,0:T(8,128)}, f32[9,32,128]{2,1,0:T(8,128)S(1)}, u32[]{:S(2)}, u32[]{:S(2)}) collective-permute-start(f32[9,32,128]{2,1,0:T(8,128)} %shard_map.86.refs_0_), channel_id=1, source_target_pairs={{0,8},{2,10},{4,12},{6,14},{8,0},{10,2},{12,4},{14,6},{1,9},{3,11}... | collective-permute-start | bytes 442376 | tf_op jit(solution)/shard_map/ppermute | solution.py:384
  6.3 13.6 %collective-permute-start.3 = (f32[9,32,128]{2,1,0:T(8,128)}, f32[9,32,128]{2,1,0:T(8,128)S(1)}, u32[]{:S(2)}, u32[]{:S(2)}) collective-permute-start(f32[9,32,128]{2,1,0:T(8,128)} %shard_map.86.refs_0_), channel_id=1, source_target_pairs={{0,4},{2,6},{4,0},{6,2},{8,12},{10,14},{12,8},{14,10},{1,5},{3,7},... | collective-permute-start | bytes 442376 | tf_op jit(solution)/shard_map/ppermute | solution.py:384
  6.6 14.6 %collective-permute-start.1 = (f32[9,32,128]{2,1,0:T(8,128)}, f32[9,32,128]{2,1,0:T(8,128)S(1)}, u32[]{:S(2)}, u32[]{:S(2)}) collective-permute-start(f32[9,32,128]{2,1,0:T(8,128)} %shard_map.86.refs_0_), channel_id=1, source_target_pairs={{0,2},{2,0},{4,6},{6,4},{8,10},{10,8},{12,14},{14,12},{1,3},{3,1},... | collective-permute-start | bytes 442376 | tf_op jit(solution)/shard_map/ppermute | solution.py:384
  7.8 13.7 %collective-permute-start = (f32[9,32,128]{2,1,0:T(8,128)}, f32[9,32,128]{2,1,0:T(8,128)S(1)}, u32[]{:S(2)}, u32[]{:S(2)}) collective-permute-start(f32[9,32,128]{2,1,0:T(8,128)} %shard_map.86.refs_0_), channel_id=1, source_target_pairs={{0,1},{1,0},{2,3},{3,2},{4,5},{5,4},{6,7},{7,6},{8,9},{9,8},{10,11... | collective-permute-start | bytes 442376 | tf_op jit(solution)/shard_map/ppermute | solution.py:387
  10.2 20.3 %copy-start = (f32[9,32,128]{2,1,0:T(8,128)}, f32[9,32,128]{2,1,0:T(8,128)S(1)}, u32[]{:S(2)}) copy-start(f32[9,32,128]{2,1,0:T(8,128)S(1)} %collective-permute-done.11.refs_12_) | copy-start | bytes 442372
  10.2 11.7 %collective-permute-start.13 = (f32[9,32,128]{2,1,0:T(8,128)S(1)}, f32[9,32,128]{2,1,0:T(8,128)S(1)}, u32[]{:S(2)}, u32[]{:S(2)}) collective-permute-start(f32[9,32,128]{2,1,0:T(8,128)S(1)} %collective-permute-done.11.refs_12_), channel_id=1, source_target_pairs={{0,2},{2,0},{4,6},{6,4},{8,10},{10,8},{12,14},{14,12},{1,3},{3,1},... | collective-permute-start | bytes 442376 | tf_op jit(solution)/shard_map/ppermute | solution.py:384
  18.6 11.8 %copy-start.1 = (f32[9,32,128]{2,1,0:T(8,128)}, f32[9,32,128]{2,1,0:T(8,128)S(1)}, u32[]{:S(2)}) copy-start(f32[9,32,128]{2,1,0:T(8,128)S(1)} %collective-permute-done.7.refs_8_) | copy-start | bytes 442372
  18.6 3.7 %collective-permute-start.12 = (f32[9,32,128]{2,1,0:T(8,128)S(1)}, f32[9,32,128]{2,1,0:T(8,128)S(1)}, u32[]{:S(2)}, u32[]{:S(2)}) collective-permute-start(f32[9,32,128]{2,1,0:T(8,128)S(1)} %collective-permute-done.11.refs_12_), channel_id=1, source_target_pairs={{0,1},{1,0},{2,3},{3,2},{4,5},{5,4},{6,7},{7,6},{8,9},{9,8},{10,11... | collective-permute-start | bytes 442376 | tf_op jit(solution)/shard_map/ppermute | solution.py:387
  20.0 10.5 %copy-start.2 = (f32[9,32,128]{2,1,0:T(8,128)}, f32[9,32,128]{2,1,0:T(8,128)S(1)}, u32[]{:S(2)}) copy-start(f32[9,32,128]{2,1,0:T(8,128)S(1)} %collective-permute-done.3.refs_4_) | copy-start | bytes 442372
  20.0 5.4 %collective-permute-start.9 = (f32[9,32,128]{2,1,0:T(8,128)S(1)}, f32[9,32,128]{2,1,0:T(8,128)S(1)}, u32[]{:S(2)}, u32[]{:S(2)}) collective-permute-start(f32[9,32,128]{2,1,0:T(8,128)S(1)} %collective-permute-done.7.refs_8_), channel_id=1, source_target_pairs={{0,2},{2,0},{4,6},{6,4},{8,10},{10,8},{12,14},{14,12},{1,3},{3,1},... | collective-permute-start | bytes 442376 | tf_op jit(solution)/shard_map/ppermute | solution.py:384
  21.2 9.2 %copy-start.3 = (f32[9,32,128]{2,1,0:T(8,128)}, f32[9,32,128]{2,1,0:T(8,128)S(1)}, u32[]{:S(2)}) copy-start(f32[9,32,128]{2,1,0:T(8,128)S(1)} %collective-permute-done.1.refs_2_) | copy-start | bytes 442372
  21.2 5.5 %collective-permute-start.8 = (f32[9,32,128]{2,1,0:T(8,128)S(1)}, f32[9,32,128]{2,1,0:T(8,128)S(1)}, u32[]{:S(2)}, u32[]{:S(2)}) collective-permute-start(f32[9,32,128]{2,1,0:T(8,128)S(1)} %collective-permute-done.7.refs_8_), channel_id=1, source_target_pairs={{0,1},{1,0},{2,3},{3,2},{4,5},{5,4},{6,7},{7,6},{8,9},{9,8},{10,11... | collective-permute-start | bytes 442376 | tf_op jit(solution)/shard_map/ppermute | solution.py:387
  21.6 8.9 %copy-start.4 = (f32[9,32,128]{2,1,0:T(8,128)}, f32[9,32,128]{2,1,0:T(8,128)S(1)}, u32[]{:S(2)}) copy-start(f32[9,32,128]{2,1,0:T(8,128)S(1)} %collective-permute-done.refs_1_) | copy-start | bytes 442372
  21.6 7.0 %collective-permute-start.5 = (f32[9,32,128]{2,1,0:T(8,128)S(1)}, f32[9,32,128]{2,1,0:T(8,128)S(1)}, u32[]{:S(2)}, u32[]{:S(2)}) collective-permute-start(f32[9,32,128]{2,1,0:T(8,128)S(1)} %collective-permute-done.3.refs_4_), channel_id=1, source_target_pairs={{0,2},{2,0},{4,6},{6,4},{8,10},{10,8},{12,14},{14,12},{1,3},{3,1},... | collective-permute-start | bytes 442376 | tf_op jit(solution)/shard_map/ppermute | solution.py:384
  21.8 8.6 %copy-start.5 = (f32[9,32,128]{2,1,0:T(8,128)}, f32[9,32,128]{2,1,0:T(8,128)S(1)}, u32[]{:S(2)}) copy-start(f32[9,32,128]{2,1,0:T(8,128)S(1)} %collective-permute-done.13.refs_14_) | copy-start | bytes 442372
  21.8 8.3 %collective-permute-start.4 = (f32[9,32,128]{2,1,0:T(8,128)S(1)}, f32[9,32,128]{2,1,0:T(8,128)S(1)}, u32[]{:S(2)}, u32[]{:S(2)}) collective-permute-start(f32[9,32,128]{2,1,0:T(8,128)S(1)} %collective-permute-done.3.refs_4_), channel_id=1, source_target_pairs={{0,1},{1,0},{2,3},{3,2},{4,5},{5,4},{6,7},{7,6},{8,9},{9,8},{10,11... | collective-permute-start | bytes 442376 | tf_op jit(solution)/shard_map/ppermute | solution.py:387
  22.3 8.2 %copy-start.6 = (f32[9,32,128]{2,1,0:T(8,128)}, f32[9,32,128]{2,1,0:T(8,128)S(1)}, u32[]{:S(2)}) copy-start(f32[9,32,128]{2,1,0:T(8,128)S(1)} %collective-permute-done.12.refs_13_) | copy-start | bytes 442372
  22.3 7.8 %collective-permute-start.2 = (f32[9,32,128]{2,1,0:T(8,128)S(1)}, f32[9,32,128]{2,1,0:T(8,128)S(1)}, u32[]{:S(2)}, u32[]{:S(2)}) collective-permute-start(f32[9,32,128]{2,1,0:T(8,128)S(1)} %collective-permute-done.1.refs_2_), channel_id=1, source_target_pairs={{0,1},{1,0},{2,3},{3,2},{4,5},{5,4},{6,7},{7,6},{8,9},{9,8},{10,11... | collective-permute-start | bytes 442376 | tf_op jit(solution)/shard_map/ppermute | solution.py:387
  25.4 5.1 %copy-start.7 = (f32[9,32,128]{2,1,0:T(8,128)}, f32[9,32,128]{2,1,0:T(8,128)S(1)}, u32[]{:S(2)}) copy-start(f32[9,32,128]{2,1,0:T(8,128)S(1)} %collective-permute-done.9.refs_10_) | copy-start | bytes 442372
  25.4 4.7 %collective-permute-start.14 = (f32[9,32,128]{2,1,0:T(8,128)S(1)}, f32[9,32,128]{2,1,0:T(8,128)S(1)}, u32[]{:S(2)}, u32[]{:S(2)}) collective-permute-start(f32[9,32,128]{2,1,0:T(8,128)S(1)} %collective-permute-done.13.refs_14_), channel_id=1, source_target_pairs={{0,1},{1,0},{2,3},{3,2},{4,5},{5,4},{6,7},{7,6},{8,9},{9,8},{10,11... | collective-permute-start | bytes 442376 | tf_op jit(solution)/shard_map/ppermute | solution.py:387
  26.7 3.8 %copy-start.8 = (f32[9,32,128]{2,1,0:T(8,128)}, f32[9,32,128]{2,1,0:T(8,128)S(1)}, u32[]{:S(2)}) copy-start(f32[9,32,128]{2,1,0:T(8,128)S(1)} %collective-permute-done.8.refs_9_) | copy-start | bytes 442372
  26.7 3.4 %collective-permute-start.10 = (f32[9,32,128]{2,1,0:T(8,128)S(1)}, f32[9,32,128]{2,1,0:T(8,128)S(1)}, u32[]{:S(2)}, u32[]{:S(2)}) collective-permute-start(f32[9,32,128]{2,1,0:T(8,128)S(1)} %collective-permute-done.9.refs_10_), channel_id=1, source_target_pairs={{0,1},{1,0},{2,3},{3,2},{4,5},{5,4},{6,7},{7,6},{8,9},{9,8},{10,11... | collective-permute-start | bytes 442376 | tf_op jit(solution)/shard_map/ppermute | solution.py:387
  28.6 1.9 %copy-start.9 = (f32[9,32,128]{2,1,0:T(8,128)}, f32[9,32,128]{2,1,0:T(8,128)S(1)}, u32[]{:S(2)}) copy-start(f32[9,32,128]{2,1,0:T(8,128)S(1)} %collective-permute-done.5.refs_6_) | copy-start | bytes 442372
  28.6 1.9 %collective-permute-start.6 = (f32[9,32,128]{2,1,0:T(8,128)S(1)}, f32[9,32,128]{2,1,0:T(8,128)S(1)}, u32[]{:S(2)}, u32[]{:S(2)}) collective-permute-start(f32[9,32,128]{2,1,0:T(8,128)S(1)} %collective-permute-done.5.refs_6_), channel_id=1, source_target_pairs={{0,1},{1,0},{2,3},{3,2},{4,5},{5,4},{6,7},{7,6},{8,9},{9,8},{10,11... | collective-permute-start | bytes 442376 | tf_op jit(solution)/shard_map/ppermute | solution.py:387
  30.1 0.6 %copy-start.10 = (f32[9,32,128]{2,1,0:T(8,128)}, f32[9,32,128]{2,1,0:T(8,128)S(1)}, u32[]{:S(2)}) copy-start(f32[9,32,128]{2,1,0:T(8,128)S(1)} %collective-permute-done.4.refs_5_) | copy-start | bytes 442372
  30.1 0.7 %copy-start.11 = (f32[9,32,128]{2,1,0:T(8,128)}, f32[9,32,128]{2,1,0:T(8,128)S(1)}, u32[]{:S(2)}) copy-start(f32[9,32,128]{2,1,0:T(8,128)S(1)} %collective-permute-done.2.refs_3_) | copy-start | bytes 442372
  30.1 0.8 %copy-start.12 = (f32[9,32,128]{2,1,0:T(8,128)}, f32[9,32,128]{2,1,0:T(8,128)S(1)}, u32[]{:S(2)}) copy-start(f32[9,32,128]{2,1,0:T(8,128)S(1)} %collective-permute-done.14.refs_15_) | copy-start | bytes 442372
  30.2 0.8 %copy-start.13 = (f32[9,32,128]{2,1,0:T(8,128)}, f32[9,32,128]{2,1,0:T(8,128)S(1)}, u32[]{:S(2)}) copy-start(f32[9,32,128]{2,1,0:T(8,128)S(1)} %collective-permute-done.10.refs_11_) | copy-start | bytes 442372
  31.0 0.7 %copy-start.14 = (f32[9,32,128]{2,1,0:T(8,128)}, f32[9,32,128]{2,1,0:T(8,128)S(1)}, u32[]{:S(2)}) copy-start(f32[9,32,128]{2,1,0:T(8,128)S(1)} %collective-permute-done.6.refs_7_) | copy-start | bytes 442372
